TPU v7x, 32 devices: a whole 2x2x4 slice. The times are simulated.
32 devices in a mesh: expert: 8 (over z, y), hid: 4 (over x, core).
Axes of the slice: x: 2, y: 2, z: 4, core: 2. Of those that a mesh axis runs over, the one named last changes fastest.
Arguments:
- tokens_in: bfloat16 [8192, 768], P(('expert', 'hid')), may hold values from -6 to 6
- out_cotangent: bfloat16 [8192, 768], P(('expert', 'hid')), may hold values from -6 to 6
- qkv_weight: float32 [768, 2304], P(('expert', 'hid')), may hold values from -0.21875 to 0.21875
- proj_weight: float32 [768, 768], P(('expert', 'hid')), may hold values from -2 to 2
- router_weight: float32 [768, 8], P(('expert', 'hid')), may hold values from -0.15625 to 0.15625
- pre_gain: float32 [768], P(('expert', 'hid')), may hold values from 0.5 to 1.5
- pre_shift: float32 [768], P(('expert', 'hid')), may hold values from -0.6 to 0.6
- mid_gain: float32 [768], P(('expert', 'hid')), may hold values from 0.5 to 1.5
- mid_shift: float32 [768], P(('expert', 'hid')), may hold values from -0.6 to 0.6
- expert_in: float32 [8, 768, 3072], P('expert', None, 'hid'), may hold values from -0.21875 to 0.21875
- expert_down: float32 [8, 3072, 768], P('expert', 'hid'), may hold values from -0.875 to 0.875
- assignment: int32 [8192], P(('expert', 'hid')), may hold values from 0 to 7, as said below
Outputs:
- layer_output: bfloat16 [8192, 768], P(('expert', 'hid'))
- balance_loss: float32 [], replicated
- input_grad: bfloat16 [8192, 768], P(('expert', 'hid'))
- qkv_grad: float32 [768, 2304], P(('expert', 'hid'))
- proj_grad: float32 [768, 768], P(('expert', 'hid'))
- router_grad: float32 [768, 8], P(('expert', 'hid'))
- pre_gain_grad: float32 [768], P(('expert', 'hid'))
- pre_shift_grad: float32 [768], P(('expert', 'hid'))
- mid_gain_grad: float32 [768], P(('expert', 'hid'))
- mid_shift_grad: float32 [768], P(('expert', 'hid'))
- expert_in_grad: float32 [8, 768, 3072], P('expert', None, 'hid')
- expert_down_grad: float32 [8, 3072, 768], P('expert', 'hid')
Inputs may be any that keep to these rules, and one draw needn't show every extreme that they name: `assignment`: in each aligned block of 256 tokens (the tokens of one device) no expert is named by more than 64 tokens; one expert, drawn from the seed, is named by exactly 64 tokens of every block.
All inputs are finite; a program needn't handle non-finite values.
Results may differ from a plain program's by a relative error of at most 0.015.
The roundings to bfloat16 on the way count: a program that leaves them out, or rounds other values in their place, can miss the bound.
Values may be sent and summed in bfloat16 or wider, within the bound.
A program may use at most 192 MiB of HBM per device.

v0:
```python
from functools import partial

import jax
import jax.numpy as jnp
from jax import lax
from jax.sharding import PartitionSpec as P

HEADS = 12


epsilon = 1e-05
balance_weight = 3.0
masked_score = -1000000000.0


def for_sending(value):

    def short(part):
        return part.astype(jnp.bfloat16) if part.dtype == jnp.float32 else part

    return jax.tree.map(short, value)


def norm_apply(values, gain, shift):
    average = jnp.mean(values, axis=-1, keepdims=True)
    centred = values - average
    spread = jnp.mean(centred * centred, axis=-1, keepdims=True)
    return centred * lax.rsqrt(spread + epsilon) * gain + shift


def contract_rows(left, right):
    return lax.dot_general(
        left, right, (((0,), (0,)), ((), ())), preferred_element_type=jnp.float32
    )


def contract_cols(left, right):
    return lax.dot_general(
        left, right, (((1,), (1,)), ((), ())), preferred_element_type=jnp.float32
    )


def build_slots(assignment, experts, capacity):
    token_count = assignment.shape[0]
    labels = jnp.arange(experts, dtype=jnp.int32)
    onehot = (assignment[:, None] == labels[None, :]).astype(jnp.int32)
    ranking = jnp.cumsum(onehot, axis=0) - 1
    slot_index = jnp.sum(ranking * onehot, axis=1)
    position = assignment * capacity + slot_index
    slot_owner = jnp.full((experts * capacity,), token_count, jnp.int32)
    slot_owner = slot_owner.at[position].set(jnp.arange(token_count, dtype=jnp.int32))
    return (position, slot_owner, onehot)


def take_rows(values, slot_owner):
    padded = jnp.concatenate([values, jnp.zeros((1, values.shape[1]), values.dtype)], axis=0)
    return padded[slot_owner]


def on_device(
    tokens_in,
    out_cotangent,
    qkv_weight,
    proj_weight,
    router_weight,
    pre_gain,
    pre_shift,
    mid_gain,
    mid_shift,
    expert_in,
    expert_down,
    assignment,
):
    token_count, model_width = tokens_in.shape
    experts = lax.axis_size("expert")
    capacity = 2 * token_count // experts
    total_tokens = token_count * experts * lax.axis_size("hid")
    head_dim = model_width // HEADS
    score_scale = head_dim ** (-0.5)
    half = jnp.bfloat16
    single = jnp.float32
    gathered = (
        lax.all_gather(qkv_weight.astype(half), ("expert", "hid"), axis=0, tiled=True),
        lax.all_gather(proj_weight.astype(half), ("expert", "hid"), axis=0, tiled=True),
        lax.all_gather(router_weight.astype(half), ("expert", "hid"), axis=0, tiled=True),
        lax.all_gather(pre_gain.astype(half), ("expert", "hid"), axis=0, tiled=True),
        lax.all_gather(pre_shift.astype(half), ("expert", "hid"), axis=0, tiled=True),
        lax.all_gather(mid_gain.astype(half), ("expert", "hid"), axis=0, tiled=True),
        lax.all_gather(mid_shift.astype(half), ("expert", "hid"), axis=0, tiled=True),
    )
    w_qkv, w_proj, w_router, gain_a, shift_a, gain_b, shift_b = gathered
    inputs = tokens_in.astype(single)
    normed_a, pre_back = jax.vjp(norm_apply, inputs, gain_a.astype(single), shift_a.astype(single))
    hidden_a = normed_a.astype(half)
    qkv_rows = jnp.dot(hidden_a, w_qkv, preferred_element_type=single).astype(half)
    queries = qkv_rows[:, :model_width].reshape(token_count, HEADS, head_dim)
    key_rows = qkv_rows[:, model_width : 2 * model_width].reshape(token_count, HEADS, head_dim)
    value_rows = qkv_rows[:, 2 * model_width :].reshape(token_count, HEADS, head_dim)
    block_rows = min(token_count, 512)
    block_count = token_count // block_rows
    key_index = jnp.arange(token_count, dtype=jnp.int32)

    def block_scores(first_row, query_block):
        raw_scores = (
            jnp.einsum("qhd,khd->hqk", query_block, key_rows, preferred_element_type=single)
            * score_scale
        )
        query_index = first_row + jnp.arange(block_rows, dtype=jnp.int32)
        allowed = key_index[None, :] <= query_index[:, None]
        return jnp.where(allowed[None], raw_scores, masked_score)

    def attend(block_index):
        first_row = block_index * block_rows
        scores = block_scores(first_row, queries)
        row_max = jnp.max(scores, axis=-1, keepdims=True)
        logsum = row_max + jnp.log(jnp.sum(jnp.exp(scores - row_max), axis=-1, keepdims=True))
        weights = jnp.exp(scores - logsum).astype(half)
        mixed_rows = jnp.einsum("hqk,khd->qhd", weights, value_rows, preferred_element_type=single)
        return (mixed_rows.astype(half), logsum)

    mixed_blocks, logsum_blocks = lax.map(attend, jnp.arange(block_count, dtype=jnp.int32))
    attended = mixed_blocks.reshape(token_count, model_width)
    residual = inputs + jnp.dot(attended, w_proj, preferred_element_type=single)
    normed_b, mid_back = jax.vjp(
        norm_apply, residual, gain_b.astype(single), shift_b.astype(single)
    )
    hidden_b = normed_b.astype(half)
    logits = jnp.dot(hidden_b, w_router, preferred_element_type=single)
    router_probs = jax.nn.softmax(logits, axis=-1)
    position, slot_owner, onehot = build_slots(assignment, experts, capacity)
    onehot_f = onehot.astype(single)
    gate_value = jnp.sum(router_probs * onehot_f, axis=1)
    counts, prob_total = lax.psum(
        (jnp.sum(onehot_f, axis=0), jnp.sum(router_probs, axis=0)), ("expert", "hid")
    )
    expert_scale = balance_weight * experts * counts / total_tokens
    balance_loss = jnp.sum(expert_scale * prob_total) / total_tokens
    outgoing = take_rows(hidden_b, slot_owner).reshape(experts, capacity, model_width)
    incoming = lax.all_to_all(outgoing, "expert", split_axis=0, concat_axis=0, tiled=True)
    in_local = expert_in[0].astype(half)
    down_local = expert_down[0].astype(half)
    gelu_exact = partial(jax.nn.gelu, approximate=False)
    local_rows = experts * capacity
    dispatched_rows = lax.all_gather(incoming, "hid", axis=0, tiled=True).reshape(-1, model_width)
    before = jnp.dot(dispatched_rows, in_local, preferred_element_type=single)
    active_f, gelu_back = jax.vjp(gelu_exact, before)
    active = active_f.astype(half)
    row_block = lax.slice_in_dim(active, 0, lax.axis_size("hid") * local_rows, axis=0)
    expert_out = lax.psum_scatter(
        jnp.dot(row_block, down_local, preferred_element_type=single).astype(jnp.bfloat16),
        "hid",
        scatter_dimension=0,
        tiled=True,
    ).astype(jnp.float32)
    returning = expert_out.astype(half).reshape(experts, capacity, model_width)
    arrived = (
        lax.all_to_all(for_sending(returning), "expert", split_axis=0, concat_axis=0, tiled=True)
        .astype(returning.dtype)
        .reshape(local_rows, model_width)
    )
    expert_tok = arrived[position]
    layer_output = (residual + gate_value[:, None] * expert_tok.astype(single)).astype(half)
    cotangent = out_cotangent.astype(single)
    grad_expert = (gate_value[:, None] * cotangent).astype(half)
    grad_gate = jnp.sum(cotangent * expert_tok.astype(single), axis=1)
    outgoing_grad = take_rows(grad_expert, slot_owner).reshape(experts, capacity, model_width)
    incoming_grad = lax.all_to_all(outgoing_grad, "expert", split_axis=0, concat_axis=0, tiled=True)
    grad_rows_all = lax.all_gather(incoming_grad, "hid", axis=0, tiled=True).reshape(
        -1, model_width
    )
    grad_active = contract_cols(grad_rows_all, down_local)
    grad_before = gelu_back(grad_active)[0].astype(half)
    down_grad = contract_rows(active, grad_rows_all)
    in_grad = contract_rows(dispatched_rows, grad_before)
    row_block = grad_before
    grad_mine = lax.psum_scatter(
        contract_cols(row_block, in_local).astype(jnp.bfloat16),
        "hid",
        scatter_dimension=0,
        tiled=True,
    ).astype(jnp.float32)
    sending_back = grad_mine.astype(half).reshape(experts, capacity, model_width)
    back_rows = lax.all_to_all(
        sending_back, "expert", split_axis=0, concat_axis=0, tiled=True
    ).reshape(local_rows, model_width)
    grad_dispatch = back_rows[position].astype(single)
    grad_probs = onehot_f * grad_gate[:, None] + expert_scale[None, :]
    grad_logits = (
        router_probs * (grad_probs - jnp.sum(router_probs * grad_probs, axis=1, keepdims=True))
    ).astype(half)
    router_local = contract_rows(hidden_b, grad_logits)
    grad_hidden_b = grad_dispatch + contract_cols(grad_logits, w_router)
    grad_resid_n, mid_gain_local, mid_shift_local = mid_back(grad_hidden_b)
    grad_resid = cotangent + grad_resid_n
    grad_proj = grad_resid.astype(half)
    proj_local = contract_rows(attended, grad_proj)
    grad_attended = (
        contract_cols(grad_proj, w_proj).astype(half).reshape(token_count, HEADS, head_dim)
    )

    def attend_back(carry, block_index):
        key_total, value_total = carry
        first_row = block_index * block_rows
        scores = block_scores(first_row, queries)
        probs_f = jnp.exp(scores - logsum_blocks[block_index])
        weights = probs_f.astype(half)
        value_total = value_total + jnp.einsum(
            "hqk,qhd->khd", weights, grad_attended, preferred_element_type=single
        )
        grad_weights = jnp.einsum(
            "qhd,khd->hqk", grad_attended, value_rows, preferred_element_type=single
        )
        grad_scores = (
            probs_f * (grad_weights - jnp.sum(probs_f * grad_weights, axis=-1, keepdims=True))
        ).astype(half)
        grad_query = (
            jnp.einsum("hqk,khd->qhd", grad_scores, key_rows, preferred_element_type=single)
            * score_scale
        )
        key_total = (
            key_total
            + jnp.einsum("hqk,qhd->khd", grad_scores, queries, preferred_element_type=single)
            * score_scale
        )
        return ((key_total, value_total), grad_query.astype(half))

    zero_heads = jnp.zeros((token_count, HEADS, head_dim), single)
    (key_total, value_total), grad_query_blocks = lax.scan(
        attend_back, (zero_heads, zero_heads), jnp.arange(block_count, dtype=jnp.int32)
    )
    grad_qkv = jnp.concatenate(
        [
            grad_query_blocks.reshape(token_count, model_width),
            key_total.reshape(token_count, model_width).astype(half),
            value_total.reshape(token_count, model_width).astype(half),
        ],
        axis=1,
    )
    qkv_local = contract_rows(hidden_a, grad_qkv)
    grad_hidden_a = contract_cols(grad_qkv, w_qkv)
    grad_in_n, pre_gain_local, pre_shift_local = pre_back(grad_hidden_a)
    input_grad = (grad_resid + grad_in_n).astype(half)
    summed = (
        lax.psum_scatter(qkv_local, ("expert", "hid"), scatter_dimension=0, tiled=True),
        lax.psum_scatter(proj_local, ("expert", "hid"), scatter_dimension=0, tiled=True),
        lax.psum_scatter(router_local, ("expert", "hid"), scatter_dimension=0, tiled=True),
        lax.psum_scatter(pre_gain_local, ("expert", "hid"), scatter_dimension=0, tiled=True),
        lax.psum_scatter(pre_shift_local, ("expert", "hid"), scatter_dimension=0, tiled=True),
        lax.psum_scatter(mid_gain_local, ("expert", "hid"), scatter_dimension=0, tiled=True),
        lax.psum_scatter(mid_shift_local, ("expert", "hid"), scatter_dimension=0, tiled=True),
    )
    (
        qkv_grad,
        proj_grad,
        router_grad,
        pre_gain_grad,
        pre_shift_grad,
        mid_gain_grad,
        mid_shift_grad,
    ) = summed
    return (
        layer_output,
        balance_loss,
        input_grad,
        qkv_grad,
        proj_grad,
        router_grad,
        pre_gain_grad,
        pre_shift_grad,
        mid_gain_grad,
        mid_shift_grad,
        in_grad[None],
        down_grad[None],
    )


def solution(mesh):
    in_specs = (
        P(("expert", "hid"), None),
        P(("expert", "hid"), None),
        P(("expert", "hid"), None),
        P(("expert", "hid"), None),
        P(("expert", "hid"), None),
        P(("expert", "hid")),
        P(("expert", "hid")),
        P(("expert", "hid")),
        P(("expert", "hid")),
        P("expert", None, "hid"),
        P("expert", "hid", None),
        P(("expert", "hid")),
    )
    out_specs = (
        P(("expert", "hid"), None),
        P(),
        P(("expert", "hid"), None),
        P(("expert", "hid"), None),
        P(("expert", "hid"), None),
        P(("expert", "hid"), None),
        P(("expert", "hid")),
        P(("expert", "hid")),
        P(("expert", "hid")),
        P(("expert", "hid")),
        P("expert", None, "hid"),
        P("expert", "hid", None),
    )
    return jax.shard_map(
        on_device, mesh=mesh, in_specs=in_specs, out_specs=out_specs, check_vma=False
    )
```

profile of v0, /device:TPU:0, one launch (start us, length us, event | category | flops | bytes accessed | tf_op | source)
XLA Modules:
  0.0 733.8 jit_solution(9915554301651066442)
XLA Ops:
  7.2 1.6 convert_element_type.161
  8.9 1.5 convert_element_type.166
  14.6 42.3 %all-reduce.12 = (bf16[768]{0:T(1024)(128)(2,1)S(1)}, bf16[768]{0:T(1024)(128)(2,1)S(1)}, bf16[768]{0:T(1024)(128)(2,1)S(1)}, bf16[768]{0:T(1024)(128)(2,1)S(1)}) all-reduce(bf16[768]{0:T(1024)(128)(2,1)S(1)} %dynamic-update-slice.1, bf16[768]{0:T(1024)(128)(2,1)S(1)} %dynamic-update-slice, ...), channel_id=1, replica_groups=mesh['expert'=8,'hid'=4] {'expert','hid'}, use_global_device_ids=true, to_apply=%add.3 | all-reduce | flops 3072 | bytes 12288
  62.1 1.4 scatter_custom_fusion
  65.4 9.1 %all-gather.6.cloned.1.call-done = bf16[768,2304]{1,0:T(8,128)(2,1)} async-done(((bf16[24,2304]{1,0:T(8,128)(2,1)}), bf16[768,2304]{1,0:T(8,128)(2,1)}) %all-gather.6.cloned.1.call-update) | async-done | bytes 3538960 | tf_op jit(solution)/shard_map/all_gather | solution.py:83
  74.5 3.3 convolution_convert_fusion
  80.0 1.7 fusion.6
  81.8 1.5 exponential_reduce_fusion
  83.9 1.6 convolution_convert_fusion.5
  85.5 45.3 %all-gather.8.cloned.1.call-done = bf16[768,768]{1,0:T(8,128)(2,1)} async-done(((bf16[24,768]{1,0:T(8,128)(2,1)}), bf16[768,768]{1,0:T(8,128)(2,1)}) %all-gather.8.cloned.1.call-update) | async-done | bytes 1179664 | tf_op jit(solution)/shard_map/all_gather | solution.py:84
  130.9 2.0 fusion.67
  136.0 2.8 gather_fusion
  138.8 25.1 %all_to_all.20 = bf16[8,64,768]{2,1,0:T(8,128)(2,1)} all-to-all(bf16[8,64,768]{2,1,0:T(8,128)(2,1)} %bitcast.91), channel_id=1, replica_groups=mesh['expert'=8,'hid'=4] {'expert'}, dimensions={0} | all-to-all | bytes 1572864 | tf_op jit(solution)/shard_map/all_to_all | solution.py:139
  164.2 27.4 %all-gather.10.cloned.1.call-done = bf16[32,64,768]{2,1,0:T(8,128)(2,1)} async-done(((bf16[8,64,768]{2,1,0:T(8,128)(2,1)}), bf16[32,64,768]{2,1,0:T(8,128)(2,1)}) %all-gather.10.cloned.1.call-update) | async-done | bytes 3145744 | tf_op jit(solution)/shard_map/all_gather | solution.py:144
  191.6 19.2 %multiply_convert_fusion = (bf16[2048,768]{1,0:T(8,128)(2,1)S(1)}, f32[2048,768]{1,0:T(8,128)}, f32[2048,768]{1,0:T(8,128)}) fusion(bf16[2048,768]{1,0:T(8,128)(2,1)} %bitcast.107, f32[1,768,768]{2,1,0:T(8,128)} %param.21), kind=kOutput, calls=%fused_computation.8 | convolution fusion | flops 2518745088 | bytes 21233664 | tf_op jit(solution)/shard_map/dot_general | solution.py:145
  210.8 1.7 copy-done.63
  212.5 4.0 convolution_convert_fusion.2
  216.6 38.1 %reduce-scatter.6.cloned.1.call-done = bf16[512,768]{1,0:T(8,128)(2,1)} async-done(((bf16[2048,768]{1,0:T(8,128)(2,1)}), bf16[512,768]{1,0:T(8,128)(2,1)}) %reduce-scatter.6.cloned.1.call-update) | async-done | bytes 786448 | tf_op jit(solution)/shard_map/reduce_scatter | solution.py:149
  254.7 5.5 all-to-all-start.1
  260.4 41.4 %psum.14 = f32[8]{0:T(128)} all-reduce(f32[8]{0:T(128)S(1)} %convert_reduce_fusion.1), channel_id=1, replica_groups=mesh['expert'=8,'hid'=4] {'expert','hid'}, use_global_device_ids=true, to_apply=%region_15.16 | all-reduce | flops 8 | bytes 64 | tf_op jit(solution)/shard_map/psum | solution.py:133
  302.5 39.9 %all-gather = bf16[32,24,8]{1,2,0:T(8,128)(2,1)S(1)} all-gather(bf16[1,24,8]{1,2,0:T(8,128)(2,1)S(1)} %convert_bitcast_fusion), channel_id=1, replica_groups=mesh['expert'=8,'hid'=4] {'expert','hid'}, dimensions={0}, use_global_device_ids=true | all-gather | bytes 12672 | tf_op jit(solution)/shard_map/all_gather | solution.py:85
  343.0 1.6 reshape.262
  346.4 1.3 fusion.68
  348.8 3.5 gather_fusion.1
  353.5 1.4 multiply_reduce_fusion.4
  355.5 2.8 gather_fusion.2
  358.3 25.1 %all_to_all.21 = bf16[8,64,768]{2,1,0:T(8,128)(2,1)} all-to-all(bf16[8,64,768]{2,1,0:T(8,128)(2,1)} %bitcast.90), channel_id=1, replica_groups=mesh['expert'=8,'hid'=4] {'expert'}, dimensions={0} | all-to-all | bytes 1572864 | tf_op jit(solution)/shard_map/all_to_all | solution.py:167
  383.7 26.5 %all-gather.12.cloned.1.call-done = bf16[32,64,768]{2,1,0:T(8,128)(2,1)} async-done(((bf16[8,64,768]{2,1,0:T(8,128)(2,1)}), bf16[32,64,768]{2,1,0:T(8,128)(2,1)}) %all-gather.12.cloned.1.call-update) | async-done | bytes 3145744 | tf_op jit(solution)/shard_map/all_gather | solution.py:168
  410.2 10.6 %add_convert_fusion = bf16[2048,768]{1,0:T(8,128)(2,1)S(1)} fusion(f32[2048,768]{1,0:T(8,128)} %get-tuple-element.86, f32[2048,768]{1,0:T(8,128)} %get-tuple-element.95, bf16[2048,768]{1,0:T(8,128)(2,1)} %bitcast.109, f32[1,768,768]{2,1,0:T(8,128)} %param.22), kind=kOutput, calls=%fused_computation.7 | convolution fusion | flops 2438529024 | bytes 21233664 | tf_op jit(solution)/shard_map/dot_general | solution.py:38
  420.8 1.7 copy-done.64
  422.5 4.0 convolution_convert_fusion.1
  426.6 38.0 %reduce-scatter.8.cloned.1.call-done = bf16[512,768]{1,0:T(8,128)(2,1)} async-done(((bf16[2048,768]{1,0:T(8,128)(2,1)}), bf16[512,768]{1,0:T(8,128)(2,1)}) %reduce-scatter.8.cloned.1.call-update) | async-done | bytes 786448 | tf_op jit(solution)/shard_map/reduce_scatter | solution.py:176
  464.7 25.8 %all_to_all.22 = bf16[8,64,768]{2,1,0:T(8,128)(2,1)} all-to-all(bf16[8,64,768]{2,1,0:T(8,128)(2,1)} %bitcast.103), channel_id=1, replica_groups=mesh['expert'=8,'hid'=4] {'expert'}, dimensions={0} | all-to-all | bytes 1572864 | tf_op jit(solution)/shard_map/all_to_all | solution.py:183
  490.4 3.6 gather_fusion.3
  494.0 2.6 multiply_reduce_fusion.1
  497.3 2.3 fusion.64
  500.7 1.9 fusion.69
  502.9 2.5 convolution_convert_fusion.4
  506.6 2.2 multiply_reduce_fusion
  512.6 4.2 fusion.38
  518.7 7.1 convolution_bitcast_fusion
  525.9 4.2 convolution_bitcast_fusion.1
  530.1 1.8 fusion.63
  532.4 40.3 %all-reduce.11 = (f32[8]{0:T(128)S(1)}, f32[768,8]{0,1:T(8,128)S(1)}, f32[768]{0:T(1024)S(1)}, f32[768]{0:T(1024)S(1)}, f32[768]{0:T(1024)S(1)}, /*index=5*/f32[768]{0:T(1024)S(1)}) all-reduce(f32[8]{0:T(128)} %get-tuple-element.72, f32[768,8]{0,1:T(8,128)} %fusion.56, ...), channel_id=1, replica_groups=mesh['expert'=8,'hid'=4] {'expert','hid'}, use_global_device_ids=true, to_apply=%region_17.18 | all-reduce | flops 9224 | bytes 73792 | tf_op jit(solution)/shard_map/psum | solution.py:133
  575.0 1.3 multiply_reduce_fusion.6
  577.6 1.7 add_convert_fusion.1
  579.3 20.6 %reduce-scatter.12.cloned.1.call-done = f32[24,768]{1,0:T(8,128)} async-done(((f32[768,768]{1,0:T(8,128)}), f32[24,768]{1,0:T(8,128)}) %reduce-scatter.12.cloned.1.call-update) | async-done | bytes 73744 | tf_op jit(solution)/shard_map/reduce_scatter | solution.py:245
  600.0 125.4 %reduce-scatter.10.cloned.1.call-done = f32[24,2304]{1,0:T(8,128)} async-done(((f32[768,2304]{1,0:T(8,128)}), f32[24,2304]{1,0:T(8,128)}) %reduce-scatter.10.cloned.1.call-update) | async-done | bytes 221200 | tf_op jit(solution)/shard_map/reduce_scatter | solution.py:244
  (214 shorter events, 36.0 us)
Async XLA Ops:
  7.2 67.4 %all-gather.6.cloned.1.call-start = ((), (), s32[]{:S(2)}) async-start(), calls=%async_computation.8 | async-start | bytes 3649536 | tf_op jit(solution)/shard_map/all_gather | solution.py:83
  8.8 122.0 %all-gather.8.cloned.1.call-start = ((), (), s32[]{:S(2)}) async-start(), calls=%async_computation.9 | async-start | bytes 1216512 | tf_op jit(solution)/shard_map/all_gather | solution.py:84
  10.4 181.2 %all-gather.10.cloned.1.call-start = ((), (), s32[]{:S(2)}) async-start(), calls=%async_computation.10 | async-start | bytes 3932160 | tf_op jit(solution)/shard_map/all_gather | solution.py:144
  56.8 17.7 %copy-start.30 = (f32[768]{0:T(1024)}, f32[768]{0:T(1024)S(1)}, u32[]{:S(2)}) copy-start(f32[768]{0:T(1024)S(1)} %convert_element_type.159) | copy-start | bytes 9220
  58.0 19.9 %copy-start.36 = (f32[256]{0:T(256)}, f32[256]{0:T(256)S(1)}, u32[]{:S(2)}) copy-start(f32[256]{0:T(256)S(1)} %broadcast_multiply_fusion.1) | copy-start | bytes 3076
  58.0 75.1 %copy-start.32 = (f32[768]{0:T(1024)}, f32[768]{0:T(1024)S(1)}, u32[]{:S(2)}) copy-start(f32[768]{0:T(1024)S(1)} %convert_element_type.168) | copy-start | bytes 9220
  65.4 9.2 %copy-start.53 = (f32[256]{0:T(256)}, f32[256]{0:T(256)S(1)}, u32[]{:S(2)}) copy-start(f32[256]{0:T(256)S(1)} %fusion.29) | copy-start | bytes 3076
  65.4 12.5 %copy-start.42 = (f32[256]{0:T(256)}, f32[256]{0:T(256)S(1)}, u32[]{:S(2)}) copy-start(f32[256]{0:T(256)S(1)} %fusion.46) | copy-start | bytes 3076
  78.1 3.6 copy-start.10
  80.0 3.9 copy-start.14
  80.0 3.9 copy-start.17
  81.7 49.1 %copy-start.1 = (bf16[256,768]{1,0:T(8,128)(2,1)S(1)}, bf16[256,768]{1,0:T(8,128)(2,1)}, u32[]{:S(2)}) copy-start(bf16[256,768]{1,0:T(8,128)(2,1)} %param.12) | copy-start | bytes 1179652
  163.9 90.7 %reduce-scatter.6.cloned.1.call-start = ((), (), s32[]{:S(2)}) async-start(), calls=%async_computation.11 | async-start | bytes 3932160 | tf_op jit(solution)/shard_map/reduce_scatter | solution.py:149
  191.6 20.9 %copy-start.61 = (f32[1,768,768]{2,1,0:T(8,128)S(1)}, f32[1,768,768]{2,1,0:T(8,128)}, u32[]{:S(2)}) copy-start(f32[1,768,768]{2,1,0:T(8,128)} %param.22) | copy-start | bytes 7077892
  216.5 43.7 %copy-start.34 = (s32[256]{0:T(256)S(1)}, s32[256]{0:T(256)}, u32[]{:S(2)}) copy-start(s32[256]{0:T(256)} %param.23) | copy-start | bytes 3076
  216.5 128.1 %copy-start.58 = (s32[256]{0:T(256)S(1)}, s32[256]{0:T(256)}, u32[]{:S(2)}) copy-start(s32[256]{0:T(256)} %copy-done.57) | copy-start | bytes 3076
  216.6 135.8 %copy-start.5 = (bf16[256,768]{1,0:T(8,128)(2,1)S(1)}, bf16[256,768]{1,0:T(8,128)(2,1)}, u32[]{:S(2)}) copy-start(bf16[256,768]{1,0:T(8,128)(2,1)} %param.13) | copy-start | bytes 1179652
  254.7 94.1 %all-to-all-start.1 = ((bf16[8,64,768]{2,1,0:T(8,128)(2,1)}), bf16[8,64,768]{2,1,0:T(8,128)(2,1)}, u32[]{:S(2)}, u32[]{:S(2)}) async-start(bf16[8,64,768]{2,1,0:T(8,128)(2,1)} %bitcast.102), calls=%async_computation.2 | async-start | bytes 1572864 | tf_op jit(solution)/shard_map/all_to_all | solution.py:157
  260.2 150.1 %all-gather.12.cloned.1.call-start = ((), (), s32[]{:S(2)}) async-start(), calls=%async_computation.12 | async-start | bytes 3932160 | tf_op jit(solution)/shard_map/all_gather | solution.py:168
  347.6 7.3 copy-start.26
  383.4 81.2 %reduce-scatter.8.cloned.1.call-start = ((), (), s32[]{:S(2)}) async-start(), calls=%async_computation.13 | async-start | bytes 3932160 | tf_op jit(solution)/shard_map/reduce_scatter | solution.py:176
  410.2 12.3 %copy-start.62 = (f32[1,768,768]{2,1,0:T(8,128)S(1)}, f32[1,768,768]{2,1,0:T(8,128)}, u32[]{:S(2)}) copy-start(f32[1,768,768]{2,1,0:T(8,128)} %param.21) | copy-start | bytes 7077892
  426.5 67.4 %copy-start.27 = (f32[256,8]{0,1:T(8,128)S(1)}, f32[256,8]{0,1:T(8,128)}, u32[]{:S(2)}) copy-start(f32[256,8]{0,1:T(8,128)} %copy-done.26) | copy-start | bytes 24580
  426.6 67.4 %copy-start.33 = (f32[768]{0:T(1024)S(1)}, f32[768]{0:T(1024)}, u32[]{:S(2)}) copy-start(f32[768]{0:T(1024)} %copy-done.32) | copy-start | bytes 9220
  426.6 173.4 %reduce-scatter.12.cloned.1.call-start = ((), (), s32[]{:S(2)}) async-start(), calls=%async_computation.15 | async-start | bytes 2433024 | tf_op jit(solution)/shard_map/reduce_scatter | solution.py:245
  490.4 6.9 copy-start.13
  494.0 6.5 copy-start.6
  494.0 6.7 copy-start.16
  499.6 3.0 copy-start.50
  502.6 222.8 %reduce-scatter.10.cloned.1.call-start = ((), (), s32[]{:S(2)}) async-start(), calls=%async_computation.14 | async-start | bytes 7299072 | tf_op jit(solution)/shard_map/reduce_scatter | solution.py:244
  506.6 2.3 copy-start.18
  506.6 2.3 copy-start.15
  506.6 2.3 copy-start.29
  510.3 2.2 copy-start.2
  510.3 2.2 copy-start.31
  510.4 2.2 copy-start.37
  510.4 2.2 copy-start.43
  518.7 7.2 copy-start.60
  518.7 7.2 copy-start.65
  525.8 4.2 copy-start.21
  525.9 4.2 copy-start.23
  525.9 4.2 copy-start.25
  525.9 4.2 copy-start.38
  525.9 4.2 copy-start.59
  530.1 1.8 copy-start.44
  530.1 2.3 copy-start.48
  530.1 47.5 %copy-start.4 = (f32[256,768]{1,0:T(8,128)S(1)}, f32[256,768]{1,0:T(8,128)}, u32[]{:S(2)}) copy-start(f32[256,768]{1,0:T(8,128)} %copy-done.3) | copy-start | bytes 2359300
  530.1 47.5 %copy-start.7 = (bf16[256,768]{1,0:T(8,128)(2,1)S(1)}, bf16[256,768]{1,0:T(8,128)(2,1)}, u32[]{:S(2)}) copy-start(bf16[256,768]{1,0:T(8,128)(2,1)} %param.13) | copy-start | bytes 1179652
  (27 other events, 27.1 us)
Sparse Core Ops, SparseCore 0:
  11.5 63.0 all-gather.5
  78.0 52.8 all-gather.7
  164.1 27.4 all-gather.9
  216.7 37.9 reduce-scatter.5
  383.6 26.6 all-gather.11
  426.7 37.9 reduce-scatter.7
  502.7 97.2 reduce-scatter.11
  607.2 118.1 reduce-scatter.9
where the time goes:
time: 742 us; the launch traced here: 734 us
  waiting for transfers between devices  331 us (45%)
  blocking collectives  240 us (32%)
  matrix products  76.8 us (10%)
  local copies, waits for them, and re-layouts  34 us (5%)
  other arithmetic  28.8 us (4%)
  between operations  17.1 us (2%)
    reduce_scatter x1, waiting for transfers between devices, on_device(): lax.psum_scatter(qkv_local, ('expert', 'hid'), scatter_dimension=0, tiled...  125 us
    psum x2, blocking collectives, on_device(): lax.psum((jnp.sum(onehot_f, axis=0), jnp.sum(router_probs, axis=0)), ('ex...  81.7 us
    all_gather x1, waiting for transfers between devices, on_device(): lax.all_gather(proj_weight.astype(half), ('expert', 'hid'), axis=0, tiled...  45.3 us
    unnamed x1, blocking collectives  42.3 us
    all_gather x1, blocking collectives, on_device(): lax.all_gather(router_weight.astype(half), ('expert', 'hid'), axis=0, til...  39.9 us
    reduce_scatter x1, waiting for transfers between devices, on_device(): lax.psum_scatter(jnp.dot(row_block, down_local, preferred_element_type=si...  38.1 us
    reduce_scatter x1, waiting for transfers between devices, on_device(): lax.psum_scatter(contract_cols(row_block, in_local).astype(jnp.bfloat16),...  38 us
    all_gather x1, waiting for transfers between devices, on_device(): lax.all_gather(incoming, 'hid', axis=0, tiled=True).reshape(-1, model_width)  27.4 us
  transfers between devices with their start and end apart: 9, of which 8 were waited for; matrix products, arithmetic and copies ran while one was open for 9% of the time, Pallas kernels for 0%

commit v1 on v0

--- a/solution.py
+++ b/solution.py
@@ -1,8 +1,10 @@
-from functools import partial
+import functools
 
 import jax
 import jax.numpy as jnp
 from jax import lax
+from jax.experimental import pallas as pl
+from jax.experimental.pallas import tpu as pltpu
 from jax.sharding import PartitionSpec as P
 
 HEADS = 12
@@ -11,14 +13,327 @@
 epsilon = 1e-05
 balance_weight = 3.0
 masked_score = -1000000000.0
-
-
-def for_sending(value):
-
-    def short(part):
-        return part.astype(jnp.bfloat16) if part.dtype == jnp.float32 else part
-
-    return jax.tree.map(short, value)
+MESH = pl.DeviceIdType.MESH
+half = jnp.bfloat16
+single = jnp.float32
+
+
+def remote(src, dst, send_sem, recv_sem, device):
+    return pltpu.make_async_remote_copy(
+        src_ref=src, dst_ref=dst, send_sem=send_sem, recv_sem=recv_sem,
+        device_id=device, device_id_type=MESH,
+    )
+
+
+def dot(a, b):
+    return jnp.dot(a, b, preferred_element_type=single)
+
+
+def dot_cols(a, b):
+    return lax.dot_general(a, b, (((1,), (1,)), ((), ())), preferred_element_type=single)
+
+
+def dot_rows(a, b):
+    return lax.dot_general(a, b, (((0,), (0,)), ((), ())), preferred_element_type=single)
+
+
+def expert_kernel(
+    E, X, G, out_h, out_g, w_in, w_dn, ret_o, ret_g, in_grad, dn_grad,
+    xh, xg, win, wdn, act, gbef, po, pg, so, sg, ro, rg, to, tg, gs, gr, before, ga,
+    send_a, recv_a, send_x, recv_x, send_p, recv_p, send_r, recv_r, send_w, recv_w, send_d, recv_d,
+):
+    e = lax.axis_index("expert")
+    h = lax.axis_index("hid")
+    x = lax.div(h, 2)
+    c = lax.rem(h, 2)
+    other = 1 - c
+    D = w_in.shape[0]
+    Fq = w_in.shape[1]
+    cap = out_h.shape[1]
+    NG = E // G
+    rows = G * cap
+    core_peer = (e, x * 2 + other)
+
+    def expert_peer(k):
+        return (lax.rem(e + k, E), h)
+
+    def x_peer(d):
+        return (e, lax.rem(x + d, X) * 2 + c)
+
+    barrier = pltpu.get_barrier_semaphore()
+
+    @pl.loop(1, E)
+    def _(k):
+        pl.semaphore_signal(barrier, inc=1, device_id=expert_peer(k), device_id_type=MESH)
+
+    for d in range(1, X):
+        pl.semaphore_signal(barrier, inc=1, device_id=x_peer(d), device_id_type=MESH)
+    pl.semaphore_signal(barrier, inc=1, device_id=core_peer, device_id_type=MESH)
+    pl.semaphore_wait(barrier, E - 1 + X - 1 + 1)
+
+    def dispatch(k, part):
+        to_e = lax.rem(e + E - k, E)
+        src, dst = ((out_h, xh), (out_g, xg))[part]
+        return remote(src.at[to_e], dst.at[0, k], send_a.at[part, k], recv_a.at[part, k], (to_e, h))
+
+    def forward(k, part, d):
+        dst = (xh, xg)[part]
+        return remote(
+            dst.at[0, k], dst.at[X - d, k], send_x.at[part, d - 1, k], recv_x.at[part, X - d - 1, k],
+            x_peer(d),
+        )
+
+    @pl.loop(1, E)
+    def _(k):
+        dispatch(k, 0).start()
+        dispatch(k, 1).start()
+
+    xh[0, 0] = out_h[e]
+    xg[0, 0] = out_g[e]
+
+    step = 32
+
+    @pl.loop(0, D // step)
+    def _(i):
+        at = pl.ds(pl.multiple_of(i * step, step), step)
+        win[c, at, :] = w_in[at, :].astype(half)
+
+    @pl.loop(0, Fq // step)
+    def _(i):
+        at = pl.ds(pl.multiple_of(i * step, step), step)
+        wdn[c, at, :] = w_dn[at, :].astype(half)
+
+    win_copy = remote(win.at[c], win.at[c], send_w.at[0], recv_w.at[0], core_peer)
+    wdn_copy = remote(wdn.at[c], wdn.at[c], send_w.at[1], recv_w.at[1], core_peer)
+    win_copy.start()
+    wdn_copy.start()
+
+    def pass_on(g):
+        @pl.loop(0, G)
+        def _(i):
+            k = g * G + i
+
+            @pl.when(k > 0)
+            def _():
+                dispatch(k, 0).wait_recv()
+                dispatch(k, 1).wait_recv()
+
+            for d in range(1, X):
+                forward(k, 0, d).start()
+                forward(k, 1, d).start()
+
+    def take(j, g):
+        @pl.loop(0, G)
+        def _(i):
+            k = g * G + i
+            forward(k, 0, X - j).wait_recv()
+            forward(k, 1, X - j).wait_recv()
+
+    def compute(j, g):
+        slots = pl.ds(g * G, G)
+        t = j * NG + g
+        xh_g = xh[j, slots].reshape(rows, D)
+        xg_g = xg[j, slots].reshape(rows, D)
+        for q in range(2):
+            before[...] = dot(xh_g, win[q])
+            ga[...] = dot_cols(xg_g, wdn[q])
+
+            @pl.loop(0, rows // step)
+            def _(i):
+                at = pl.ds(pl.multiple_of(i * step, step), step)
+                v = before[at, :]
+                cdf = 0.5 * (1.0 + lax.erf(v * (0.5 ** 0.5)))
+                slope = cdf + v * (jnp.exp(-0.5 * v * v) * 0.3989422804014327)
+                act[q, t, at, :] = (v * cdf).astype(half)
+                gbef[q, t, at, :] = (slope * ga[at, :]).astype(half)
+
+        out = dot(act[0, t], wdn[0]) + dot(act[1, t], wdn[1])
+        gin = dot_cols(gbef[0, t], win[0]) + dot_cols(gbef[1, t], win[1])
+        return out, gin
+
+    def partial(j, g, part):
+        src, dst = ((so, ro), (sg, rg))[part]
+        return remote(
+            src.at[j - 1, pl.ds(g * G, G)], dst.at[X - j - 1, pl.ds(g * G, G)],
+            send_p.at[part, j - 1, g], recv_p.at[part, X - j - 1, g], x_peer(j),
+        )
+
+    def give_back(k, part):
+        src, dst = ((to, ret_o), (tg, ret_g))[part]
+        return remote(src.at[k], dst.at[e], send_r.at[part, k], recv_r.at[part, k], expert_peer(k))
+
+    def finish(g):
+        for j in range(1, X):
+            for part in range(2):
+                partial(X - j, g, part).wait_recv()
+
+        @pl.loop(0, G)
+        def _(i):
+            k = g * G + i
+            for part, own, got, total in ((0, po, ro, to), (1, pg, rg, tg)):
+                value = own[k]
+                for j in range(X - 1):
+                    value = value + got[j, k].astype(single)
+                total[k] = value.astype(half)
+
+            @pl.when(k > 0)
+            def _():
+                give_back(k, 0).start()
+                give_back(k, 1).start()
+
+            @pl.when(k == 0)
+            def _():
+                ret_o[e] = to[0]
+                ret_g[e] = tg[0]
+
+    @pl.loop(0, NG * X)
+    def _(t):
+        g = lax.div(t, X)
+        j = lax.rem(t, X)
+
+        @pl.when(j == 0)
+        def _():
+            pass_on(g)
+
+        for d in range(1, X):
+            @pl.when(j == d)
+            def _():
+                take(d, g)
+
+        @pl.when(t == 0)
+        def _():
+            win_copy.wait_recv()
+            wdn_copy.wait_recv()
+
+        out, gin = compute(j, g)
+        slots = pl.ds(g * G, G)
+
+        @pl.when(j == 0)
+        def _():
+            po[slots] = out.reshape(G, cap, D)
+            pg[slots] = gin.reshape(G, cap, D)
+
+        for d in range(1, X):
+            @pl.when(j == d)
+            def _():
+                so[d - 1, slots] = out.astype(half).reshape(G, cap, D)
+                sg[d - 1, slots] = gin.astype(half).reshape(G, cap, D)
+                partial(d, g, 0).start()
+                partial(d, g, 1).start()
+
+        @pl.when((j == 0) & (g > 0))
+        def _():
+            finish(g - 1)
+
+    finish(NG - 1)
+
+    T = X * NG * rows
+    tile = 256 if Fq % 256 == 0 else 128
+
+    def grad_in(q, i):
+        lhs = xh[:, :, :, pl.ds(pl.multiple_of(i * tile, tile), tile)].reshape(T, tile)
+        return dot_rows(lhs, gbef[q].reshape(T, Fq))
+
+    def grad_dn(q, i):
+        lhs = act[q, :, :, pl.ds(pl.multiple_of(i * tile, tile), tile)].reshape(T, tile)
+        return dot_rows(lhs, xg[...].reshape(T, D))
+
+    @pl.loop(0, D // tile)
+    def _(i):
+        gs[0, pl.ds(pl.multiple_of(i * tile, tile), tile), :Fq] = grad_in(other, i)
+
+    in_copy = remote(gs.at[0, :, :Fq], gr.at[0, :, :Fq], send_d.at[0], recv_d.at[0], core_peer)
+    in_copy.start()
+
+    @pl.loop(0, Fq // tile)
+    def _(i):
+        gs[1, pl.ds(pl.multiple_of(i * tile, tile), tile), :] = grad_dn(other, i)
+
+    dn_copy = remote(gs.at[1, :Fq], gr.at[1, :Fq], send_d.at[1], recv_d.at[1], core_peer)
+    dn_copy.start()
+
+    @pl.loop(0, D // tile)
+    def _(i):
+        in_grad[pl.ds(pl.multiple_of(i * tile, tile), tile), :] = grad_in(c, i)
+
+    @pl.loop(0, Fq // tile)
+    def _(i):
+        dn_grad[pl.ds(pl.multiple_of(i * tile, tile), tile), :] = grad_dn(c, i)
+
+    in_copy.wait_recv()
+
+    @pl.loop(0, D // step)
+    def _(i):
+        at = pl.ds(pl.multiple_of(i * step, step), step)
+        in_grad[at, :] += gr[0, at, :Fq]
+
+    dn_copy.wait_recv()
+
+    @pl.loop(0, Fq // step)
+    def _(i):
+        at = pl.ds(pl.multiple_of(i * step, step), step)
+        dn_grad[at, :] += gr[1, at, :]
+
+    win_copy.wait_send()
+    wdn_copy.wait_send()
+    in_copy.wait_send()
+    dn_copy.wait_send()
+
+    @pl.loop(0, E)
+    def _(k):
+        for part in range(2):
+            @pl.when(k > 0)
+            def _():
+                dispatch(k, part).wait_send()
+                give_back(k, part).wait()
+
+            for d in range(1, X):
+                forward(k, part, d).wait_send()
+
+    for g in range(NG):
+        for part in range(2):
+            for j in range(1, X):
+                partial(j, g, part).wait_send()
+
+
+def expert_call(out_h, out_g, w_in, w_dn, X):
+    E, cap, D = out_h.shape
+    Fq = w_in.shape[1]
+    G = max(1, min(E, 256 // cap))
+    NG = E // G
+    rows = G * cap
+    dma = pltpu.SemaphoreType.DMA
+    token = jax.ShapeDtypeStruct((E, cap, D), half)
+    vmem = pl.BlockSpec(memory_space=pltpu.VMEM)
+    return pl.pallas_call(
+        functools.partial(expert_kernel, E, X, G),
+        out_shape=(
+            token, token,
+            jax.ShapeDtypeStruct((D, Fq), single), jax.ShapeDtypeStruct((Fq, D), single),
+        ),
+        in_specs=[vmem] * 4,
+        out_specs=(vmem,) * 4,
+        scratch_shapes=[
+            pltpu.VMEM((X, E, cap, D), half), pltpu.VMEM((X, E, cap, D), half),
+            pltpu.VMEM((2, D, Fq), half), pltpu.VMEM((2, Fq, D), half),
+            pltpu.VMEM((2, X * NG, rows, Fq), half), pltpu.VMEM((2, X * NG, rows, Fq), half),
+            pltpu.VMEM((E, cap, D), single), pltpu.VMEM((E, cap, D), single),
+            pltpu.VMEM((X - 1, E, cap, D), half), pltpu.VMEM((X - 1, E, cap, D), half),
+            pltpu.VMEM((X - 1, E, cap, D), half), pltpu.VMEM((X - 1, E, cap, D), half),
+            pltpu.VMEM((E, cap, D), half), pltpu.VMEM((E, cap, D), half),
+            pltpu.VMEM((2, D, D), single), pltpu.VMEM((2, D, D), single),
+            pltpu.VMEM((rows, Fq), single), pltpu.VMEM((rows, Fq), single),
+            dma((2, E)), dma((2, E)),
+            dma((2, X - 1, E)), dma((2, X - 1, E)),
+            dma((2, X - 1, NG)), dma((2, X - 1, NG)),
+            dma((2, E)), dma((2, E)),
+            dma((2,)), dma((2,)), dma((2,)), dma((2,)),
+        ],
+        compiler_params=pltpu.CompilerParams(
+            collective_id=1, has_side_effects=True, vmem_limit_bytes=60 * 1024 * 1024,
+        ),
+        name="experts",
+    )(out_h, out_g, w_in, w_dn)
 
 
 def norm_apply(values, gain, shift):
@@ -136,54 +451,17 @@
     expert_scale = balance_weight * experts * counts / total_tokens
     balance_loss = jnp.sum(expert_scale * prob_total) / total_tokens
     outgoing = take_rows(hidden_b, slot_owner).reshape(experts, capacity, model_width)
-    incoming = lax.all_to_all(outgoing, "expert", split_axis=0, concat_axis=0, tiled=True)
-    in_local = expert_in[0].astype(half)
-    down_local = expert_down[0].astype(half)
-    gelu_exact = partial(jax.nn.gelu, approximate=False)
-    local_rows = experts * capacity
-    dispatched_rows = lax.all_gather(incoming, "hid", axis=0, tiled=True).reshape(-1, model_width)
-    before = jnp.dot(dispatched_rows, in_local, preferred_element_type=single)
-    active_f, gelu_back = jax.vjp(gelu_exact, before)
-    active = active_f.astype(half)
-    row_block = lax.slice_in_dim(active, 0, lax.axis_size("hid") * local_rows, axis=0)
-    expert_out = lax.psum_scatter(
-        jnp.dot(row_block, down_local, preferred_element_type=single).astype(jnp.bfloat16),
-        "hid",
-        scatter_dimension=0,
-        tiled=True,
-    ).astype(jnp.float32)
-    returning = expert_out.astype(half).reshape(experts, capacity, model_width)
-    arrived = (
-        lax.all_to_all(for_sending(returning), "expert", split_axis=0, concat_axis=0, tiled=True)
-        .astype(returning.dtype)
-        .reshape(local_rows, model_width)
-    )
-    expert_tok = arrived[position]
-    layer_output = (residual + gate_value[:, None] * expert_tok.astype(single)).astype(half)
     cotangent = out_cotangent.astype(single)
     grad_expert = (gate_value[:, None] * cotangent).astype(half)
+    outgoing_grad = take_rows(grad_expert, slot_owner).reshape(experts, capacity, model_width)
+    arrived, back_rows, in_grad, down_grad = expert_call(
+        outgoing, outgoing_grad, expert_in[0], expert_down[0], lax.axis_size("hid") // 2
+    )
+    local_rows = experts * capacity
+    expert_tok = arrived.reshape(local_rows, model_width)[position]
+    layer_output = (residual + gate_value[:, None] * expert_tok.astype(single)).astype(half)
     grad_gate = jnp.sum(cotangent * expert_tok.astype(single), axis=1)
-    outgoing_grad = take_rows(grad_expert, slot_owner).reshape(experts, capacity, model_width)
-    incoming_grad = lax.all_to_all(outgoing_grad, "expert", split_axis=0, concat_axis=0, tiled=True)
-    grad_rows_all = lax.all_gather(incoming_grad, "hid", axis=0, tiled=True).reshape(
-        -1, model_width
-    )
-    grad_active = contract_cols(grad_rows_all, down_local)
-    grad_before = gelu_back(grad_active)[0].astype(half)
-    down_grad = contract_rows(active, grad_rows_all)
-    in_grad = contract_rows(dispatched_rows, grad_before)
-    row_block = grad_before
-    grad_mine = lax.psum_scatter(
-        contract_cols(row_block, in_local).astype(jnp.bfloat16),
-        "hid",
-        scatter_dimension=0,
-        tiled=True,
-    ).astype(jnp.float32)
-    sending_back = grad_mine.astype(half).reshape(experts, capacity, model_width)
-    back_rows = lax.all_to_all(
-        sending_back, "expert", split_axis=0, concat_axis=0, tiled=True
-    ).reshape(local_rows, model_width)
-    grad_dispatch = back_rows[position].astype(single)
+    grad_dispatch = back_rows.reshape(local_rows, model_width)[position].astype(single)
     grad_probs = onehot_f * grad_gate[:, None] + expert_scale[None, :]
     grad_logits = (
         router_probs * (grad_probs - jnp.sum(router_probs * grad_probs, axis=1, keepdims=True))

time: 742 us -> 538 us (0.73)
  waiting for transfers between devices: 331 us -> 175 us
  Pallas kernels: 0 us -> 105 us
  blocking collectives: 240 us -> 167 us
  matrix products: 76.8 us -> 26.3 us
  other arithmetic: 28.8 us -> 19.6 us
    pallas_call x0 -> x1, Pallas kernels: none -> 105 us  [expert_call(): pl.pallas_call(functools.partial(expert_kernel, E, X, G), out_shape=(toke...]
    reduce_scatter x2 -> x0, waiting for transfers between devices: 76.1 us -> none  [the longest x1 38.1 us: on_device(): lax.psum_scatter(jnp.dot(row_block, down_local, preferred_element_type=si...]
    all_to_all x3 -> x0, blocking collectives: 75.9 us -> none  [the longest x1 25.8 us: on_device(): lax.all_to_all(sending_back, 'expert', split_axis=0, concat_axis=0, tiled...]
    all_gather x2 -> x0, waiting for transfers between devices: 54 us -> none  [the longest x1 27.4 us: on_device(): lax.all_gather(incoming, 'hid', axis=0, tiled=True).reshape(-1, model_width)]
    all_gather x1, waiting for transfers between devices: 45.3 us -> 19.3 us  [on_device(): lax.all_gather(proj_weight.astype(half), ('expert', 'hid'), axis=0, tiled...]
    dot_general x2 -> x0, matrix products: 23.2 us -> none  [the longest x1 19.2 us: on_device(): before = jnp.dot(dispatched_rows, in_local, preferred_element_type=single)]
    dot_general x5 -> x3, matrix products: 21.5 us -> 8.99 us  [contract_cols(): lax.dot_general(left, right, (((1,), (1,)), ((), ())), preferred_element_...]
    dot_general x5 -> x3, matrix products: 18.2 us -> 6.33 us  [contract_rows(): lax.dot_general(left, right, (((0,), (0,)), ((), ())), preferred_element_...]
  transfers between devices with their start and end apart: 9 -> 4, of which waited for: 8 -> 3; matrix products, arithmetic and copies ran while one was open for 9% -> 8% of each run, Pallas kernels for 0% -> 0%
where the time goes in v1:
time: 538 us; the launch traced here: 537 us
  waiting for transfers between devices  175 us (33%)
  blocking collectives  167 us (31%)
  Pallas kernels  105 us (20%)
  local copies, waits for them, and re-layouts  27.4 us (5%)
  matrix products  26.3 us (5%)
  other arithmetic  19.6 us (4%)
  between operations  16.3 us (3%)
    reduce_scatter x1, waiting for transfers between devices, on_device(): lax.psum_scatter(qkv_local, ('expert', 'hid'), scatter_dimension=0, tiled...  125 us
    pallas_call x1, Pallas kernels, expert_call(): pl.pallas_call(functools.partial(expert_kernel, E, X, G), out_shape=(toke...  105 us
    psum x2, blocking collectives, on_device(): lax.psum((jnp.sum(onehot_f, axis=0), jnp.sum(router_probs, axis=0)), ('ex...  84.4 us
    unnamed x1, blocking collectives  42.3 us
    all_gather x1, blocking collectives, on_device(): lax.all_gather(router_weight.astype(half), ('expert', 'hid'), axis=0, til...  40.2 us
    reduce_scatter x1, waiting for transfers between devices, on_device(): lax.psum_scatter(proj_local, ('expert', 'hid'), scatter_dimension=0, tile...  30.9 us
    all_gather x1, waiting for transfers between devices, on_device(): lax.all_gather(proj_weight.astype(half), ('expert', 'hid'), axis=0, tiled...  19.3 us
    unnamed x116, local copies, waits for them, and re-layouts  13.1 us
  transfers between devices with their start and end apart: 4, of which 3 were waited for; matrix products, arithmetic and copies ran while one was open for 8% of the time, Pallas kernels for 0%

profile of v1, /device:TPU:0, one launch (start us, length us, event | category | flops | bytes accessed | tf_op | source)
XLA Modules:
  0.0 536.9 jit_solution(3064248253534197280)
XLA Ops:
  7.2 1.6 convert_element_type.131
  8.9 1.5 convert_element_type.136
  10.5 0.7 convert_element_type.126
  11.2 0.7 convert_element_type.128
  11.9 0.7 convert_element_type.137
  13.2 1.1 convert_reduce_fusion
  14.3 0.7 convert_bitcast_fusion
  15.8 42.3 %all-reduce.12 = (bf16[768]{0:T(1024)(128)(2,1)S(1)}, bf16[768]{0:T(1024)(128)(2,1)S(1)}, bf16[768]{0:T(1024)(128)(2,1)S(1)}, bf16[768]{0:T(1024)(128)(2,1)S(1)}) all-reduce(bf16[768]{0:T(1024)(128)(2,1)S(1)} %dynamic-update-slice.1, bf16[768]{0:T(1024)(128)(2,1)S(1)} %dynamic-update-slice, ...), channel_id=1, replica_groups=mesh['expert'=8,'hid'=4] {'expert','hid'}, use_global_device_ids=true, to_apply=%add.3 | all-reduce | flops 3072 | bytes 12288
  58.1 0.7 fusion.23
  59.6 0.8 fusion.22
  60.4 0.7 compare_select_fusion.1
  61.1 1.4 scatter_custom_fusion
  62.5 40.2 %all-gather = bf16[32,24,8]{1,2,0:T(8,128)(2,1)S(1)} all-gather(bf16[1,24,8]{1,2,0:T(8,128)(2,1)S(1)} %convert_bitcast_fusion), channel_id=1, replica_groups=mesh['expert'=8,'hid'=4] {'expert','hid'}, dimensions={0}, use_global_device_ids=true | all-gather | bytes 12672 | tf_op jit(solution)/shard_map/all_gather | solution.py:400
  102.9 1.2 fusion.15
  104.2 3.3 convolution_convert_fusion
  108.2 0.7 fusion
  109.6 0.9 copy-done
  110.5 0.9 convolution_convert_fusion.3
  111.4 19.3 %all-gather.6.cloned.1.call-done = bf16[768,768]{1,0:T(8,128)(2,1)} async-done(((bf16[24,768]{1,0:T(8,128)(2,1)}), bf16[768,768]{1,0:T(8,128)(2,1)}) %all-gather.6.cloned.1.call-update) | async-done | bytes 1179664 | tf_op jit(solution)/shard_map/all_gather | solution.py:399
  130.7 1.9 fusion.48
  133.5 39.4 %psum.14 = f32[8]{0:T(128)S(1)} all-reduce(f32[8]{0:T(128)S(1)} %get-tuple-element.80), channel_id=1, replica_groups=mesh['expert'=8,'hid'=4] {'expert','hid'}, use_global_device_ids=true, to_apply=%region_14.15 | all-reduce | flops 8 | bytes 64 | tf_op jit(solution)/shard_map/psum | solution.py:448
  173.1 2.7 gather_fusion.1
  175.8 2.7 gather_fusion
  178.5 104.6 %experts.1 = (bf16[8,64,768]{2,1,0:T(8,128)(2,1)}, bf16[8,64,768]{2,1,0:T(8,128)(2,1)}, f32[768,768]{1,0:T(8,128)}, f32[768,768]{1,0:T(8,128)}) custom-call(bf16[8,64,768]{2,1,0:T(8,128)(2,1)} %bitcast.67, bf16[8,64,768]{2,1,0:T(8,128)(2,1)} %bitcast.66, f32[768,768]{1,0:T(8,128)} %bitcast.68, f32[768,768]{1,0:T(8,128)} %bitcast.69), custom_call_target="tpu_custom_call" | custom-call | tf_op jit(solution)/shard_map/experts/pallas_call | solution.py:308
  283.1 2.7 gather_fusion.2
  285.8 1.9 gather_fusion.3
  288.6 2.2 multiply_reduce_fusion.1
  290.9 1.2 fusion.46
  292.3 0.7 copy-done.4
  292.9 0.7 copy-done.10
  293.7 1.9 fusion.50
  295.9 2.8 convolution_convert_fusion.2
  298.6 1.9 copy.50
  300.6 2.2 multiply_reduce_fusion
  302.8 0.9 multiply_convert_fusion
  304.9 0.8 convolution_convert_fusion.1
  305.7 0.7 copy-done.24
  306.5 4.2 fusion.20
  310.7 1.0 copy-done.21
  312.0 4.0 fusion.45
  316.8 45.0 %all-reduce.11 = (f32[8]{0:T(128)S(1)}, f32[768,8]{0,1:T(8,128)S(1)}, f32[768]{0:T(1024)S(1)}, f32[768]{0:T(1024)S(1)}, f32[768]{0:T(1024)S(1)}, /*index=5*/f32[768]{0:T(1024)S(1)}) all-reduce(f32[8]{0:T(128)} %get-tuple-element.79, f32[768,8]{0,1:T(8,128)S(1)} %fusion.38, ...), channel_id=1, replica_groups=mesh['expert'=8,'hid'=4] {'expert','hid'}, use_global_device_ids=true, to_apply=%region_16.17 | all-reduce | flops 9224 | bytes 73792 | tf_op jit(solution)/shard_map/psum | solution.py:448
  364.1 1.3 multiply_reduce_fusion.6
  366.0 0.7 constant_dynamic-slice_fusion
  366.7 1.8 add_convert_fusion
  368.5 30.9 %reduce-scatter.6.cloned.1.call-done = f32[24,768]{1,0:T(8,128)} async-done(((f32[768,768]{1,0:T(8,128)}), f32[24,768]{1,0:T(8,128)}) %reduce-scatter.6.cloned.1.call-update) | async-done | bytes 73744 | tf_op jit(solution)/shard_map/reduce_scatter | solution.py:523
  399.4 125.2 %reduce-scatter.4.cloned.1.call-done = f32[24,2304]{1,0:T(8,128)} async-done(((f32[768,2304]{1,0:T(8,128)}), f32[24,2304]{1,0:T(8,128)}) %reduce-scatter.4.cloned.1.call-update) | async-done | bytes 221200 | tf_op jit(solution)/shard_map/reduce_scatter | solution.py:522
  524.6 3.2 copy.68
  527.8 1.4 copy.69
  (162 shorter events, 10.8 us)
Async XLA Ops:
  7.2 97.0 %all-gather.4.cloned.1.call-start = ((), (), s32[]{:S(2)}) async-start(), calls=%async_computation.2 | async-start | bytes 3649536 | tf_op jit(solution)/shard_map/all_gather | solution.py:398
  8.8 121.9 %all-gather.6.cloned.1.call-start = ((), (), s32[]{:S(2)}) async-start(), calls=%async_computation.3 | async-start | bytes 1216512 | tf_op jit(solution)/shard_map/all_gather | solution.py:399
  10.4 389.0 %reduce-scatter.6.cloned.1.call-start = ((), (), s32[]{:S(2)}) async-start(), calls=%async_computation.5 | async-start | bytes 2433024 | tf_op jit(solution)/shard_map/reduce_scatter | solution.py:523
  10.5 99.1 %copy-start.16 = (pred[256,256]{0,1:T(8,128)(4,1)}, pred[256,256]{0,1:T(8,128)(4,1)S(1)}, u32[]{:S(2)}) copy-start(pred[256,256]{0,1:T(8,128)(4,1)S(1)} %iota_compare_fusion) | copy-start | bytes 196612
  14.3 93.2 %copy-start.32 = (f32[256]{0:T(256)}, f32[256]{0:T(256)S(1)}, u32[]{:S(2)}) copy-start(f32[256]{0:T(256)S(1)} %broadcast_multiply_fusion.1) | copy-start | bytes 3076
  104.1 3.4 copy-start.45
  104.2 3.4 copy-start.37
  107.8 1.1 copy-start.11
  108.0 1.6 copy-start.13
  108.2 1.4 copy-start.18
  108.9 1.7 copy-start
  108.9 21.8 %copy-start.2 = (bf16[256,768]{1,0:T(8,128)(2,1)S(1)}, bf16[256,768]{1,0:T(8,128)(2,1)}, u32[]{:S(2)}) copy-start(bf16[256,768]{1,0:T(8,128)(2,1)} %param.12) | copy-start | bytes 1179652
  109.6 23.0 %copy-start.26 = (f32[12,256]{1,0:T(8,128)}, f32[12,256]{1,0:T(8,128)S(1)}, u32[]{:S(2)}) copy-start(f32[12,256]{1,0:T(8,128)S(1)} %log_add_fusion) | copy-start | bytes 36868
  111.4 21.9 %copy-start.28 = (s32[256]{0:T(256)S(1)}, s32[256]{0:T(256)}, u32[]{:S(2)}) copy-start(s32[256]{0:T(256)} %param.23) | copy-start | bytes 3076
  111.4 61.5 %copy-start.6 = (bf16[256,768]{1,0:T(8,128)(2,1)S(1)}, bf16[256,768]{1,0:T(8,128)(2,1)}, u32[]{:S(2)}) copy-start(bf16[256,768]{1,0:T(8,128)(2,1)} %param.13) | copy-start | bytes 1179652
  133.0 39.9 %copy-start.8 = (bf16[256,768]{1,0:T(8,128)(2,1)}, bf16[256,768]{1,0:T(8,128)(2,1)S(1)}, u32[]{:S(2)}) copy-start(bf16[256,768]{1,0:T(8,128)(2,1)S(1)} %add_convert_fusion.1) | copy-start | bytes 1179652
  133.3 155.3 %copy-start.30 = (f32[256]{0:T(256)}, f32[256]{0:T(256)S(1)}, u32[]{:S(2)}) copy-start(f32[256]{0:T(256)S(1)} %get-tuple-element.102) | copy-start | bytes 3076
  133.3 155.3 %copy-start.35 = (f32[256]{0:T(256)}, f32[256]{0:T(256)S(1)}, u32[]{:S(2)}) copy-start(f32[256]{0:T(256)S(1)} %fusion.25) | copy-start | bytes 3076
  172.8 3.0 copy-start.49
  172.8 115.8 %copy-start.47 = (f32[8]{0:T(128)}, f32[8]{0:T(128)S(1)}, u32[]{:S(2)}) copy-start(f32[8]{0:T(128)S(1)} %broadcast_multiply_fusion.2) | copy-start | bytes 100
  283.1 2.7 copy-start.3
  288.0 4.3 copy-start.40
  288.6 3.6 copy-start.43
  295.6 5.0 copy-start.1
  295.6 229.0 %reduce-scatter.4.cloned.1.call-start = ((), (), s32[]{:S(2)}) async-start(), calls=%async_computation.4 | async-start | bytes 7299072 | tf_op jit(solution)/shard_map/reduce_scatter | solution.py:522
  300.6 2.2 copy-start.17
  300.6 2.2 copy-start.27
  302.8 1.6 copy-start.12
  303.8 1.0 copy-start.19
  304.4 1.3 copy-start.20
  304.4 2.0 copy-start.33
  304.4 2.0 copy-start.38
  310.7 1.0 copy-start.21
  310.7 1.1 copy-start.23
  310.7 1.2 copy-start.25
  310.7 1.2 copy-start.34
  311.9 4.1 copy-start.46
  312.0 4.1 copy-start.39
  312.0 4.5 copy-start.9
  312.0 4.5 copy-start.29
  312.0 4.5 copy-start.31
  312.0 4.5 copy-start.36
  312.0 4.5 copy-start.41
  312.0 4.5 copy-start.44
  312.0 4.5 copy-start.48
  312.0 54.7 %copy-start.5 = (f32[256,768]{1,0:T(8,128)S(1)}, f32[256,768]{1,0:T(8,128)}, u32[]{:S(2)}) copy-start(f32[256,768]{1,0:T(8,128)} %copy-done.4) | copy-start | bytes 2359300
  312.0 54.7 %copy-start.7 = (bf16[256,768]{1,0:T(8,128)(2,1)S(1)}, bf16[256,768]{1,0:T(8,128)(2,1)}, u32[]{:S(2)}) copy-start(bf16[256,768]{1,0:T(8,128)(2,1)} %param.13) | copy-start | bytes 1179652
  368.5 159.3 %copy-start.15 = (f32[768,768]{1,0:T(8,128)S(1)}, f32[768,768]{1,0:T(8,128)}, u32[]{:S(2)}) copy-start(f32[768,768]{1,0:T(8,128)} %get-tuple-element.70) | copy-start | bytes 7077892
  (6 other events, 5.1 us)
Sparse Core Ops, SparseCore 0:
  11.5 62.8 all-gather.3
  77.8 52.8 all-gather.5
  295.7 103.6 reduce-scatter.5
  406.5 118.0 reduce-scatter.3

commit v2 on v1

--- a/solution.py
+++ b/solution.py
@@ -6,9 +6,6 @@
 from jax.experimental import pallas as pl
 from jax.experimental.pallas import tpu as pltpu
 from jax.sharding import PartitionSpec as P
-
-HEADS = 12
-
 
 epsilon = 1e-05
 balance_weight = 3.0
@@ -336,219 +333,710 @@
     )(out_h, out_g, w_in, w_dn)
 
 
-def norm_apply(values, gain, shift):
+HEAD_DIM = 64
+LANES = 128
+
+
+def norm_stats(values):
     average = jnp.mean(values, axis=-1, keepdims=True)
     centred = values - average
     spread = jnp.mean(centred * centred, axis=-1, keepdims=True)
-    return centred * lax.rsqrt(spread + epsilon) * gain + shift
-
-
-def contract_rows(left, right):
-    return lax.dot_general(
-        left, right, (((0,), (0,)), ((), ())), preferred_element_type=jnp.float32
+    return centred, lax.rsqrt(spread + epsilon)
+
+
+def norm_back(grad, values, gain):
+    centred, rate = norm_stats(values)
+    unit = centred * rate
+    scaled = grad * gain
+    toward = rate * (
+        scaled
+        - jnp.mean(scaled, axis=-1, keepdims=True)
+        - unit * jnp.mean(scaled * unit, axis=-1, keepdims=True)
     )
-
-
-def contract_cols(left, right):
-    return lax.dot_general(
-        left, right, (((1,), (1,)), ((), ())), preferred_element_type=jnp.float32
+    gain_grad = jnp.sum(grad * unit, axis=0, keepdims=True)
+    shift_grad = jnp.sum(grad, axis=0, keepdims=True)
+    return toward, gain_grad, shift_grad
+
+
+def iota(shape, axis):
+    return lax.broadcasted_iota(jnp.int32, shape, axis)
+
+
+def slot_places(assign, capacity):
+    T = assign.shape[1]
+    down, across = iota((T, T), 0), iota((T, T), 1)
+    column = jnp.sum(jnp.where(down == across, assign, 0.0), axis=1, keepdims=True)
+    same = column == assign
+    rank_column = jnp.sum(jnp.where(same & (across < down), 1.0, 0.0), axis=1, keepdims=True)
+    rank_row = jnp.sum(jnp.where(same & (down < across), 1.0, 0.0), axis=0, keepdims=True)
+    place_column = (column * capacity + rank_column).astype(jnp.int32)
+    place_row = (assign * capacity + rank_row).astype(jnp.int32)
+    return column.astype(jnp.int32), place_column, place_row
+
+
+def head_probs(q_one, k_pair, allowed):
+    scores = dot_cols(q_one, k_pair) * (HEAD_DIM ** -0.5)
+    scores = jnp.where(allowed, scores, masked_score)
+    powers = jnp.exp(scores - jnp.max(scores, axis=-1, keepdims=True))
+    return powers * (1.0 / jnp.sum(powers, axis=-1, keepdims=True))
+
+
+def head_masks(T):
+    first = iota((T, LANES), 1) < HEAD_DIM
+    low_lanes = jnp.where(first, 1.0, 0.0).astype(half)
+    high_lanes = jnp.where(first, 0.0, 1.0).astype(half)
+    return first, (low_lanes, high_lanes)
+
+
+def forward_body(E, tokens, cotangent, assign, wts, small, hid_a, qkv, att, resid, hid_b, probs, out_h, out_g):
+    T, D = tokens.shape
+    cap = out_h.shape[1]
+    small_t = small[...].astype(single).T
+    inputs = tokens[...].astype(single)
+    centred, rate = norm_stats(inputs)
+    hid_a[...] = (centred * rate * small_t[E : E + 1] + small_t[E + 1 : E + 2]).astype(half)
+    for m in range(3):
+        qkv[m] = dot(hid_a[...], wts[m]).astype(half)
+    allowed = iota((T, T), 1) <= iota((T, T), 0)
+    first, masks = head_masks(T)
+
+    @pl.loop(0, D // LANES)
+    def _(p):
+        at = pl.ds(pl.multiple_of(p * LANES, LANES), LANES)
+        q_pair, k_pair, v_pair = qkv[0, :, at], qkv[1, :, at], qkv[2, :, at]
+        mixed = [
+            dot(head_probs(q_pair * mask, k_pair, allowed).astype(half), v_pair) for mask in masks
+        ]
+        att[:, at] = jnp.where(first, mixed[0], mixed[1]).astype(half)
+
+    resid[...] = inputs + dot(att[...], wts[3])
+    centred, rate = norm_stats(resid[...])
+    hid_b[...] = (centred * rate * small_t[E + 2 : E + 3] + small_t[E + 3 : E + 4]).astype(half)
+    lane = iota((T, LANES), 1)
+    logits = jnp.where(lane < E, dot(hid_b[...], small[...]), -1e30)
+    powers = jnp.exp(logits - jnp.max(logits, axis=-1, keepdims=True))
+    chance = powers * (1.0 / jnp.sum(powers, axis=-1, keepdims=True))
+    probs[...] = chance
+    column, _, place_row = slot_places(assign[...], cap)
+    gate = jnp.sum(jnp.where(lane == column, chance, 0.0), axis=1, keepdims=True)
+    pick = jnp.where(iota((E * cap, T), 0) == place_row, 1.0, 0.0).astype(half)
+    out_h[...] = dot(pick, hid_b[...]).astype(half).reshape(E, cap, D)
+    grad_expert = (gate * cotangent[...].astype(single)).astype(half)
+    out_g[...] = dot(pick, grad_expert).astype(half).reshape(E, cap, D)
+
+
+def backward_body(
+    E, total_tokens, tokens, cotangent, assign, small, counts, proj_w, resid, hid_b, probs, qkv, ret_o, ret_g,
+    layer_out, grad_res, gall, gatt, router_grad,
+):
+    T, D = tokens.shape
+    cap = ret_o.shape[1]
+    small_t = small[...].astype(single).T
+    cot = cotangent[...].astype(single)
+    column, place_column, _ = slot_places(assign[...], cap)
+    lane = iota((T, LANES), 1)
+    chance = probs[...]
+    mine = lane == column
+    gate = jnp.sum(jnp.where(mine, chance, 0.0), axis=1, keepdims=True)
+    pick = jnp.where(iota((T, E * cap), 1) == place_column, 1.0, 0.0).astype(half)
+    expert_tok = dot(pick, ret_o[...].reshape(E * cap, D))
+    layer_out[...] = (resid[...] + gate * expert_tok).astype(half)
+    grad_gate = jnp.sum(cot * expert_tok, axis=1, keepdims=True)
+    scale = counts * (balance_weight * E / total_tokens)
+    grad_probs = jnp.where(mine, grad_gate, 0.0) + scale
+    grad_logits = chance * (grad_probs - jnp.sum(chance * grad_probs, axis=1, keepdims=True))
+    grad_logits = jnp.where(lane < E, grad_logits, 0.0).astype(half)
+    router_grad[...] = dot_rows(hid_b[...], grad_logits)
+    grad_hidden_b = dot(pick, ret_g[...].reshape(E * cap, D)) + dot_cols(grad_logits, small[...])
+    toward, mid_gain, mid_shift = norm_back(grad_hidden_b, resid[...], small_t[E + 2 : E + 3])
+    grad_res[...] = cot + toward
+    gall[3] = grad_res[...].astype(half)
+    gatt[...] = dot_cols(gall[3], proj_w).astype(half)
+    allowed = iota((T, T), 1) <= iota((T, T), 0)
+    first, masks = head_masks(T)
+
+    @pl.loop(0, D // LANES)
+    def _(p):
+        at = pl.ds(pl.multiple_of(p * LANES, LANES), LANES)
+        q_pair, k_pair, v_pair, g_pair = qkv[0, :, at], qkv[1, :, at], qkv[2, :, at], gatt[:, at]
+        found = []
+        for mask in masks:
+            weights = head_probs(q_pair * mask, k_pair, allowed)
+            grad_w = dot_cols(g_pair * mask, v_pair)
+            grad_s = weights * (grad_w - jnp.sum(weights * grad_w, axis=-1, keepdims=True))
+            grad_s = grad_s.astype(half)
+            found.append(
+                (
+                    dot(grad_s, k_pair) * (HEAD_DIM ** -0.5),
+                    dot_rows(grad_s, q_pair) * (HEAD_DIM ** -0.5),
+                    dot_rows(weights.astype(half), g_pair),
+                )
+            )
+        for m in range(3):
+            gall[m, :, at] = jnp.where(first, found[0][m], found[1][m]).astype(half)
+
+    return mid_gain, mid_shift
+
+
+def input_body(E, tokens, small, wts, gall, grad_res, input_grad):
+    small_t = small[...].astype(single).T
+    grad_hidden_a = dot_cols(gall[0], wts[0]) + dot_cols(gall[1], wts[1]) + dot_cols(gall[2], wts[2])
+    toward, pre_gain, pre_shift = norm_back(
+        grad_hidden_a, tokens[...].astype(single), small_t[E : E + 1]
     )
-
-
-def build_slots(assignment, experts, capacity):
-    token_count = assignment.shape[0]
-    labels = jnp.arange(experts, dtype=jnp.int32)
-    onehot = (assignment[:, None] == labels[None, :]).astype(jnp.int32)
-    ranking = jnp.cumsum(onehot, axis=0) - 1
-    slot_index = jnp.sum(ranking * onehot, axis=1)
-    position = assignment * capacity + slot_index
-    slot_owner = jnp.full((experts * capacity,), token_count, jnp.int32)
-    slot_owner = slot_owner.at[position].set(jnp.arange(token_count, dtype=jnp.int32))
-    return (position, slot_owner, onehot)
-
-
-def take_rows(values, slot_owner):
-    padded = jnp.concatenate([values, jnp.zeros((1, values.shape[1]), values.dtype)], axis=0)
-    return padded[slot_owner]
+    input_grad[...] = (grad_res[...] + toward).astype(half)
+    return pre_gain, pre_shift
+
+
+def small_grads(E, router, rows, chance_sum, block, D):
+    lane = iota((D, LANES), 1)
+    eight = iota((LANES, D), 0)
+    stacked = jnp.zeros((LANES, D), single)
+    for i, row in enumerate(rows):
+        stacked = jnp.where(eight == E + i, row, stacked)
+    packed = jnp.where(lane < E, router, stacked.T)
+    if block:
+        place = lax.rem(iota((D, LANES), 0), block)
+        copy = jnp.sum(jnp.where(place == lane, chance_sum, 0.0), axis=1, keepdims=True)
+        packed = jnp.where(lane == E + 4, copy, packed)
+    return packed
+
+
+class Place:
+    def __init__(self, E):
+        e, h = lax.axis_index("expert"), lax.axis_index("hid")
+        self.Z = E // 2
+        self.z, self.y = lax.div(e, 2), lax.rem(e, 2)
+        self.x, self.c = lax.div(h, 2), lax.rem(h, 2)
+
+    def device(self, z, y, x, c):
+        return (z * 2 + y, x * 2 + c)
+
+    def z_at(self, d):
+        return lax.rem(self.z + d, self.Z)
+
+    def z_peer(self, d):
+        return self.device(self.z_at(d), self.y, self.x, self.c)
+
+    def y_peer(self):
+        return self.device(self.z, 1 - self.y, self.x, self.c)
+
+    def x_peer(self):
+        return self.device(self.z, self.y, 1 - self.x, self.c)
+
+    def core_peer(self):
+        return self.device(self.z, self.y, self.x, 1 - self.c)
+
+    def z_steps(self):
+        return sorted(range(1, self.Z), key=lambda d: min(d, self.Z - d))
+
+    def greet(self):
+        barrier = pltpu.get_barrier_semaphore()
+        peers = [self.z_peer(d) for d in range(1, self.Z)]
+        peers += [self.y_peer(), self.x_peer(), self.core_peer()]
+        for peer in peers:
+            pl.semaphore_signal(barrier, inc=1, device_id=peer, device_id_type=MESH)
+        pl.semaphore_wait(barrier, len(peers))
+
+
+def chip_index(z, y, x):
+    return (z * 2 + y) * 2 + x
+
+
+class Sends:
+    def __init__(self, sems):
+        self.sems, self.started = sems, []
+
+    def start(self, src, dst, recv_sem, device):
+        copy = remote(src, dst, self.sems.at[len(self.started)], recv_sem, device)
+        copy.start()
+        self.started.append(copy)
+
+    def finish(self):
+        for copy in self.started:
+            copy.wait_send()
+
+
+def arrive(dst, send_sem, recv_sem, device):
+    remote(dst, dst, send_sem, recv_sem, device).wait_recv()
+
+
+def gather_weights(at, sends, shard, small_shard, other, other_small, wts, small, recv, recv_own):
+    Z, z, y, x, c = at.Z, at.z, at.y, at.x, at.c
+    rows, D = shard.shape[1], shard.shape[2]
+    core = at.core_peer()
+    mine, theirs = 2 * c, 2 * (1 - c)
+    for o in range(2):
+        sends.start(shard.at[theirs + o], other.at[o], recv_own.at[o], core)
+    sends.start(small_shard, other_small, recv_own.at[2], core)
+    span = 2 * rows
+
+    def rows_of(chip):
+        return pl.ds(pl.multiple_of(chip * span, span), span)
+
+    def block(o, chip):
+        return small.at[rows_of(chip), :] if o == 2 else wts.at[mine + o, rows_of(chip), :]
+
+    def send(o, chip, device):
+        sends.start(block(o, chip), block(o, chip), recv.at[o, chip], device)
+
+    def share(o, chip):
+        if o < 2:
+            sends.start(block(o, chip), block(o, chip), recv.at[3 + o, chip], core)
+
+    def wait(o, chip):
+        arrive(block(o, chip), sends.sems.at[0], recv.at[o, chip], core)
+
+    own = chip_index(z, y, x)
+    for o, there in ((2, other_small), (0, other.at[0]), (1, other.at[1])):
+        arrive(there, sends.sems.at[0], recv_own.at[o], core)
+        here = small_shard[...] if o == 2 else shard[mine + o]
+        got = there[...]
+        low = jnp.where(c == 0, here, got)
+        high = jnp.where(c == 0, got, here)
+        both = jnp.concatenate([low, high], axis=0).astype(half)
+        if o == 2:
+            small[rows_of(own), :] = both
+        else:
+            wts[mine + o, rows_of(own), :] = both
+        if o == 1:
+            send(o, own, at.x_peer())
+        for d in at.z_steps():
+            send(o, own, at.z_peer(d))
+        send(o, own, at.y_peer())
+        if o != 1:
+            send(o, own, at.x_peer())
+    share(0, own)
+    share(1, own)
+    wait(1, chip_index(z, y, 1 - x))
+    for d in at.z_steps():
+        send(1, chip_index(z, y, 1 - x), at.z_peer(d))
+    send(1, chip_index(z, y, 1 - x), at.y_peer())
+    share(1, chip_index(z, y, 1 - x))
+    for d in at.z_steps():
+        for o in (2, 0):
+            chip = chip_index(at.z_at(d), y, x)
+            wait(o, chip)
+            send(o, chip, at.y_peer())
+            send(o, chip, at.x_peer())
+            share(o, chip)
+        for there in (x, 1 - x):
+            chip = chip_index(at.z_at(d), y, there)
+            wait(1, chip)
+            send(1, chip, at.y_peer())
+            share(1, chip)
+    for d in [0] + at.z_steps():
+        for o in (2, 0):
+            chip = chip_index(at.z_at(d), 1 - y, x)
+            wait(o, chip)
+            send(o, chip, at.x_peer())
+            share(o, chip)
+        for there in (x, 1 - x):
+            chip = chip_index(at.z_at(d), 1 - y, there)
+            wait(1, chip)
+            share(1, chip)
+    for d in [0] + at.z_steps():
+        for there in (y, 1 - y):
+            for o in (2, 0):
+                chip = chip_index(at.z_at(d), there, 1 - x)
+                wait(o, chip)
+                share(o, chip)
+
+    def wait_shared():
+        for o in range(2):
+            for chip in range(4 * Z):
+                theirs_block = wts.at[theirs + o, rows_of(chip), :]
+                arrive(theirs_block, sends.sems.at[0], recv.at[3 + o, chip], core)
+
+    return wait_shared
+
+
+class SumScatter:
+    def __init__(self, at, sends, acc, give, got, sent, came, final, other, recv):
+        self.at, self.sends = at, sends
+        self.acc, self.give, self.got, self.sent, self.came = acc, give, got, sent, came
+        self.final, self.other, self.recv = final, other, recv
+        self.span = final.shape[1]
+
+    def rows_of(self, chip):
+        return pl.ds(pl.multiple_of(chip * self.span, self.span), self.span)
+
+    def swap(self, o):
+        self.sends.start(self.give.at[o], self.got.at[o], self.recv.at[o, 0], self.at.core_peer())
+
+    def wait_swap(self, o):
+        arrive(self.got.at[o], self.sends.sems.at[0], self.recv.at[o, 0], self.at.core_peer())
+
+    def send(self, o, slot, value, device):
+        self.sent[o, slot] = value.astype(half)
+        self.sends.start(self.sent.at[o, slot], self.came.at[o, slot], self.recv.at[o, 1 + slot], device)
+
+    def take(self, o, slot):
+        arrive(
+            self.came.at[o, slot], self.sends.sems.at[0], self.recv.at[o, 1 + slot], self.at.core_peer()
+        )
+        return self.came[o, slot].astype(single)
+
+    def base(self, o, chip):
+        rows = self.rows_of(chip)
+        return self.acc[o, rows, :] + self.got[o, rows, :].astype(single)
+
+    def one(self, o):
+        at = self.at
+        for dz in range(at.Z):
+            for b in range(2):
+                z = at.z_at(dz)
+                if o == 0:
+                    chip, device = chip_index(z, b, 1 - at.x), at.x_peer()
+                else:
+                    chip, device = chip_index(z, 1 - at.y, b), at.y_peer()
+                self.send(o, dz * 2 + b, self.base(o, chip), device)
+
+    def two(self, o):
+        at = self.at
+        first = 2 * at.Z
+        if o == 0:
+            for dz in range(at.Z):
+                for flip in (1, 0):
+                    y = 1 - at.y if flip else at.y
+                    chip = chip_index(at.z_at(dz), y, at.x)
+                    value = self.base(o, chip)
+                    value = value + self.pick(o, dz * 2, y)
+                    if flip:
+                        self.send(o, first + dz, value, at.y_peer())
+                    else:
+                        self.acc[o, self.rows_of(chip), :] = value
+        else:
+            for dz in at.z_steps() + [0]:
+                for b in range(2):
+                    chip = chip_index(at.z_at(dz), at.y, b)
+                    value = self.base(o, chip) + self.take(o, dz * 2 + b)
+                    if dz:
+                        self.send(o, first + dz * 2 + b, value, at.z_peer(dz))
+                    else:
+                        self.acc[o, self.rows_of(chip), :] = value
+
+    def pick(self, o, slot, index):
+        place = slot + index
+        arrive(
+            self.came.at[o, place], self.sends.sems.at[0], self.recv.at[o, 1 + place], self.at.core_peer()
+        )
+        return self.came[o, place].astype(single)
+
+    def three(self, o):
+        at = self.at
+        first = 2 * at.Z
+        if o == 0:
+            second = first + at.Z
+            for dz in at.z_steps() + [0]:
+                rows = self.rows_of(chip_index(at.z_at(dz), at.y, at.x))
+                value = self.acc[o, rows, :] + self.take(o, first + dz)
+                if dz:
+                    self.send(o, second + dz, value, at.z_peer(dz))
+                else:
+                    self.final[o] = value
+        else:
+            second = first + 2 * at.Z
+            for flip in (1, 0):
+                x = 1 - at.x if flip else at.x
+                value = self.acc[o, self.rows_of(chip_index(at.z, at.y, x)), :]
+                for dz in range(1, at.Z):
+                    value = value + self.pick(o, first + dz * 2, x)
+                if flip:
+                    self.send(o, second, value, at.x_peer())
+                else:
+                    self.final[o] = value
+
+    def four(self, o):
+        at = self.at
+        if o == 0:
+            second = 2 * at.Z + at.Z
+            for dz in range(1, at.Z):
+                self.final[o] += self.take(o, second + dz)
+        else:
+            self.final[o] += self.take(o, 2 * at.Z + 2 * at.Z)
+        rows = self.span // 2
+        last = self.recv.shape[1] - 1
+        there = self.final.at[o, pl.ds(pl.multiple_of((1 - at.c) * rows, rows), rows), :]
+        self.sends.start(there, self.other.at[o], self.recv.at[o, last], at.core_peer())
+
+    def end(self, o):
+        last = self.recv.shape[1] - 1
+        arrive(self.other.at[o], self.sends.sems.at[0], self.recv.at[o, last], self.at.core_peer())
+
+
+def start_kernel(E, fused, *refs):
+    if fused:
+        (tokens, cotangent, assign, qkv_shard, proj_shard, small_in,
+         out_h, out_g, wts, small, counts, hid_a, qkv, att, resid, hid_b, probs,
+         shard, small_shard, other, other_small, send, recv, recv_own) = refs
+        rows, D = proj_shard.shape
+        at = Place(E)
+        at.greet()
+        for m in range(3):
+            shard[m] = qkv_shard[:, m * D : (m + 1) * D]
+        shard[3] = proj_shard[...]
+        numbers = iota((rows, tokens.shape[0]), 0).astype(single)
+        count = jnp.sum(jnp.where(assign[...] == numbers, 1.0, 0.0), axis=1, keepdims=True)
+        small_shard[...] = jnp.where(iota((rows, LANES), 1) == E + 4, count, small_in[...])
+        sends = Sends(send)
+        wait_shared = gather_weights(
+            at, sends, shard, small_shard, other, other_small, wts, small, recv, recv_own
+        )
+        wait_shared()
+        place = lax.rem(iota((D, LANES), 0), rows)
+        column = small[:, E + 4 : E + 5].astype(single)
+        total = jnp.sum(jnp.where(place == iota((D, LANES), 1), column, 0.0), axis=0, keepdims=True)
+        counts[...] = jnp.broadcast_to(total, counts.shape)
+    else:
+        (tokens, cotangent, assign, wts, small, out_h, out_g, hid_a, qkv, att, resid, hid_b, probs) = refs
+    forward_body(
+        E, tokens, cotangent, assign, wts, small, hid_a, qkv, att, resid, hid_b, probs, out_h, out_g
+    )
+    if fused:
+        sends.finish()
+
+
+def end_kernel(E, total_tokens, fused, *refs):
+    (tokens, cotangent, assign, wts, small, counts, hid_a, qkv, att, resid, hid_b, probs, ret_o, ret_g,
+     layer_out, input_grad) = refs[:16]
+    T, D = tokens.shape
+    if fused:
+        (qkv_grad, proj_grad, small_out, gall, gatt, grad_res, router_grad,
+         acc, give, got, sent, came, final, other,
+         pack, pack_other, pack_sent, pack_came, send, recv, pack_recv) = refs[16:]
+        at = Place(E)
+        at.greet()
+    else:
+        weight_grads, small_out, gall, gatt, grad_res, router_grad = refs[16:]
+    mid_gain, mid_shift = backward_body(
+        E, total_tokens, tokens, cotangent, assign, small, counts[0:1], wts[3], resid, hid_b, probs, qkv,
+        ret_o, ret_g, layer_out, grad_res, gall, gatt, router_grad,
+    )
+    tile = 256 if D % 256 == 0 else LANES
+
+    def fill(write, m):
+        @pl.loop(0, D // tile)
+        def _(i):
+            cols = pl.ds(pl.multiple_of(i * tile, tile), tile)
+            if isinstance(m, int):
+                left = att[:, cols] if m == 3 else hid_a[:, cols]
+            else:
+                left = jnp.where(m == 3, att[:, cols].astype(single), hid_a[:, cols].astype(single))
+                left = left.astype(half)
+            write(cols, dot_rows(left, gall[m]))
+
+    chance_sum = jnp.sum(probs[...], axis=0, keepdims=True)
+    if not fused:
+        for m in range(4):
+            def write(cols, value):
+                weight_grads[m, cols, :] = value
+            fill(write, m)
+        pre_gain, pre_shift = input_body(E, tokens, small, wts, gall, grad_res, input_grad)
+        small_out[...] = small_grads(
+            E, router_grad[...], (pre_gain, pre_shift, mid_gain, mid_shift), chance_sum, 0, D
+        )
+        return
+
+    rows = proj_grad.shape[0]
+    sends = Sends(send)
+    sums = SumScatter(at, sends, acc, give, got, sent, came, final, other, recv)
+    mine, theirs = 2 * at.c, 2 * (1 - at.c)
+    for o in (1, 0):
+        def write(cols, value):
+            give[o, cols, :] = value.astype(half)
+        fill(write, theirs + o)
+        sums.swap(o)
+    for o in (1, 0):
+        def write(cols, value):
+            acc[o, cols, :] = value
+        fill(write, mine + o)
+    for o in (1, 0):
+        sums.wait_swap(o)
+        sums.one(o)
+    pre_gain, pre_shift = input_body(E, tokens, small, wts, gall, grad_res, input_grad)
+    pack[...] = small_grads(
+        E, router_grad[...], (pre_gain, pre_shift, mid_gain, mid_shift), chance_sum, rows, D
+    )
+    sends.start(pack, pack_other, pack_recv.at[0], at.core_peer())
+    sums.two(1)
+    sums.two(0)
+    arrive(pack_other, send.at[0], pack_recv.at[0], at.core_peer())
+    pack_other[...] += pack[...]
+
+    def pack_rows(z, y, x):
+        first = chip_index(z, y, x) * 2 * rows + at.c * rows
+        return pl.ds(pl.multiple_of(first, rows), rows)
+
+    def pack_send(slot, value, device):
+        pack_sent[slot] = value
+        sends.start(pack_sent.at[slot], pack_came.at[slot], pack_recv.at[1 + slot], device)
+
+    def pack_take(slot):
+        arrive(pack_came.at[slot], send.at[0], pack_recv.at[1 + slot], at.core_peer())
+        return pack_came[slot]
+
+    Z = at.Z
+    for dz in range(Z):
+        for y in range(2):
+            pack_send(dz * 2 + y, pack_other[pack_rows(at.z_at(dz), y, 1 - at.x), :], at.x_peer())
+    sums.three(1)
+    sums.three(0)
+    for dz in range(Z):
+        for flip in (1, 0):
+            y = 1 - at.y if flip else at.y
+            here = pack_rows(at.z_at(dz), y, at.x)
+            value = pack_other[here, :] + pack_take(dz * 2 + y)
+            if flip:
+                pack_send(2 * Z + dz, value, at.y_peer())
+            else:
+                pack_other[here, :] = value
+    sums.four(1)
+    sums.four(0)
+    for dz in at.z_steps() + [0]:
+        value = pack_other[pack_rows(at.z_at(dz), at.y, at.x), :] + pack_take(2 * Z + dz)
+        if dz:
+            pack_send(3 * Z + dz, value, at.z_peer(dz))
+        else:
+            total = value
+    for dz in range(1, Z):
+        total = total + pack_take(3 * Z + dz)
+    lane = iota((rows, LANES), 1)
+    scale = counts[0:1] * (balance_weight * E / total_tokens)
+    chance = jnp.sum(jnp.where(lane == E + 4, total, 0.0), axis=1, keepdims=True)
+    chosen = jnp.where((lane == iota((rows, LANES), 0)) & (lane < E), chance * scale, 0.0)
+    loss = jnp.sum(jnp.sum(chosen, axis=1, keepdims=True), axis=0, keepdims=True) / total_tokens
+    small_out[...] = jnp.where(lane == E + 5, loss, total)
+    sums.end(1)
+    sums.end(0)
+    half_rows = pl.ds(pl.multiple_of(at.c * rows, rows), rows)
+
+    def put(o_mine, o_other):
+        for m, value in o_mine + o_other:
+            if m == 3:
+                proj_grad[...] = value
+            else:
+                qkv_grad[:, m * D : (m + 1) * D] = value
+
+    @pl.when(at.c == 0)
+    def _():
+        put([(o, final[o, half_rows, :]) for o in range(2)], [(2 + o, other[o]) for o in range(2)])
+
+    @pl.when(at.c == 1)
+    def _():
+        put([(2 + o, final[o, half_rows, :]) for o in range(2)], [(o, other[o]) for o in range(2)])
+
+    sends.finish()
+
+
+DMA = pltpu.SemaphoreType.DMA
+VMEM_SPEC = pl.BlockSpec(memory_space=pltpu.VMEM)
+
+
+def call(kernel, outs, scratch, collective, name, *args):
+    if collective is None:
+        params = pltpu.CompilerParams(vmem_limit_bytes=60 * 1024 * 1024)
+    else:
+        params = pltpu.CompilerParams(
+            collective_id=collective, has_side_effects=True, vmem_limit_bytes=60 * 1024 * 1024
+        )
+    return pl.pallas_call(
+        kernel,
+        out_shape=tuple(jax.ShapeDtypeStruct(shape, kind) for shape, kind in outs),
+        in_specs=[VMEM_SPEC] * len(args),
+        out_specs=(VMEM_SPEC,) * len(outs),
+        scratch_shapes=scratch,
+        compiler_params=params,
+        name=name,
+    )(*args)
 
 
 def on_device(
-    tokens_in,
-    out_cotangent,
-    qkv_weight,
-    proj_weight,
-    router_weight,
-    pre_gain,
-    pre_shift,
-    mid_gain,
-    mid_shift,
-    expert_in,
-    expert_down,
-    assignment,
+    tokens_in, out_cotangent, qkv_weight, proj_weight, router_weight, pre_gain, pre_shift, mid_gain, mid_shift,
+    expert_in, expert_down, assignment,
 ):
-    token_count, model_width = tokens_in.shape
-    experts = lax.axis_size("expert")
-    capacity = 2 * token_count // experts
-    total_tokens = token_count * experts * lax.axis_size("hid")
-    head_dim = model_width // HEADS
-    score_scale = head_dim ** (-0.5)
-    half = jnp.bfloat16
-    single = jnp.float32
-    gathered = (
-        lax.all_gather(qkv_weight.astype(half), ("expert", "hid"), axis=0, tiled=True),
-        lax.all_gather(proj_weight.astype(half), ("expert", "hid"), axis=0, tiled=True),
-        lax.all_gather(router_weight.astype(half), ("expert", "hid"), axis=0, tiled=True),
-        lax.all_gather(pre_gain.astype(half), ("expert", "hid"), axis=0, tiled=True),
-        lax.all_gather(pre_shift.astype(half), ("expert", "hid"), axis=0, tiled=True),
-        lax.all_gather(mid_gain.astype(half), ("expert", "hid"), axis=0, tiled=True),
-        lax.all_gather(mid_shift.astype(half), ("expert", "hid"), axis=0, tiled=True),
+    T, D = tokens_in.shape
+    E, H = lax.axis_size("expert"), lax.axis_size("hid")
+    X = H // 2
+    Z = E // 2
+    cap = 2 * T // E
+    total_tokens = T * E * H
+    rows = proj_weight.shape[0]
+    both = ("expert", "hid")
+    fused = X == 2 and E % 2 == 0 and rows % 8 == 0 and rows >= E
+    assign = assignment.astype(single).reshape(1, T)
+    columns = [v[:, None] for v in (pre_gain, pre_shift, mid_gain, mid_shift)]
+    small_in = jnp.concatenate([router_weight] + columns, axis=1)
+    small_in = jnp.pad(small_in, ((0, 0), (0, LANES - small_in.shape[1])))
+    kept = [
+        ((E, cap, D), half), ((E, cap, D), half),
+    ]
+    saved = [
+        ((T, D), half), ((3, T, D), half), ((T, D), half), ((T, D), single), ((T, D), half), ((T, LANES), single),
+    ]
+    if fused:
+        out_h, out_g, wts, small, counts, *rest = call(
+            functools.partial(start_kernel, E, True),
+            kept + [((4, D, D), half), ((D, LANES), half), ((8, LANES), single)] + saved,
+            [
+                pltpu.VMEM((4, rows, D), single), pltpu.VMEM((rows, LANES), single),
+                pltpu.VMEM((2, rows, D), single), pltpu.VMEM((rows, LANES), single),
+                DMA((20 * Z + 8,)), DMA((5, 4 * Z)), DMA((3,)),
+            ],
+            2, "start", tokens_in, out_cotangent, assign, qkv_weight, proj_weight, small_in,
+        )
+    else:
+        shard = jnp.concatenate([qkv_weight, proj_weight], axis=1).astype(half)
+        wts = lax.all_gather(shard, both, axis=0, tiled=True).reshape(D, 4, D).transpose(1, 0, 2)
+        small = lax.all_gather(small_in.astype(half), both, axis=0, tiled=True)
+        onehot = assignment[:, None] == jnp.arange(LANES, dtype=jnp.int32)[None, :]
+        counts = lax.psum(jnp.sum(onehot.astype(single), axis=0), both)
+        counts = jnp.broadcast_to(counts[None, :], (8, LANES))
+        out_h, out_g, *rest = call(
+            functools.partial(start_kernel, E, False), kept + saved, [], None, "start",
+            tokens_in, out_cotangent, assign, wts, small,
+        )
+    hid_a, qkv, att, resid, hid_b, probs = rest
+    ret_o, ret_g, in_grad, down_grad = expert_call(out_h, out_g, expert_in[0], expert_down[0], X)
+    given = (
+        tokens_in, out_cotangent, assign, wts, small, counts, hid_a, qkv, att, resid, hid_b, probs, ret_o, ret_g,
     )
-    w_qkv, w_proj, w_router, gain_a, shift_a, gain_b, shift_b = gathered
-    inputs = tokens_in.astype(single)
-    normed_a, pre_back = jax.vjp(norm_apply, inputs, gain_a.astype(single), shift_a.astype(single))
-    hidden_a = normed_a.astype(half)
-    qkv_rows = jnp.dot(hidden_a, w_qkv, preferred_element_type=single).astype(half)
-    queries = qkv_rows[:, :model_width].reshape(token_count, HEADS, head_dim)
-    key_rows = qkv_rows[:, model_width : 2 * model_width].reshape(token_count, HEADS, head_dim)
-    value_rows = qkv_rows[:, 2 * model_width :].reshape(token_count, HEADS, head_dim)
-    block_rows = min(token_count, 512)
-    block_count = token_count // block_rows
-    key_index = jnp.arange(token_count, dtype=jnp.int32)
-
-    def block_scores(first_row, query_block):
-        raw_scores = (
-            jnp.einsum("qhd,khd->hqk", query_block, key_rows, preferred_element_type=single)
-            * score_scale
+    outs = [((T, D), half), ((T, D), half)]
+    working = [
+        pltpu.VMEM((4, T, D), half), pltpu.VMEM((T, D), half), pltpu.VMEM((T, D), single),
+        pltpu.VMEM((D, LANES), single),
+    ]
+    if fused:
+        slots = 4 * Z + 1
+        layer_out, input_grad, qkv_grad, proj_grad, small_out = call(
+            functools.partial(end_kernel, E, total_tokens, True),
+            outs + [((rows, 3 * D), single), ((rows, D), single), ((rows, LANES), single)],
+            working + [
+                pltpu.VMEM((2, D, D), single), pltpu.VMEM((2, D, D), half), pltpu.VMEM((2, D, D), half),
+                pltpu.VMEM((2, slots, 2 * rows, D), half), pltpu.VMEM((2, slots, 2 * rows, D), half),
+                pltpu.VMEM((2, 2 * rows, D), single), pltpu.VMEM((2, rows, D), single),
+                pltpu.VMEM((D, LANES), single), pltpu.VMEM((D, LANES), single),
+                pltpu.VMEM((4 * Z, rows, LANES), single), pltpu.VMEM((4 * Z, rows, LANES), single),
+                DMA((12 * Z + 8,)), DMA((2, slots + 2)), DMA((4 * Z + 1,)),
+            ],
+            3, "end", *given,
         )
-        query_index = first_row + jnp.arange(block_rows, dtype=jnp.int32)
-        allowed = key_index[None, :] <= query_index[:, None]
-        return jnp.where(allowed[None], raw_scores, masked_score)
-
-    def attend(block_index):
-        first_row = block_index * block_rows
-        scores = block_scores(first_row, queries)
-        row_max = jnp.max(scores, axis=-1, keepdims=True)
-        logsum = row_max + jnp.log(jnp.sum(jnp.exp(scores - row_max), axis=-1, keepdims=True))
-        weights = jnp.exp(scores - logsum).astype(half)
-        mixed_rows = jnp.einsum("hqk,khd->qhd", weights, value_rows, preferred_element_type=single)
-        return (mixed_rows.astype(half), logsum)
-
-    mixed_blocks, logsum_blocks = lax.map(attend, jnp.arange(block_count, dtype=jnp.int32))
-    attended = mixed_blocks.reshape(token_count, model_width)
-    residual = inputs + jnp.dot(attended, w_proj, preferred_element_type=single)
-    normed_b, mid_back = jax.vjp(
-        norm_apply, residual, gain_b.astype(single), shift_b.astype(single)
-    )
-    hidden_b = normed_b.astype(half)
-    logits = jnp.dot(hidden_b, w_router, preferred_element_type=single)
-    router_probs = jax.nn.softmax(logits, axis=-1)
-    position, slot_owner, onehot = build_slots(assignment, experts, capacity)
-    onehot_f = onehot.astype(single)
-    gate_value = jnp.sum(router_probs * onehot_f, axis=1)
-    counts, prob_total = lax.psum(
-        (jnp.sum(onehot_f, axis=0), jnp.sum(router_probs, axis=0)), ("expert", "hid")
-    )
-    expert_scale = balance_weight * experts * counts / total_tokens
-    balance_loss = jnp.sum(expert_scale * prob_total) / total_tokens
-    outgoing = take_rows(hidden_b, slot_owner).reshape(experts, capacity, model_width)
-    cotangent = out_cotangent.astype(single)
-    grad_expert = (gate_value[:, None] * cotangent).astype(half)
-    outgoing_grad = take_rows(grad_expert, slot_owner).reshape(experts, capacity, model_width)
-    arrived, back_rows, in_grad, down_grad = expert_call(
-        outgoing, outgoing_grad, expert_in[0], expert_down[0], lax.axis_size("hid") // 2
-    )
-    local_rows = experts * capacity
-    expert_tok = arrived.reshape(local_rows, model_width)[position]
-    layer_output = (residual + gate_value[:, None] * expert_tok.astype(single)).astype(half)
-    grad_gate = jnp.sum(cotangent * expert_tok.astype(single), axis=1)
-    grad_dispatch = back_rows.reshape(local_rows, model_width)[position].astype(single)
-    grad_probs = onehot_f * grad_gate[:, None] + expert_scale[None, :]
-    grad_logits = (
-        router_probs * (grad_probs - jnp.sum(router_probs * grad_probs, axis=1, keepdims=True))
-    ).astype(half)
-    router_local = contract_rows(hidden_b, grad_logits)
-    grad_hidden_b = grad_dispatch + contract_cols(grad_logits, w_router)
-    grad_resid_n, mid_gain_local, mid_shift_local = mid_back(grad_hidden_b)
-    grad_resid = cotangent + grad_resid_n
-    grad_proj = grad_resid.astype(half)
-    proj_local = contract_rows(attended, grad_proj)
-    grad_attended = (
-        contract_cols(grad_proj, w_proj).astype(half).reshape(token_count, HEADS, head_dim)
-    )
-
-    def attend_back(carry, block_index):
-        key_total, value_total = carry
-        first_row = block_index * block_rows
-        scores = block_scores(first_row, queries)
-        probs_f = jnp.exp(scores - logsum_blocks[block_index])
-        weights = probs_f.astype(half)
-        value_total = value_total + jnp.einsum(
-            "hqk,qhd->khd", weights, grad_attended, preferred_element_type=single
+        balance_loss = small_out[0, E + 5]
+    else:
+        layer_out, input_grad, weight_grads, packed = call(
+            functools.partial(end_kernel, E, total_tokens, False),
+            outs + [((4, D, D), single), ((D, LANES), single)], working, None, "end", *given,
         )
-        grad_weights = jnp.einsum(
-            "qhd,khd->hqk", grad_attended, value_rows, preferred_element_type=single
-        )
-        grad_scores = (
-            probs_f * (grad_weights - jnp.sum(probs_f * grad_weights, axis=-1, keepdims=True))
-        ).astype(half)
-        grad_query = (
-            jnp.einsum("hqk,khd->qhd", grad_scores, key_rows, preferred_element_type=single)
-            * score_scale
-        )
-        key_total = (
-            key_total
-            + jnp.einsum("hqk,qhd->khd", grad_scores, queries, preferred_element_type=single)
-            * score_scale
-        )
-        return ((key_total, value_total), grad_query.astype(half))
-
-    zero_heads = jnp.zeros((token_count, HEADS, head_dim), single)
-    (key_total, value_total), grad_query_blocks = lax.scan(
-        attend_back, (zero_heads, zero_heads), jnp.arange(block_count, dtype=jnp.int32)
-    )
-    grad_qkv = jnp.concatenate(
-        [
-            grad_query_blocks.reshape(token_count, model_width),
-            key_total.reshape(token_count, model_width).astype(half),
-            value_total.reshape(token_count, model_width).astype(half),
-        ],
-        axis=1,
-    )
-    qkv_local = contract_rows(hidden_a, grad_qkv)
-    grad_hidden_a = contract_cols(grad_qkv, w_qkv)
-    grad_in_n, pre_gain_local, pre_shift_local = pre_back(grad_hidden_a)
-    input_grad = (grad_resid + grad_in_n).astype(half)
-    summed = (
-        lax.psum_scatter(qkv_local, ("expert", "hid"), scatter_dimension=0, tiled=True),
-        lax.psum_scatter(proj_local, ("expert", "hid"), scatter_dimension=0, tiled=True),
-        lax.psum_scatter(router_local, ("expert", "hid"), scatter_dimension=0, tiled=True),
-        lax.psum_scatter(pre_gain_local, ("expert", "hid"), scatter_dimension=0, tiled=True),
-        lax.psum_scatter(pre_shift_local, ("expert", "hid"), scatter_dimension=0, tiled=True),
-        lax.psum_scatter(mid_gain_local, ("expert", "hid"), scatter_dimension=0, tiled=True),
-        lax.psum_scatter(mid_shift_local, ("expert", "hid"), scatter_dimension=0, tiled=True),
-    )
-    (
-        qkv_grad,
-        proj_grad,
-        router_grad,
-        pre_gain_grad,
-        pre_shift_grad,
-        mid_gain_grad,
-        mid_shift_grad,
-    ) = summed
+        gathered = weight_grads.transpose(1, 0, 2).reshape(D, 4 * D)
+        gathered = lax.psum_scatter(gathered, both, scatter_dimension=0, tiled=True)
+        qkv_grad, proj_grad = gathered[:, : 3 * D], gathered[:, 3 * D :]
+        small_out = lax.psum_scatter(packed, both, scatter_dimension=0, tiled=True)
+        chance = lax.psum(jnp.sum(probs, axis=0), both)
+        balance_loss = jnp.sum(chance * counts[0]) * (balance_weight * E / total_tokens) / total_tokens
+    grads = [small_out[:, E + i] for i in range(4)]
     return (
-        layer_output,
-        balance_loss,
-        input_grad,
-        qkv_grad,
-        proj_grad,
-        router_grad,
-        pre_gain_grad,
-        pre_shift_grad,
-        mid_gain_grad,
-        mid_shift_grad,
-        in_grad[None],
-        down_grad[None],
+        layer_out, balance_loss, input_grad, qkv_grad, proj_grad, small_out[:, :E], *grads,
+        in_grad[None], down_grad[None],
     )
 
 

time: 538 us -> 253 us (0.47)
  waiting for transfers between devices: 175 us -> 0 us
  blocking collectives: 167 us -> 0 us
  Pallas kernels: 105 us -> 231 us
  matrix products: 26.3 us -> 0 us
  other arithmetic: 19.6 us -> 1.24 us
  between operations: 16.3 us -> 0.69 us
  local copies, waits for them, and re-layouts: 27.4 us -> 19.2 us
    reduce_scatter x2 -> x0, waiting for transfers between devices: 156 us -> none  [the longest x1 125 us: on_device(): lax.psum_scatter(qkv_local, ('expert', 'hid'), scatter_dimension=0, tiled...]
    pallas_call x0 -> x2, Pallas kernels: none -> 117 us  [call(): pl.pallas_call(kernel, out_shape=tuple((jax.ShapeDtypeStruct(shape, kind)...]
    psum x2 -> x0, blocking collectives: 84.4 us -> none  [on_device(): lax.psum((jnp.sum(onehot_f, axis=0), jnp.sum(router_probs, axis=0)), ('ex...]
    unnamed x1 -> x0, blocking collectives: 42.3 us -> none
    all_gather x1 -> x0, blocking collectives: 40.2 us -> none  [on_device(): lax.all_gather(router_weight.astype(half), ('expert', 'hid'), axis=0, til...]
    dot_general x15 -> x0, matrix products: 26.3 us -> none  [the longest x3 8.99 us: contract_cols(): lax.dot_general(left, right, (((1,), (1,)), ((), ())), preferred_element_...]
    all_gather x2 -> x0, waiting for transfers between devices: 19.3 us -> none  [the longest x1 19.3 us: on_device(): lax.all_gather(proj_weight.astype(half), ('expert', 'hid'), axis=0, tiled...]
    gather x4 -> x0, local copies, waits for them, and re-layouts: 10.1 us -> none  [the longest x2 5.42 us: take_rows(): return padded[slot_owner]]
  transfers between devices with their start and end apart: 4 -> 0, of which waited for: 3 -> 0; matrix products, arithmetic and copies ran while one was open for 8% -> 0% of each run, Pallas kernels for 0% -> 0%
where the time goes in v2:
time: 253 us
  Pallas kernels  231 us (91%)
  local copies, waits for them, and re-layouts  19.2 us (8%)
    pallas_call x2, Pallas kernels, call(): pl.pallas_call(kernel, out_shape=tuple((jax.ShapeDtypeStruct(shape, kind)...  117 us
    pallas_call x1, Pallas kernels, expert_call(): pl.pallas_call(functools.partial(expert_kernel, E, X, G), out_shape=(toke...  114 us
    unnamed x12, local copies, waits for them, and re-layouts  12.7 us

profile of v2, /device:TPU:0, one launch (start us, length us, event | category | flops | bytes accessed | tf_op | source)
XLA Modules:
  0.0 252.6 jit_solution(17477360060661761580)
XLA Ops:
  0.6 1.2 convert_element_type.5
  1.9 0.8 copy.30
  2.6 0.7 copy.31
  3.4 0.7 copy.32
  4.1 0.7 copy.33
  4.8 0.7 copy.34
  5.6 0.1 concatenate.3
  5.7 0.6 pad.4.refs_5_
  6.3 52.9 %start.1 = (bf16[8,64,768]{2,1,0:T(8,128)(2,1)}, bf16[8,64,768]{2,1,0:T(8,128)(2,1)}, bf16[4,768,768]{2,1,0:T(8,128)(2,1)}, bf16[768,128]{1,0:T(8,128)(2,1)}, f3...) custom-call(bf16[256,768]{1,0:T(8,128)(2,1)} %refs_0_.3, ...), custom_call_target="tpu_custom_call" | custom-call | tf_op jit(solution)/shard_map/start/pallas_call | solution.py:943
  59.2 114.1 %experts.1 = (bf16[8,64,768]{2,1,0:T(8,128)(2,1)}, bf16[8,64,768]{2,1,0:T(8,128)(2,1)}, f32[768,768]{1,0:T(8,128)}, f32[768,768]{1,0:T(8,128)}) custom-call(bf16[8,64,768]{2,1,0:T(8,128)(2,1)} %get-tuple-element.41.out_h, bf16[8,64,768]{2,1,0:T(8,128)(2,1)} %get-tuple-element.42.out_g, f32[768,768]{1,0:T(8,128)} %bitcast.11, f32[768,768]{1,0:T(8,128)} %bitcast.12), custom_call_target="tpu_custom_call" | custom-call | tf_op jit(solution)/shard_map/experts/pallas_call | solution.py:305
  173.3 0.0 copy-start.1
  173.3 64.5 %end.1 = (bf16[256,768]{1,0:T(8,128)(2,1)}, bf16[256,768]{1,0:T(8,128)(2,1)}, f32[24,2304]{1,0:T(8,128)}, f32[24,768]{1,0:T(8,128)}, f32[24,128]{1,0:T(8,128)}) custom-call(bf16[256,768]{1,0:T(8,128)(2,1)} %refs_0_.3, bf16[256,768]{1,0:T(8,128)(2,1)} %refs_1_.3, f32[1,256]{1,0:T(1,128)} %bitcast.17, bf16[4,768,768]{2,1,0:T(8,128)(2,1)} %get-tuple-element.32.refs_3_, ...), custom_call_target="tpu_custom_call" | custom-call | tf_op jit(solution)/shard_map/end/pallas_call | solution.py:943
  237.8 1.3 slice.18
  239.0 1.6 slice_reduce_fusion
  240.6 1.4 copy.35
  242.0 1.8 copy.42
  243.8 1.8 copy.43
  245.5 1.6 copy.44
  247.2 1.5 copy.45
  248.7 0.0 copy-done.1
  248.7 0.0 copy-start
  248.7 1.4 copy.46
  250.1 1.1 copy-done
  251.2 1.4 copy.47
Async XLA Ops:
  173.3 75.4 %copy-start.1 = (f32[768,768]{1,0:T(8,128)S(1)}, f32[768,768]{1,0:T(8,128)}, u32[]{:S(2)}) copy-start(f32[768,768]{1,0:T(8,128)} %get-tuple-element.50) | copy-start | bytes 7077892
  248.7 2.5 copy-start

commit v3 on v0

v3 whole, which is shorter than its diff:
```python
import functools

import jax
import jax.numpy as jnp
from jax import lax
from jax.experimental import pallas as pl
from jax.experimental.pallas import tpu as pltpu
from jax.sharding import PartitionSpec as P

epsilon = 1e-05
balance_weight = 3.0
masked_score = -1000000000.0


MESH = pl.DeviceIdType.MESH
DMA = pltpu.SemaphoreType.DMA
VMEM_SPEC = pl.BlockSpec(memory_space=pltpu.VMEM)
ANY_SPEC = pl.BlockSpec(memory_space=pl.ANY)
half = jnp.bfloat16
single = jnp.float32
STEP = 32


def remote(src, dst, send_sem, recv_sem, device):
    return pltpu.make_async_remote_copy(
        src_ref=src, dst_ref=dst, send_sem=send_sem, recv_sem=recv_sem,
        device_id=device, device_id_type=MESH,
    )


def dot(a, b):
    return jnp.dot(a, b, preferred_element_type=single)


def dot_cols(a, b):
    return lax.dot_general(a, b, (((1,), (1,)), ((), ())), preferred_element_type=single)


def dot_rows(a, b):
    return lax.dot_general(a, b, (((0,), (0,)), ((), ())), preferred_element_type=single)


def steps(count, step):
    def run(body):
        @pl.loop(0, count // step)
        def _(i):
            body(pl.ds(pl.multiple_of(i * step, step), step))
    return run


class Named:
    def __init__(self, names, refs):
        self.__dict__.update(zip(names, refs, strict=True))


def expert_scratch(E, X, cap, D, Fq):
    P, token = 2 * X, (E, cap, D)
    return dict(
        xh=pltpu.VMEM(token, half), xg=pltpu.VMEM(token, half),
        win=pltpu.VMEM((P, D, Fq), half), wdn=pltpu.VMEM((P, Fq, D), half),
        act=pltpu.VMEM((P, E * cap, Fq), half), gbef=pltpu.VMEM((P, E * cap, Fq), half),
        to=pltpu.VMEM(token, half), tg=pltpu.VMEM(token, half), xh_t=pltpu.VMEM((D, E * cap), half),
        core_in=pltpu.VMEM((X, D, Fq), half), core_dn=pltpu.VMEM((X, Fq, D), half),
        xgate=pltpu.VMEM((E, 8, E * cap), single),
        send_a=DMA((3, E)), recv_a=DMA((3, E)), send_r=DMA((2, E)), recv_r=DMA((2, E)),
        send_w=DMA((2, X)), recv_w=DMA((2, X)), send_f=DMA((2, X)), recv_f=DMA((2, X)),
        send_d=DMA((2, X)), recv_d=DMA((2, X)), send_s=DMA((2, X)), recv_s=DMA((2, X)),
    )


class Experts:
    def __init__(self, E, X, G, r, gated):
        self.E, self.X, self.G, self.r, self.gated = E, X, G, r, gated
        self.e, self.h = lax.axis_index("expert"), lax.axis_index("hid")
        self.x, self.c = lax.div(self.h, 2), lax.rem(self.h, 2)
        self.cap, self.D = r.out_h.shape[1], r.out_h.shape[2]
        self.Fq = r.win.shape[2]
        self.NG, self.rows = E // G, G * self.cap
        self.core_peer = (self.e, self.x * 2 + 1 - self.c)

    def expert_at(self, k):
        found, bit = 0, 1
        while bit < self.E:
            a, b = lax.rem(lax.div(self.e, bit), 2), lax.rem(lax.div(k, bit), 2)
            found = found + bit * (a + b - 2 * a * b)
            bit *= 2
        return found

    def x_peer(self, d):
        return (self.e, lax.rem(self.x + d, self.X) * 2 + self.c)

    def part(self, j, core):
        return lax.rem(self.x + j, self.X) * 2 + core

    def greet(self):
        barrier = pltpu.get_barrier_semaphore()

        @pl.loop(1, self.E)
        def _(k):
            pl.semaphore_signal(
                barrier, inc=1, device_id=(self.expert_at(k), self.h), device_id_type=MESH
            )

        for d in range(1, self.X):
            pl.semaphore_signal(barrier, inc=1, device_id=self.x_peer(d), device_id_type=MESH)
        pl.semaphore_signal(barrier, inc=1, device_id=self.core_peer, device_id_type=MESH)
        pl.semaphore_wait(barrier, self.E - 1 + self.X - 1 + 1)

    def weight_to_x(self, i, d):
        r, w, q = self.r, (self.r.win, self.r.wdn)[i], self.part(0, self.c)
        return remote(
            w.at[q], w.at[q], r.send_w.at[i, d], r.recv_w.at[i, self.X - d], self.x_peer(d)
        )

    def weight_to_core(self, i, j, core):
        r, w, q = self.r, (self.r.win, self.r.wdn)[i], self.part(j, core)
        return remote(w.at[q], w.at[q], r.send_f.at[i, j], r.recv_f.at[i, j], self.core_peer)

    def share_weights(self, w_in, w_dn):
        r, q = self.r, self.part(0, self.c)

        @steps(self.D, STEP)
        def _(at):
            r.win[q, at, :] = w_in[at, :].astype(half)

        for d in range(1, self.X):
            self.weight_to_x(0, d).start()

        @steps(self.Fq, STEP)
        def _(at):
            r.wdn[q, at, :] = w_dn[at, :].astype(half)

        for d in range(1, self.X):
            self.weight_to_x(1, d).start()
        for i in range(2):
            self.weight_to_core(i, 0, self.c).start()

    def wait_weights(self, j, core):
        for i in range(2):
            if core == 0:
                if j:
                    self.weight_to_x(i, self.X - j).wait_recv()
                    self.weight_to_core(i, j, self.c).start()
            else:
                self.weight_to_core(i, j, 1 - self.c).wait_recv()

    def end_weights(self):
        for i in range(2):
            for j in range(self.X):
                self.weight_to_core(i, j, self.c).wait_send()
                if j:
                    self.weight_to_x(i, j).wait_send()

    def dispatch(self, k, part):
        r = self.r
        peer = self.expert_at(k)
        if part == 2:
            src, dst = r.gates, r.xgate
        else:
            src, dst = ((r.out_h.at[peer], r.xh), (r.out_g.at[peer], r.xg))[part]
        return remote(src, dst.at[k], r.send_a.at[part, k], r.recv_a.at[part, k], (peer, self.h))

    def send_out(self, *parts):
        r = self.r

        @pl.loop(1, self.E)
        def _(k):
            for part in parts:
                self.dispatch(k, part).start()

        for part in parts:
            if part == 2:
                r.xgate[0] = r.gates[...]
            else:
                src, dst = ((r.out_h, r.xh), (r.out_g, r.xg))[part]
                dst[0] = src[self.e]

    def take(self, g):
        r, cap = self.r, self.cap

        @pl.loop(0, self.G)
        def _(i):
            k = g * self.G + i

            @pl.when(k > 0)
            def _():
                for part in (1, 2, 0) if self.gated else (1, 0):
                    self.dispatch(k, part).wait_recv()

            if self.gated:
                lane = iota((cap, self.E * cap), 1)
                wanted = iota((cap, self.E * cap), 0) + self.e * cap
                gate = jnp.where(lane == wanted, r.xgate[k, 0:1, :], 0.0)
                gate = jnp.sum(gate, axis=1, keepdims=True)
                r.xg[k] = (gate * r.xg[k].astype(single)).astype(half)

    def compute(self, g):
        r = self.r
        slots = pl.ds(g * self.G, self.G)
        at = pl.ds(pl.multiple_of(g * self.rows, self.rows), self.rows)
        xh_g = r.xh[slots].reshape(self.rows, self.D)
        xg_g = r.xg[slots].reshape(self.rows, self.D)
        parts = []
        for n in range(2 * self.X):
            j, core = n // 2, n % 2
            q = self.part(j, self.c if core == 0 else 1 - self.c)
            parts.append(q)

            @pl.when(g == 0)
            def _():
                self.wait_weights(j, core)

            v = dot(xh_g, r.win[q])
            ga = dot_cols(xg_g, r.wdn[q])
            cdf = 0.5 * (1.0 + lax.erf(v * (0.5 ** 0.5)))
            slope = cdf + v * (jnp.exp(-0.5 * v * v) * 0.3989422804014327)
            r.act[q, at, :] = (v * cdf).astype(half)
            r.gbef[q, at, :] = (slope * ga).astype(half)
        out = sum(dot(r.act[q, at, :], r.wdn[q]) for q in parts)
        gin = sum(dot_cols(r.gbef[q, at, :], r.win[q]) for q in parts)
        shape = (self.G, self.cap, self.D)
        r.to[slots] = out.astype(half).reshape(shape)
        r.tg[slots] = gin.astype(half).reshape(shape)

    def give_back(self, k, part):
        r = self.r
        src, dst = ((r.to, r.ret_o), (r.tg, r.ret_g))[part]
        return remote(
            src.at[k], dst.at[self.e], r.send_r.at[part, k], r.recv_r.at[part, k],
            (self.expert_at(k), self.h),
        )

    def run(self):
        r = self.r

        @pl.loop(0, self.NG)
        def _(g):
            self.take(g)
            self.compute(g)

            @pl.loop(0, self.G)
            def _(i):
                k = g * self.G + i

                @pl.when(k > 0)
                def _():
                    self.give_back(k, 0).start()
                    self.give_back(k, 1).start()

                @pl.when(k == 0)
                def _():
                    r.ret_o[self.e] = r.to[0]
                    r.ret_g[self.e] = r.tg[0]

    def grad_to_core(self, i, j):
        r, w, came = self.r, (self.r.win, self.r.wdn)[i], (self.r.core_in, self.r.core_dn)[i]
        return remote(w.at[j], came.at[j], r.send_d.at[i, j], r.recv_d.at[i, j], self.core_peer)

    def grad_to_x(self, i, j):
        r, w, came = self.r, (self.r.win, self.r.wdn)[i], (self.r.in_came, self.r.dn_came)[i]
        return remote(
            w.at[self.X + j], came.at[self.X - j - 1], r.send_s.at[i, j], r.recv_s.at[i, self.X - j],
            self.x_peer(j),
        )

    def weight_grads(self, in_grad, dn_grad):
        r, D, Fq = self.r, self.D, self.Fq
        T = self.E * self.cap
        tile = 256 if Fq % 256 == 0 else 128
        r.xh_t[...] = r.xh[...].reshape(T, D).T

        def grad(i, q, at):
            if i == 0:
                return dot(r.xh_t[at, :], r.gbef[q])
            return dot_rows(r.act[q, :, at], r.xg[...].reshape(T, D))

        for j in list(range(1, self.X)) + [0]:
            for i, (w, size) in enumerate(((r.win, D), (r.wdn, Fq))):
                @steps(size, tile)
                def _(at):
                    w[j, at, :] = grad(i, self.part(j, 1 - self.c), at).astype(half)

                self.grad_to_core(i, j).start()
            for i, (w, came, size) in enumerate(((r.win, r.core_in, D), (r.wdn, r.core_dn, Fq))):
                self.grad_to_core(i, j).wait_recv()

                @steps(size, tile)
                def _(at):
                    total = grad(i, self.part(j, self.c), at) + came[j, at, :].astype(single)
                    if j:
                        w[self.X + j, at, :] = total.astype(half)
                    else:
                        (in_grad, dn_grad)[i][at, :] = total

                if j:
                    self.grad_to_x(i, j).start()

    def wait_returns(self):
        @pl.loop(1, self.E)
        def _(k):
            self.give_back(k, 0).wait_recv()
            self.give_back(k, 1).wait_recv()

    def end(self):
        for i in range(2):
            for j in range(self.X):
                self.grad_to_core(i, j).wait_send()
                if j:
                    self.grad_to_x(i, j).wait()

        @pl.loop(1, self.E)
        def _(k):
            for part in range(3 if self.gated else 2):
                self.dispatch(k, part).wait_send()
                if part < 2:
                    self.give_back(k, part).wait_send()


def expert_kernel(E, X, G, names, *refs):
    r = Named(names, refs)
    experts = Experts(E, X, G, r, False)
    experts.greet()
    experts.send_out(0, 1)
    experts.share_weights(r.w_in, r.w_dn)
    experts.run()
    experts.end_weights()
    experts.weight_grads(r.in_grad, r.dn_grad)
    experts.wait_returns()
    experts.end()


def group_size(E, cap):
    return max(1, min(E, GROUP_ROWS // cap))


def call(kernel, ins, outs, scratch, collective, name):
    names = list(ins) + list(outs) + list(scratch)
    extra = dict() if collective is None else dict(collective_id=collective, has_side_effects=True)
    pairs = [value if isinstance(value, tuple) else (value, VMEM_SPEC) for value in ins.values()]
    return pl.pallas_call(
        functools.partial(kernel, names),
        out_shape=tuple(jax.ShapeDtypeStruct(value[0], value[1]) for value in outs.values()),
        in_specs=[spec for _, spec in pairs],
        out_specs=tuple(value[2] if len(value) > 2 else VMEM_SPEC for value in outs.values()),
        scratch_shapes=list(scratch.values()),
        compiler_params=pltpu.CompilerParams(vmem_limit_bytes=VMEM_LIMIT, **extra),
        name=name,
    )(*[array for array, _ in pairs])


HEAD_DIM = 64
LANES = 128


def norm_stats(values):
    average = jnp.mean(values, axis=-1, keepdims=True)
    centred = values - average
    spread = jnp.mean(centred * centred, axis=-1, keepdims=True)
    return centred, lax.rsqrt(spread + epsilon)


def norm_back(grad, values, gain):
    centred, rate = norm_stats(values)
    unit = centred * rate
    scaled = grad * gain
    toward = rate * (
        scaled
        - jnp.mean(scaled, axis=-1, keepdims=True)
        - unit * jnp.mean(scaled * unit, axis=-1, keepdims=True)
    )
    gain_grad = jnp.sum(grad * unit, axis=0, keepdims=True)
    shift_grad = jnp.sum(grad, axis=0, keepdims=True)
    return toward, gain_grad, shift_grad


def iota(shape, axis):
    return lax.broadcasted_iota(jnp.int32, shape, axis)


def slot_places(assign, capacity):
    T = assign.shape[1]
    down, across = iota((T, T), 0), iota((T, T), 1)
    column = jnp.sum(jnp.where(down == across, assign, 0.0), axis=1, keepdims=True)
    same = column == assign
    rank_column = jnp.sum(jnp.where(same & (across < down), 1.0, 0.0), axis=1, keepdims=True)
    rank_row = jnp.sum(jnp.where(same & (down < across), 1.0, 0.0), axis=0, keepdims=True)
    place_column = (column * capacity + rank_column).astype(jnp.int32)
    place_row = (assign * capacity + rank_row).astype(jnp.int32)
    return column.astype(jnp.int32), place_column, place_row


def head_probs(q_one, k_pair, allowed):
    scores = dot_cols(q_one, k_pair) * (HEAD_DIM ** -0.5)
    scores = jnp.where(allowed, scores, masked_score)
    powers = jnp.exp(scores - jnp.max(scores, axis=-1, keepdims=True))
    return powers * (1.0 / jnp.sum(powers, axis=-1, keepdims=True))


def head_masks(T):
    first = iota((T, LANES), 1) < HEAD_DIM
    low_lanes = jnp.where(first, 1.0, 0.0).astype(half)
    high_lanes = jnp.where(first, 0.0, 1.0).astype(half)
    return first, (low_lanes, high_lanes)


def columns_of(D):
    return pl.ds(0, 3 * D // 2), pl.ds(3 * D // 2, D // 2)


def pair_columns(D, m, p):
    return pl.ds(pl.multiple_of(m * (D // 2) + p * LANES, LANES), LANES)


def attend(E, r, wts, small, between=lambda: None, then=lambda: None):
    T, D = r.tokens.shape
    first_cols, last_cols = columns_of(D)
    small_t = small[...].astype(single).T
    inputs = r.tokens[...].astype(single)
    centred, rate = norm_stats(inputs)
    r.hid_a[...] = (centred * rate * small_t[E : E + 1] + small_t[E + 1 : E + 2]).astype(half)
    for part in range(2):
        r.qkv[part] = dot(r.hid_a[...], wts[part, :, first_cols]).astype(half)
    between()
    allowed = iota((T, T), 1) <= iota((T, T), 0)
    first, masks = head_masks(T)
    count = D // LANES // 2

    @pl.loop(0, 2 * count)
    def _(i):
        part, p = lax.div(i, count), lax.rem(i, count)
        q_pair, k_pair, v_pair = (r.qkv[part, :, pair_columns(D, m, p)] for m in range(3))
        mixed = [
            dot(head_probs(q_pair * mask, k_pair, allowed).astype(half), v_pair) for mask in masks
        ]
        at = pl.ds(pl.multiple_of(i * LANES, LANES), LANES)
        r.att[:, at] = jnp.where(first, mixed[0], mixed[1]).astype(half)

    then()
    for part in range(2):
        at = pl.ds(part * (D // 2), D // 2)
        r.resid[:, at] = r.tokens[:, at].astype(single) + dot(r.att[...], wts[part, :, last_cols])
    centred, rate = norm_stats(r.resid[...])
    r.hid_b[...] = (centred * rate * small_t[E + 2 : E + 3] + small_t[E + 3 : E + 4]).astype(half)
    lane = iota((T, LANES), 1)
    logits = jnp.where(lane < E, dot(r.hid_b[...], small[...]), -1e30)
    powers = jnp.exp(logits - jnp.max(logits, axis=-1, keepdims=True))
    chance = powers * (1.0 / jnp.sum(powers, axis=-1, keepdims=True))
    r.probs[...] = chance
    return jnp.sum(jnp.where(r.mine[...] > 0.0, chance, 0.0), axis=1, keepdims=True)


def set_places(E, cap, r):
    T = r.tokens.shape[0]
    column, place_column, place_row = slot_places(r.assign[...].astype(single), cap)
    r.pick[...] = jnp.where(iota((E * cap, T), 0) == place_row, 1.0, 0.0).astype(half)
    r.place[...] = jnp.where(iota((T, E * cap), 1) == place_column, 1.0, 0.0).astype(half)
    r.mine[...] = jnp.where(iota((T, LANES), 1) == column, 1.0, 0.0)


def to_slots(r, rows, out):
    out[...] = dot(r.pick[...], rows).astype(half).reshape(out.shape)


def backward_body(E, total_tokens, r, wts, small, counts):
    T, D = r.tokens.shape
    slots = r.place.shape[1]
    small_t = small[...].astype(single).T
    cot = r.cotangent[...].astype(single)
    lane = iota((T, LANES), 1)
    chance = r.probs[...]
    mine = r.mine[...]
    gate = jnp.sum(mine * chance, axis=1, keepdims=True)
    expert_tok = dot(r.place[...], r.ret_o[...].reshape(slots, D))
    r.layer_out[...] = (r.resid[...] + gate * expert_tok).astype(half)
    grad_gate = jnp.sum(cot * expert_tok, axis=1, keepdims=True)
    scale = counts * (balance_weight * E / total_tokens)
    grad_probs = mine * grad_gate + scale
    grad_logits = chance * (grad_probs - jnp.sum(chance * grad_probs, axis=1, keepdims=True))
    grad_logits = jnp.where(lane < E, grad_logits, 0.0).astype(half)
    r.router_sum[...] = dot_rows(r.hid_b[...], grad_logits)
    grad_hidden_b = dot(r.place[...], r.ret_g[...].reshape(slots, D)) + dot_cols(grad_logits, small[...])
    toward, mid_gain, mid_shift = norm_back(grad_hidden_b, r.resid[...], small_t[E + 2 : E + 3])
    r.grad_res[...] = cot + toward
    r.gproj[...] = r.grad_res[...].astype(half)
    _, last_cols = columns_of(D)
    r.gatt[...] = sum(
        dot_cols(r.gproj[:, part * (D // 2) : (part + 1) * (D // 2)], wts[part, :, last_cols])
        for part in range(2)
    ).astype(half)
    return mid_gain, mid_shift


def attend_back(r, part):
    T, D = r.tokens.shape
    allowed = iota((T, T), 1) <= iota((T, T), 0)
    first, masks = head_masks(T)

    @pl.loop(0, D // LANES // 2)
    def _(p):
        q_pair, k_pair, v_pair = (r.qkv[part, :, pair_columns(D, m, p)] for m in range(3))
        g_pair = r.gatt[:, pl.ds(pl.multiple_of(part * (D // 2) + p * LANES, LANES), LANES)]
        found = []
        for mask in masks:
            weights = head_probs(q_pair * mask, k_pair, allowed)
            grad_w = dot_cols(g_pair * mask, v_pair)
            grad_s = weights * (grad_w - jnp.sum(weights * grad_w, axis=-1, keepdims=True))
            grad_s = grad_s.astype(half)
            found.append(
                (
                    dot(grad_s, k_pair) * (HEAD_DIM ** -0.5),
                    dot_rows(grad_s, q_pair) * (HEAD_DIM ** -0.5),
                    dot_rows(weights.astype(half), g_pair),
                )
            )
        for m in range(3):
            r.gqkv[part, :, pair_columns(D, m, p)] = jnp.where(first, found[0][m], found[1][m]).astype(half)


def transposes(r):
    r.hid_a_t[...] = r.hid_a[...].T
    r.att_t[...] = r.att[...].T


def qkv_weight_grad(r, part, write):
    D = r.hid_a_t.shape[0]

    @steps(D, 256 if D % 256 == 0 else LANES)
    def _(rows):
        write(rows, dot(r.hid_a_t[rows, :], r.gqkv[part]))


def proj_weight_grad(r, part, write):
    D = r.att_t.shape[0]
    cols = pl.ds(pl.multiple_of(part * (D // 2), D // 2), D // 2)

    @steps(D, 256 if D % 256 == 0 else LANES)
    def _(rows):
        write(rows, dot(r.att_t[rows, :], r.gproj[:, cols]))


def input_body(E, r, wts, small):
    small_t = small[...].astype(single).T
    first_cols, _ = columns_of(r.tokens.shape[1])
    grad_hidden_a = sum(dot_cols(r.gqkv[part], wts[part, :, first_cols]) for part in range(2))
    toward, pre_gain, pre_shift = norm_back(
        grad_hidden_a, r.tokens[...].astype(single), small_t[E : E + 1]
    )
    r.input_grad[...] = (r.grad_res[...] + toward).astype(half)
    return pre_gain, pre_shift


def small_grads(E, router, rows, chance_sum, block, D):
    lane = iota((D, LANES), 1)
    eight = iota((LANES, D), 0)
    stacked = jnp.zeros((LANES, D), single)
    for i, row in enumerate(rows):
        stacked = jnp.where(eight == E + i, row, stacked)
    packed = jnp.where(lane < E, router, stacked.T)
    if block:
        place = lax.rem(iota((D, LANES), 0), block)
        copy = jnp.sum(jnp.where(place == lane, chance_sum, 0.0), axis=1, keepdims=True)
        packed = jnp.where(lane == E + 4, copy, packed)
    return packed


class Place:
    def __init__(self, E):
        e, h = lax.axis_index("expert"), lax.axis_index("hid")
        self.Z = E // 2
        self.z, self.y = lax.div(e, 2), lax.rem(e, 2)
        self.x, self.c = lax.div(h, 2), lax.rem(h, 2)

    def device(self, z, y, x, c):
        return (z * 2 + y, x * 2 + c)

    def z_at(self, d):
        return lax.rem(self.z + d, self.Z)

    def z_peer(self, d):
        return self.device(self.z_at(d), self.y, self.x, self.c)

    def y_peer(self):
        return self.device(self.z, 1 - self.y, self.x, self.c)

    def x_peer(self):
        return self.device(self.z, self.y, 1 - self.x, self.c)

    def core_peer(self):
        return self.device(self.z, self.y, self.x, 1 - self.c)

    def z_steps(self):
        return sorted(range(1, self.Z), key=lambda d: min(d, self.Z - d))

    def greet(self):
        barrier = pltpu.get_barrier_semaphore()
        peers = [self.z_peer(d) for d in range(1, self.Z)]
        peers += [self.y_peer(), self.x_peer(), self.core_peer()]
        for peer in peers:
            pl.semaphore_signal(barrier, inc=1, device_id=peer, device_id_type=MESH)
        pl.semaphore_wait(barrier, len(peers))


def chip_index(z, y, x):
    return (z * 2 + y) * 2 + x


class Sends:
    def __init__(self, sems):
        self.sems, self.started = sems, []

    def start(self, src, dst, recv_sem, device):
        copy = remote(src, dst, self.sems.at[len(self.started)], recv_sem, device)
        copy.start()
        self.started.append(copy)

    def finish(self):
        for copy in self.started:
            copy.wait_send()


def arrive(dst, send_sem, recv_sem, device):
    remote(dst, dst, send_sem, recv_sem, device).wait_recv()


class Gather:
    def __init__(self, at, sends, wts, small, spans, recv, rows):
        self.at, self.sends, self.wts, self.small, self.spans = at, sends, wts, small, spans
        self.recv, self.span = recv, 2 * rows

    def rows_of(self, chip):
        return pl.ds(pl.multiple_of(chip * self.span, self.span), self.span)

    def block(self, o, chip, core):
        if o == len(self.spans):
            return self.small.at[self.rows_of(chip), :]
        return self.wts.at[core, self.rows_of(chip), self.spans[o]]

    def send(self, o, chip, device):
        block = self.block(o, chip, self.at.c)
        self.sends.start(block, block, self.recv.at[0, o, chip], device)

    def share(self, o, chip):
        if o < len(self.spans):
            block = self.block(o, chip, self.at.c)
            self.sends.start(block, block, self.recv.at[1, o, chip], self.at.core_peer())

    def wait(self, o, chip):
        block = self.block(o, chip, self.at.c)
        arrive(block, self.sends.sems.at[0], self.recv.at[0, o, chip], self.at.core_peer())

    def spread(self, o, chip):
        for d in self.at.z_steps():
            self.send(o, chip, self.at.z_peer(d))
        self.send(o, chip, self.at.y_peer())
        self.share(o, chip)

    def along_x(self, o):
        at = self.at
        self.send(o, chip_index(at.z, at.y, at.x), at.x_peer())

    def own(self, o):
        at = self.at
        self.spread(o, chip_index(at.z, at.y, at.x))

    def second(self, o):
        at = self.at
        chip = chip_index(at.z, at.y, 1 - at.x)
        self.wait(o, chip)
        self.spread(o, chip)

    def third(self, o):
        at = self.at
        for x in (at.x, 1 - at.x):
            for d in at.z_steps():
                chip = chip_index(at.z_at(d), at.y, x)
                self.wait(o, chip)
                self.send(o, chip, at.y_peer())
                self.share(o, chip)

    def fourth(self, o):
        at = self.at
        for x in (at.x, 1 - at.x):
            for d in [0] + at.z_steps():
                chip = chip_index(at.z_at(d), 1 - at.y, x)
                self.wait(o, chip)
                self.share(o, chip)

    def finish(self, o):
        if o < len(self.spans):
            @pl.loop(0, 4 * self.at.Z)
            def _(chip):
                block = self.block(o, chip, 1 - self.at.c)
                arrive(block, self.sends.sems.at[0], self.recv.at[1, o, chip], self.at.core_peer())


class SumScatter:
    def __init__(self, at, sends, cols, r, recv):
        self.at, self.sends, self.cols, self.r, self.recv = at, sends, cols, r, recv
        self.span = r.final.shape[0]

    def rows_of(self, chip):
        return pl.ds(pl.multiple_of(chip * self.span, self.span), self.span)

    def swap(self):
        r = self.r
        self.sends.start(r.give.at[:, self.cols], r.got.at[:, self.cols], self.recv.at[0], self.at.core_peer())

    def wait_swap(self):
        there = self.r.got.at[:, self.cols]
        arrive(there, self.sends.sems.at[0], self.recv.at[0], self.at.core_peer())

    def send(self, slot, value, device):
        r = self.r
        r.sent[slot, :, self.cols] = value.astype(half)
        self.sends.start(
            r.sent.at[slot, :, self.cols], r.came.at[slot, :, self.cols], self.recv.at[1 + slot], device
        )

    def take(self, slot):
        there = self.r.came.at[slot, :, self.cols]
        arrive(there, self.sends.sems.at[0], self.recv.at[1 + slot], self.at.core_peer())
        return there[...].astype(single)

    def base(self, chip):
        rows = self.rows_of(chip)
        return self.r.acc[rows, self.cols] + self.r.got[rows, self.cols].astype(single)

    def one(self):
        at = self.at
        for dz in at.z_steps() + [0]:
            for x in range(2):
                chip = chip_index(at.z_at(dz), 1 - at.y, x)
                self.send(dz * 2 + x, self.base(chip), at.y_peer())

    def two(self):
        at = self.at
        for dz in at.z_steps() + [0]:
            for x in range(2):
                chip = chip_index(at.z_at(dz), at.y, x)
                value = self.base(chip) + self.take(dz * 2 + x)
                if dz:
                    self.send(2 * at.Z + dz * 2 + x, value, at.z_peer(dz))
                else:
                    self.r.acc[self.rows_of(chip), self.cols] = value

    def three(self):
        at = self.at
        for flip in (1, 0):
            x = 1 - at.x if flip else at.x
            value = self.r.acc[self.rows_of(chip_index(at.z, at.y, x)), self.cols]
            for dz in range(1, at.Z):
                value = value + self.take(2 * at.Z + dz * 2 + x)
            if flip:
                self.send(4 * at.Z, value, at.x_peer())
            else:
                self.r.final[:, self.cols] = value

    def four(self):
        at, r = self.at, self.r
        r.final[:, self.cols] += self.take(4 * at.Z)
        rows = self.span // 2
        there = r.final.at[pl.ds(pl.multiple_of((1 - at.c) * rows, rows), rows), self.cols]
        last = self.recv.shape[0] - 1
        self.sends.start(there, r.final_other.at[:, self.cols], self.recv.at[last], at.core_peer())

    def end(self):
        there = self.r.final_other.at[:, self.cols]
        arrive(there, self.sends.sems.at[0], self.recv.at[self.recv.shape[0] - 1], self.at.core_peer())


VMEM_LIMIT = 62 * 1024 * 1024
GROUP_ROWS = 128


def model_scratch(E, T, D, cap):
    slots = E * cap
    return dict(
        pick=pltpu.VMEM((slots, T), half), place=pltpu.VMEM((T, slots), half),
        mine=pltpu.VMEM((T, LANES), single),
    )


def end_scratch(T, D):
    return dict(
        gqkv=pltpu.VMEM((2, T, 3 * D // 2), half), gproj=pltpu.VMEM((T, D), half), gatt=pltpu.VMEM((T, D), half),
        grad_res=pltpu.VMEM((T, D), single), router_sum=pltpu.VMEM((D, LANES), single),
        hid_a_t=pltpu.VMEM((D, T), half), att_t=pltpu.VMEM((D, T), half),
    )


def start_kernel(E, names, *refs):
    r = Named(names, refs)
    cap = r.out_h.shape[1]
    set_places(E, cap, r)
    gate = attend(E, r, r.wts, r.small)
    to_slots(r, r.hid_b[...], r.out_h)
    to_slots(r, (gate * r.cotangent[...].astype(single)).astype(half), r.out_g)


def end_kernel(E, total_tokens, names, *refs):
    r = Named(names, refs)
    D = r.tokens.shape[1]
    set_places(E, r.ret_o.shape[1], r)
    transposes(r)
    mid_gain, mid_shift = backward_body(E, total_tokens, r, r.wts, r.small, r.counts[0:1])
    first_cols, last_cols = columns_of(D)
    for part in range(2):
        attend_back(r, part)

        def write_first(rows, value):
            r.weight_grads[part, rows, first_cols] = value

        def write_last(rows, value):
            r.weight_grads[part, rows, last_cols] = value

        qkv_weight_grad(r, part, write_first)
        proj_weight_grad(r, part, write_last)
    pre_gain, pre_shift = input_body(E, r, r.wts, r.small)
    chance_sum = jnp.sum(r.probs[...], axis=0, keepdims=True)
    r.small_out[...] = small_grads(
        E, r.router_sum[...], (pre_gain, pre_shift, mid_gain, mid_shift), chance_sum, 0, D
    )


class SmallSum:
    def __init__(self, at, sends, r, rows):
        self.at, self.sends, self.r, self.rows = at, sends, r, rows

    def rows_of(self, z, y, x):
        first = chip_index(z, y, x) * 2 * self.rows + self.at.c * self.rows
        return pl.ds(pl.multiple_of(first, self.rows), self.rows)

    def send(self, slot, value, device):
        r = self.r
        r.pack_sent[slot] = value
        self.sends.start(r.pack_sent.at[slot], r.pack_came.at[slot], r.pack_recv.at[1 + slot], device)

    def take(self, slot):
        r = self.r
        arrive(r.pack_came.at[slot], r.send.at[0], r.pack_recv.at[1 + slot], self.at.core_peer())
        return r.pack_came[slot]

    def zero(self):
        r = self.r
        self.sends.start(r.pack, r.pack_other, r.pack_recv.at[0], self.at.core_peer())

    def one(self):
        r, at = self.r, self.at
        arrive(r.pack_other, r.send.at[0], r.pack_recv.at[0], at.core_peer())
        r.pack_other[...] += r.pack[...]
        for dz in range(at.Z):
            for y in range(2):
                self.send(dz * 2 + y, r.pack_other[self.rows_of(at.z_at(dz), y, 1 - at.x), :], at.x_peer())

    def two(self):
        r, at = self.r, self.at
        for dz in range(at.Z):
            for flip in (1, 0):
                y = 1 - at.y if flip else at.y
                here = self.rows_of(at.z_at(dz), y, at.x)
                value = r.pack_other[here, :] + self.take(dz * 2 + y)
                if flip:
                    self.send(2 * at.Z + dz, value, at.y_peer())
                else:
                    r.pack_other[here, :] = value

    def three(self):
        r, at = self.r, self.at
        for dz in at.z_steps() + [0]:
            value = r.pack_other[self.rows_of(at.z_at(dz), at.y, at.x), :] + self.take(2 * at.Z + dz)
            if dz:
                self.send(3 * at.Z + dz, value, at.z_peer(dz))
        return value

    def four(self, total):
        for dz in range(1, self.at.Z):
            total = total + self.take(3 * self.at.Z + dz)
        return total


def whole_scratch(E, T, D, cap, rows):
    Z = E // 2
    slots = 4 * Z + 1
    token = (E, cap, D)
    return dict(
        wts=pltpu.VMEM((2, D, 2 * D), half), small=pltpu.VMEM((D, LANES), half),
        shard=pltpu.VMEM((2, rows, 2 * D), single), small_shard=pltpu.VMEM((rows, LANES), single),
        other=pltpu.VMEM((rows, 2 * D), single), other_small=pltpu.VMEM((rows, LANES), single),
        square=pltpu.VMEM((LANES, LANES), single), counts=pltpu.VMEM((8, LANES), single),
        hid_a=pltpu.VMEM((T, D), half), qkv=pltpu.VMEM((2, T, 3 * D // 2), half), att=pltpu.VMEM((T, D), half),
        resid=pltpu.VMEM((T, D), single), hid_b=pltpu.VMEM((T, D), half),
        probs=pltpu.VMEM((T, LANES), single), gates=pltpu.VMEM((8, E * cap), single),
        out_h=pltpu.VMEM(token, half), out_g=pltpu.VMEM(token, half),
        ret_o=pltpu.VMEM(token, half), ret_g=pltpu.VMEM(token, half),
        acc=pltpu.VMEM((D, 2 * D), single), give=pltpu.VMEM((D, 2 * D), half), got=pltpu.VMEM((D, 2 * D), half),
        sent=pltpu.VMEM((slots, 2 * rows, 2 * D), half), came=pltpu.VMEM((slots, 2 * rows, 2 * D), half),
        final=pltpu.VMEM((2 * rows, 2 * D), single), final_other=pltpu.VMEM((rows, 2 * D), single),
        pack=pltpu.VMEM((D, LANES), single), pack_other=pltpu.VMEM((D, LANES), single),
        pack_sent=pltpu.VMEM((4 * Z, rows, LANES), single),
        pack_came=pltpu.VMEM((4 * Z, rows, LANES), single),
        local=DMA((4,)), send=DMA((40 * Z + 16,)), gather_recv=DMA((2, 3, 4 * Z)), own_recv=DMA((2,)),
        sum_recv=DMA((2, slots + 2)), pack_recv=DMA((4 * Z + 1,)),
    )


def whole_kernel(E, total_tokens, G, names, *refs):
    r = Named(names, refs)
    rows, D = r.proj_shard.shape
    T = r.tokens.shape[0]
    cap = r.out_h.shape[1]
    at = Place(E)
    experts = Experts(E, 2, G, r, True)
    sends = Sends(r.send)
    width = D // 2
    first_cols, last_cols = columns_of(D)
    through = r.acc.at[:, 0:D], r.acc.at[:, D : 2 * D]
    loads = [
        pltpu.make_async_copy(w.at[0], there, r.local.at[i])
        for i, (w, there) in enumerate(zip((r.w_in, r.w_dn), through))
    ]
    for load in loads:
        load.start()
    for part in range(2):
        for m in range(3):
            first = m * D + part * width
            r.shard[part, :, m * width : (m + 1) * width] = r.qkv_shard[:, first : first + width]
        r.shard[part, :, 3 * width :] = r.proj_shard[:, part * width : (part + 1) * width]
    assign = r.assign[...].astype(single)
    r.square[...] = jnp.zeros_like(r.square)
    r.square[0:E, 0:rows] = r.router[...]
    for i, gain in enumerate((r.pre_gain, r.pre_shift, r.mid_gain, r.mid_shift)):
        r.square[E + i : E + i + 1, 0:rows] = gain[...]
    numbers = iota((rows, T), 0).astype(single)
    count = jnp.sum(jnp.where(assign == numbers, 1.0, 0.0), axis=1, keepdims=True)
    lane = iota((rows, LANES), 1)
    r.small_shard[...] = jnp.where(lane == E + 4, count, r.square[...].T[0:rows, :])

    experts.greet()
    core = at.core_peer()
    sends.start(r.shard.at[1 - at.c], r.other, r.own_recv.at[0], core)
    sends.start(r.small_shard, r.other_small, r.own_recv.at[1], core)
    gather = Gather(at, sends, r.wts, r.small, (first_cols, last_cols), r.gather_recv, rows)
    own_rows = gather.rows_of(chip_index(at.z, at.y, at.x))

    def both(here, there):
        low, high = jnp.where(at.c == 0, here, there), jnp.where(at.c == 0, there, here)
        return jnp.concatenate([low, high], axis=0).astype(half)

    arrive(r.other, r.send.at[0], r.own_recv.at[0], core)
    r.wts[at.c, own_rows, :] = both(r.shard[at.c], r.other[...])
    gather.along_x(0)
    gather.own(0)
    arrive(r.other_small, r.send.at[0], r.own_recv.at[1], core)
    r.small[own_rows, :] = both(r.small_shard[...], r.other_small[...])
    gather.along_x(2)
    gather.along_x(1)
    gather.own(2)
    for load in loads:
        load.wait()
    experts.share_weights(*through)
    gather.second(0)
    gather.second(2)
    gather.third(0)
    gather.third(2)
    set_places(E, cap, r)
    to_slots(r, r.cotangent[...], r.out_g)
    gather.own(1)
    gather.fourth(0)
    gather.fourth(2)
    gather.second(1)
    experts.send_out(1)
    gather.finish(0)
    place = lax.rem(iota((D, LANES), 0), rows)
    column = r.small[:, E + 4 : E + 5].astype(single)
    total = jnp.sum(jnp.where(place == iota((D, LANES), 1), column, 0.0), axis=0, keepdims=True)
    r.counts[...] = jnp.broadcast_to(total, r.counts.shape)

    def between():
        gather.third(1)

    def then():
        gather.fourth(1)
        gather.finish(1)

    gate = attend(E, r, r.wts, r.small, between, then)
    to_slots(r, r.hid_b[...], r.out_h)
    gates = jnp.sum(r.place[...].astype(single) * gate, axis=0, keepdims=True)
    r.gates[...] = jnp.broadcast_to(gates, r.gates.shape)
    experts.send_out(2, 0)
    experts.run()
    experts.end_weights()
    experts.weight_grads(*through)
    stores = [
        pltpu.make_async_copy(there, w.at[0], r.local.at[2 + i])
        for i, (w, there) in enumerate(zip((r.in_own, r.dn_own), through))
    ]
    for store in stores:
        store.start()
    transposes(r)
    experts.wait_returns()

    mid_gain, mid_shift = backward_body(E, total_tokens, r, r.wts, r.small, r.counts[0:1])
    for store in stores:
        store.wait()
    first = SumScatter(at, sends, first_cols, r, r.sum_recv.at[0])
    last = SumScatter(at, sends, last_cols, r, r.sum_recv.at[1])
    smalls = SmallSum(at, sends, r, rows)

    def give_last(here, value):
        r.give[here, last_cols] = value.astype(half)

    def keep_last(here, value):
        r.acc[here, last_cols] = value

    def give_first(here, value):
        r.give[here, first_cols] = value.astype(half)

    def keep_first(here, value):
        r.acc[here, first_cols] = value

    proj_weight_grad(r, 1 - at.c, give_last)
    last.swap()
    proj_weight_grad(r, at.c, keep_last)
    attend_back(r, 1 - at.c)
    qkv_weight_grad(r, 1 - at.c, give_first)
    first.swap()
    last.wait_swap()
    last.one()
    attend_back(r, at.c)
    qkv_weight_grad(r, at.c, keep_first)
    first.wait_swap()
    first.one()
    last.two()
    pre_gain, pre_shift = input_body(E, r, r.wts, r.small)
    chance_sum = jnp.sum(r.probs[...], axis=0, keepdims=True)
    r.pack[...] = small_grads(
        E, r.router_sum[...], (pre_gain, pre_shift, mid_gain, mid_shift), chance_sum, rows, D
    )
    smalls.zero()
    last.three()
    first.two()
    smalls.one()
    last.four()
    smalls.two()
    first.three()
    total = smalls.three()
    first.four()
    total = smalls.four(total)
    scale = r.counts[0:1] * (balance_weight * E / total_tokens)
    chance = jnp.sum(jnp.where(lane == E + 4, total, 0.0), axis=1, keepdims=True)
    chosen = jnp.where((lane == iota((rows, LANES), 0)) & (lane < E), chance * scale, 0.0)
    loss = jnp.sum(jnp.sum(chosen, axis=1, keepdims=True), axis=0, keepdims=True) / total_tokens
    r.square[0:rows, :] = jnp.where(lane == E + 5, loss, total)
    r.small_out[...] = r.square[...].T[0 : r.small_out.shape[0], :]
    last.end()
    first.end()
    half_rows = pl.ds(pl.multiple_of(at.c * rows, rows), rows)
    mine, theirs = r.final[half_rows, :], r.final_other[...]
    for part, value in enumerate((jnp.where(at.c == 0, mine, theirs), jnp.where(at.c == 0, theirs, mine))):
        for m in range(3):
            begin = m * D + part * width
            r.qkv_grad[:, begin : begin + width] = value[:, m * width : (m + 1) * width]
        r.proj_grad[:, part * width : (part + 1) * width] = value[:, 3 * width :]
    experts.end()
    sends.finish()


def out_kernel(E, names, *refs):
    r = Named(names, refs)
    pairs = [
        (r.in_own, r.h0), (r.in_came, r.h1), (r.dn_own, r.h2), (r.dn_came, r.h3),
        (r.layer_in, r.h4), (r.input_in, r.h5), (r.qkv_in, r.h6), (r.proj_in, r.h7),
    ]
    loads = [pltpu.make_async_copy(src, there, r.sems.at[0, i]) for i, (src, there) in enumerate(pairs)]
    outs = [
        (r.h0, r.in_grad), (r.h2, r.dn_grad), (r.h4, r.layer_out), (r.h5, r.input_grad), (r.h6, r.qkv_grad),
        (r.h7, r.proj_grad),
    ]
    stores = [pltpu.make_async_copy(there, dst, r.sems.at[1, i]) for i, (there, dst) in enumerate(outs)]
    for load in loads:
        load.start()
    rows = r.proj_in.shape[0]
    r.router[...] = r.small_in[0:E, 0:rows]
    for i, gain in enumerate((r.pre_gain, r.pre_shift, r.mid_gain, r.mid_shift)):
        gain[...] = r.small_in[E + i : E + i + 1, 0:rows]
    r.loss[...] = r.small_in[E + 5 : E + 6, 0:1]
    for i, (own, came) in enumerate(((r.h0, r.h1), (r.h2, r.h3))):
        loads[2 * i].wait()
        loads[2 * i + 1].wait()

        @steps(own.shape[1], STEP)
        def _(at):
            own[0, at, :] += sum(came[j, at, :].astype(single) for j in range(came.shape[0]))

        stores[i].start()
    for load, store in zip(loads[4:], stores[2:]):
        load.wait()
        store.start()
    for store in stores:
        store.wait()


def on_device(
    tokens_in, out_cotangent, qkv_weight, proj_weight, router_weight, pre_gain, pre_shift, mid_gain, mid_shift,
    expert_in, expert_down, assignment,
):
    T, D = tokens_in.shape
    E, H = lax.axis_size("expert"), lax.axis_size("hid")
    X = H // 2
    Z = E // 2
    cap = 2 * T // E
    G = group_size(E, cap)
    Fq = expert_in.shape[2]
    total_tokens = T * E * H
    rows = proj_weight.shape[0]
    both = ("expert", "hid")
    assign = assignment.reshape(1, T)
    token = ((T, D), half)
    slot = ((E, cap, D), half)
    vectors = dict(pre_gain=pre_gain, pre_shift=pre_shift, mid_gain=mid_gain, mid_shift=mid_shift)
    if X == 2 and E % 2 == 0 and rows % 8 == 0 and E <= rows <= LANES and Fq == D and D % 256 == 0:
        small_rows = E + 8
        found = call(
            functools.partial(whole_kernel, E, total_tokens, G),
            dict(
                tokens=tokens_in, cotangent=out_cotangent, assign=assign,
                qkv_shard=qkv_weight, proj_shard=proj_weight, router=router_weight.T,
                **dict((name, value.reshape(1, rows)) for name, value in vectors.items()),
                w_in=(expert_in, ANY_SPEC), w_dn=(expert_down, ANY_SPEC),
            ),
            dict(
                layer_out=token, input_grad=token, qkv_grad=((rows, 3 * D), single),
                proj_grad=((rows, D), single), small_out=((small_rows, LANES), single),
                in_own=((1, D, Fq), single, ANY_SPEC), dn_own=((1, Fq, D), single, ANY_SPEC),
                in_came=((X - 1, D, Fq), half, ANY_SPEC), dn_came=((X - 1, Fq, D), half, ANY_SPEC),
            ),
            dict(
                **whole_scratch(E, T, D, cap, rows), **model_scratch(E, T, D, cap), **end_scratch(T, D),
                **expert_scratch(E, X, cap, D, Fq),
            ),
            1, "layer",
        )
        layer_out, input_grad, qkv_grad, proj_grad, small_out, in_own, dn_own, in_came, dn_came = found
        vector = ((1, rows), single)
        found = call(
            functools.partial(out_kernel, E),
            dict(
                layer_in=(layer_out, ANY_SPEC), input_in=(input_grad, ANY_SPEC),
                qkv_in=(qkv_grad, ANY_SPEC), proj_in=(proj_grad, ANY_SPEC),
                in_own=(in_own, ANY_SPEC), dn_own=(dn_own, ANY_SPEC),
                in_came=(in_came, ANY_SPEC), dn_came=(dn_came, ANY_SPEC), small_in=small_out,
            ),
            dict(
                layer_out=token + (ANY_SPEC,), input_grad=token + (ANY_SPEC,),
                qkv_grad=((rows, 3 * D), single, ANY_SPEC), proj_grad=((rows, D), single, ANY_SPEC),
                in_grad=((1, D, Fq), single, ANY_SPEC), dn_grad=((1, Fq, D), single, ANY_SPEC),
                router=((E, rows), single), pre_gain=vector, pre_shift=vector, mid_gain=vector,
                mid_shift=vector, loss=((1, 1), single),
            ),
            dict(
                h0=pltpu.VMEM((1, D, Fq), single), h1=pltpu.VMEM((X - 1, D, Fq), half),
                h2=pltpu.VMEM((1, Fq, D), single), h3=pltpu.VMEM((X - 1, Fq, D), half),
                h4=pltpu.VMEM(*token), h5=pltpu.VMEM(*token), h6=pltpu.VMEM((rows, 3 * D), single),
                h7=pltpu.VMEM((rows, D), single), sems=DMA((2, 8)),
            ),
            None, "results",
        )
        layer_out, input_grad, qkv_grad, proj_grad, in_grad, dn_grad, router, *grads, loss = found
        return (
            layer_out, loss.reshape(()), input_grad, qkv_grad, proj_grad, router.T,
            *[value.reshape(rows) for value in grads], in_grad, dn_grad,
        )

    small_in = jnp.concatenate([router_weight] + [value[:, None] for value in vectors.values()], axis=1)
    small_in = jnp.pad(small_in, ((0, 0), (0, LANES - small_in.shape[1])))
    shard = jnp.concatenate([qkv_weight, proj_weight], axis=1).astype(half)
    wts = lax.all_gather(shard, both, axis=0, tiled=True).reshape(D, 4, 2, D // 2)
    wts = wts.transpose(2, 0, 1, 3).reshape(2, D, 2 * D)
    small = lax.all_gather(small_in.astype(half), both, axis=0, tiled=True)
    onehot = assignment[:, None] == jnp.arange(LANES, dtype=jnp.int32)[None, :]
    counts = lax.psum(jnp.sum(onehot.astype(single), axis=0), both)
    saved = dict(
        hid_a=token, qkv=((2, T, 3 * D // 2), half), att=token, resid=((T, D), single), hid_b=token,
        probs=((T, LANES), single),
    )
    given = dict(tokens=tokens_in, cotangent=out_cotangent, assign=assign, wts=wts, small=small)
    out_h, out_g, *rest = call(
        functools.partial(start_kernel, E), given, dict(out_h=slot, out_g=slot, **saved),
        model_scratch(E, T, D, cap), None, "start",
    )
    ret_o, ret_g, in_own, dn_own, in_came, dn_came = call(
        functools.partial(expert_kernel, E, X, G),
        dict(out_h=out_h, out_g=out_g, w_in=expert_in[0], w_dn=expert_down[0]),
        dict(
            ret_o=slot, ret_g=slot, in_grad=((D, Fq), single), dn_grad=((Fq, D), single),
            in_came=((X - 1, D, Fq), half), dn_came=((X - 1, Fq, D), half),
        ),
        expert_scratch(E, X, cap, D, Fq), 1, "experts",
    )
    in_grad = in_own + jnp.sum(in_came.astype(single), axis=0)
    dn_grad = dn_own + jnp.sum(dn_came.astype(single), axis=0)
    layer_out, input_grad, weight_grads, packed = call(
        functools.partial(end_kernel, E, total_tokens),
        dict(
            **given, counts=jnp.broadcast_to(counts[None, :], (8, LANES)), **dict(zip(saved, rest)),
            ret_o=ret_o, ret_g=ret_g,
        ),
        dict(
            layer_out=token, input_grad=token, weight_grads=((2, D, 2 * D), single),
            small_out=((D, LANES), single),
        ),
        dict(**model_scratch(E, T, D, cap), **end_scratch(T, D)), None, "end",
    )
    gathered = weight_grads.reshape(2, D, 4, D // 2).transpose(1, 2, 0, 3).reshape(D, 4 * D)
    gathered = lax.psum_scatter(gathered, both, scatter_dimension=0, tiled=True)
    small_out = lax.psum_scatter(packed, both, scatter_dimension=0, tiled=True)
    chance = lax.psum(jnp.sum(rest[-1], axis=0), both)
    balance_loss = jnp.sum(chance * counts) * (balance_weight * E / total_tokens) / total_tokens
    return (
        layer_out, balance_loss, input_grad, gathered[:, : 3 * D], gathered[:, 3 * D :], small_out[:, :E],
        *[small_out[:, E + i] for i in range(4)], in_grad[None], dn_grad[None],
    )


def solution(mesh):
    in_specs = (
        P(("expert", "hid"), None),
        P(("expert", "hid"), None),
        P(("expert", "hid"), None),
        P(("expert", "hid"), None),
        P(("expert", "hid"), None),
        P(("expert", "hid")),
        P(("expert", "hid")),
        P(("expert", "hid")),
        P(("expert", "hid")),
        P("expert", None, "hid"),
        P("expert", "hid", None),
        P(("expert", "hid")),
    )
    out_specs = (
        P(("expert", "hid"), None),
        P(),
        P(("expert", "hid"), None),
        P(("expert", "hid"), None),
        P(("expert", "hid"), None),
        P(("expert", "hid"), None),
        P(("expert", "hid")),
        P(("expert", "hid")),
        P(("expert", "hid")),
        P(("expert", "hid")),
        P("expert", None, "hid"),
        P("expert", "hid", None),
    )
    return jax.shard_map(
        on_device, mesh=mesh, in_specs=in_specs, out_specs=out_specs, check_vma=False
    )
```

time: 742 us -> 178 us (0.24); the launches traced: 734 us -> 177 us
  waiting for transfers between devices: 331 us -> 0 us
  blocking collectives: 240 us -> 0 us
  Pallas kernels: 0 us -> 177 us
  matrix products: 76.8 us -> 0 us
  local copies, waits for them, and re-layouts: 34 us -> 0 us
  other arithmetic: 28.8 us -> 0 us
  between operations: 17.1 us -> 0.82 us
    reduce_scatter x4 -> x0, waiting for transfers between devices: 222 us -> none  [the longest x1 125 us: on_device(): lax.psum_scatter(qkv_local, ('expert', 'hid'), scatter_dimension=0, tiled...]
    pallas_call x0 -> x2, Pallas kernels: none -> 177 us  [call(): pl.pallas_call(functools.partial(kernel, names), out_shape=tuple((jax.Sha...]
    all_gather x4 -> x0, waiting for transfers between devices: 108 us -> none  [the longest x1 45.3 us: on_device(): lax.all_gather(proj_weight.astype(half), ('expert', 'hid'), axis=0, tiled...]
    psum x2 -> x0, blocking collectives: 81.7 us -> none  [on_device(): lax.psum((jnp.sum(onehot_f, axis=0), jnp.sum(router_probs, axis=0)), ('ex...]
    dot_general x21 -> x0, matrix products: 76.8 us -> none  [the longest x5 21.5 us: contract_cols(): lax.dot_general(left, right, (((1,), (1,)), ((), ())), preferred_element_...]
    all_to_all x3 -> x0, blocking collectives: 75.9 us -> none  [the longest x1 25.8 us: on_device(): lax.all_to_all(sending_back, 'expert', split_axis=0, concat_axis=0, tiled...]
    unnamed x1 -> x0, blocking collectives: 42.3 us -> none
    all_gather x1 -> x0, blocking collectives: 39.9 us -> none  [on_device(): lax.all_gather(router_weight.astype(half), ('expert', 'hid'), axis=0, til...]
  transfers between devices with their start and end apart: 9 -> 0, of which waited for: 8 -> 0; matrix products, arithmetic and copies ran while one was open for 9% -> 0% of each run, Pallas kernels for 0% -> 0%
where the time goes in v3:
time: 178 us; the launch traced here: 177 us
  Pallas kernels  177 us (99%)
    pallas_call x2, Pallas kernels, call(): pl.pallas_call(functools.partial(kernel, names), out_shape=tuple((jax.Sha...  177 us

profile of v3, /device:TPU:0, one launch (start us, length us, event | category | flops | bytes accessed | tf_op | source)
XLA Modules:
  0.0 177.4 jit_solution(11775764798053218146)
XLA Ops:
  0.6 170.1 %layer.1 = (bf16[256,768]{1,0:T(8,128)(2,1)}, bf16[256,768]{1,0:T(8,128)(2,1)}, f32[24,2304]{1,0:T(8,128)}, f32[24,768]{1,0:T(8,128)}, f32[16,128]{1,0:T(8,128)}...) custom-call(bf16[256,768]{1,0:T(8,128)(2,1)} %refs_0_.1, ...), custom_call_target="tpu_custom_call" | custom-call | tf_op jit(solution)/shard_map/layer/pallas_call | solution.py:340
  170.8 6.5 %results.1 = (bf16[256,768]{1,0:T(8,128)(2,1)}, bf16[256,768]{1,0:T(8,128)(2,1)}, f32[24,2304]{1,0:T(8,128)}, f32[24,768]{1,0:T(8,128)}, f32[1,768,768]{2,1,0:T(...) custom-call(bf16[256,768]{1,0:T(8,128)(2,1)} %get-tuple-element.33.r, ...), custom_call_target="tpu_custom_call" | custom-call | tf_op jit(solution)/shard_map/results/pallas_call | solution.py:340

commit v4 on v3

--- a/solution.py
+++ b/solution.py
@@ -38,6 +38,10 @@
 
 def dot_rows(a, b):
     return lax.dot_general(a, b, (((0,), (0,)), ((), ())), preferred_element_type=single)
+
+
+def grad_rows(size):
+    return 256 if size % 256 == 0 else 128
 
 
 def steps(count, step):
@@ -61,8 +65,9 @@
         act=pltpu.VMEM((P, E * cap, Fq), half), gbef=pltpu.VMEM((P, E * cap, Fq), half),
         to=pltpu.VMEM(token, half), tg=pltpu.VMEM(token, half), xh_t=pltpu.VMEM((D, E * cap), half),
         core_in=pltpu.VMEM((X, D, Fq), half), core_dn=pltpu.VMEM((X, Fq, D), half),
-        xgate=pltpu.VMEM((E, 8, E * cap), single),
-        send_a=DMA((3, E)), recv_a=DMA((3, E)), send_r=DMA((2, E)), recv_r=DMA((2, E)),
+        xgate=pltpu.VMEM((E, 8, E * cap), single), raw=pltpu.VMEM(token, half),
+        tgg=pltpu.VMEM((E, 8, E * cap), single), ret_gg=pltpu.VMEM((E, 8, E * cap), single),
+        send_a=DMA((3, E)), recv_a=DMA((3, E)), send_r=DMA((3, E)), recv_r=DMA((3, E)),
         send_w=DMA((2, X)), recv_w=DMA((2, X)), send_f=DMA((2, X)), recv_f=DMA((2, X)),
         send_d=DMA((2, X)), recv_d=DMA((2, X)), send_s=DMA((2, X)), recv_s=DMA((2, X)),
     )
@@ -77,6 +82,7 @@
         self.Fq = r.win.shape[2]
         self.NG, self.rows = E // G, G * self.cap
         self.core_peer = (self.e, self.x * 2 + 1 - self.c)
+        self.landing = r.raw if gated else r.xg
 
     def expert_at(self, k):
         found, bit = 0, 1
@@ -104,7 +110,9 @@
         for d in range(1, self.X):
             pl.semaphore_signal(barrier, inc=1, device_id=self.x_peer(d), device_id_type=MESH)
         pl.semaphore_signal(barrier, inc=1, device_id=self.core_peer, device_id_type=MESH)
-        pl.semaphore_wait(barrier, self.E - 1 + self.X - 1 + 1)
+
+    def meet(self):
+        pl.semaphore_wait(pltpu.get_barrier_semaphore(), self.E - 1 + self.X - 1 + 1)
 
     def weight_to_x(self, i, d):
         r, w, q = self.r, (self.r.win, self.r.wdn)[i], self.part(0, self.c)
@@ -157,7 +165,7 @@
         if part == 2:
             src, dst = r.gates, r.xgate
         else:
-            src, dst = ((r.out_h.at[peer], r.xh), (r.out_g.at[peer], r.xg))[part]
+            src, dst = ((r.out_h.at[peer], r.xh), (r.out_g.at[peer], self.landing))[part]
         return remote(src, dst.at[k], r.send_a.at[part, k], r.recv_a.at[part, k], (peer, self.h))
 
     def send_out(self, *parts):
@@ -172,8 +180,12 @@
             if part == 2:
                 r.xgate[0] = r.gates[...]
             else:
-                src, dst = ((r.out_h, r.xh), (r.out_g, r.xg))[part]
+                src, dst = ((r.out_h, r.xh), (r.out_g, self.landing))[part]
                 dst[0] = src[self.e]
+
+    def own_lanes(self):
+        shape = (self.cap, self.E * self.cap)
+        return iota(shape, 1) == iota(shape, 0) + self.e * self.cap
 
     def take(self, g):
         r, cap = self.r, self.cap
@@ -188,11 +200,9 @@
                     self.dispatch(k, part).wait_recv()
 
             if self.gated:
-                lane = iota((cap, self.E * cap), 1)
-                wanted = iota((cap, self.E * cap), 0) + self.e * cap
-                gate = jnp.where(lane == wanted, r.xgate[k, 0:1, :], 0.0)
+                gate = jnp.where(self.own_lanes(), r.xgate[k, 0:1, :], 0.0)
                 gate = jnp.sum(gate, axis=1, keepdims=True)
-                r.xg[k] = (gate * r.xg[k].astype(single)).astype(half)
+                r.xg[k] = (gate * r.raw[k].astype(single)).astype(half)
 
     def compute(self, g):
         r = self.r
@@ -221,10 +231,17 @@
         shape = (self.G, self.cap, self.D)
         r.to[slots] = out.astype(half).reshape(shape)
         r.tg[slots] = gin.astype(half).reshape(shape)
+        if self.gated:
+            @pl.loop(0, self.G)
+            def _(i):
+                k = g * self.G + i
+                toward = jnp.sum(r.raw[k].astype(single) * r.to[k].astype(single), axis=1, keepdims=True)
+                row = jnp.sum(jnp.where(self.own_lanes(), toward, 0.0), axis=0, keepdims=True)
+                r.tgg[k] = jnp.broadcast_to(row, r.tgg.shape[1:])
 
     def give_back(self, k, part):
         r = self.r
-        src, dst = ((r.to, r.ret_o), (r.tg, r.ret_g))[part]
+        src, dst = ((r.to, r.ret_o), (r.tg, r.ret_g), (r.tgg, r.ret_gg))[part]
         return remote(
             src.at[k], dst.at[self.e], r.send_r.at[part, k], r.recv_r.at[part, k],
             (self.expert_at(k), self.h),
@@ -232,6 +249,7 @@
 
     def run(self):
         r = self.r
+        parts = (1, 2) if self.gated else (1,)
 
         @pl.loop(0, self.NG)
         def _(g):
@@ -244,13 +262,17 @@
 
                 @pl.when(k > 0)
                 def _():
-                    self.give_back(k, 0).start()
-                    self.give_back(k, 1).start()
-
-                @pl.when(k == 0)
-                def _():
-                    r.ret_o[self.e] = r.to[0]
-                    r.ret_g[self.e] = r.tg[0]
+                    for part in parts:
+                        self.give_back(k, part).start()
+
+        @pl.loop(1, self.E)
+        def _(k):
+            self.give_back(k, 0).start()
+
+        r.ret_o[self.e] = r.to[0]
+        r.ret_g[self.e] = r.tg[0]
+        if self.gated:
+            r.ret_gg[self.e] = r.tgg[0]
 
     def grad_to_core(self, i, j):
         r, w, came = self.r, (self.r.win, self.r.wdn)[i], (self.r.core_in, self.r.core_dn)[i]
@@ -263,43 +285,45 @@
             self.x_peer(j),
         )
 
-    def weight_grads(self, in_grad, dn_grad):
-        r, D, Fq = self.r, self.D, self.Fq
-        T = self.E * self.cap
-        tile = 256 if Fq % 256 == 0 else 128
-        r.xh_t[...] = r.xh[...].reshape(T, D).T
-
-        def grad(i, q, at):
-            if i == 0:
-                return dot(r.xh_t[at, :], r.gbef[q])
-            return dot_rows(r.act[q, :, at], r.xg[...].reshape(T, D))
-
-        for j in list(range(1, self.X)) + [0]:
-            for i, (w, size) in enumerate(((r.win, D), (r.wdn, Fq))):
-                @steps(size, tile)
+    def grad(self, i, q, at):
+        r, T = self.r, self.E * self.cap
+        if i == 0:
+            return dot(r.xh_t[at, :], r.gbef[q])
+        return dot_rows(r.act[q, :, at], r.xg[...].reshape(T, self.D))
+
+    def start_grads(self, j):
+        r = self.r
+        for i, (w, size) in enumerate(((r.win, self.D), (r.wdn, self.Fq))):
+            @steps(size, grad_rows(size))
+            def _(at):
+                w[j, at, :] = self.grad(i, self.part(j, 1 - self.c), at).astype(half)
+
+            self.grad_to_core(i, j).start()
+
+    def own_grads(self, j, store):
+        r = self.r
+        for i, (w, came, size) in enumerate(((r.win, r.core_in, self.D), (r.wdn, r.core_dn, self.Fq))):
+            self.grad_to_core(i, j).wait_recv()
+            if j:
+                @steps(size, grad_rows(size))
                 def _(at):
-                    w[j, at, :] = grad(i, self.part(j, 1 - self.c), at).astype(half)
-
-                self.grad_to_core(i, j).start()
-            for i, (w, came, size) in enumerate(((r.win, r.core_in, D), (r.wdn, r.core_dn, Fq))):
-                self.grad_to_core(i, j).wait_recv()
-
-                @steps(size, tile)
-                def _(at):
-                    total = grad(i, self.part(j, self.c), at) + came[j, at, :].astype(single)
-                    if j:
-                        w[self.X + j, at, :] = total.astype(half)
-                    else:
-                        (in_grad, dn_grad)[i][at, :] = total
-
-                if j:
-                    self.grad_to_x(i, j).start()
-
-    def wait_returns(self):
+                    total = self.grad(i, self.part(j, self.c), at) + came[j, at, :].astype(single)
+                    w[self.X + j, at, :] = total.astype(half)
+
+                self.grad_to_x(i, j).start()
+            else:
+                for first in range(0, size, grad_rows(size)):
+                    at = pl.ds(first, grad_rows(size))
+                    store(i, at, self.grad(i, self.part(j, self.c), at) + came[j, at, :].astype(single))
+
+    def turn_rows(self):
+        self.r.xh_t[...] = self.r.xh[...].reshape(self.E * self.cap, self.D).T
+
+    def wait_returns(self, *parts):
         @pl.loop(1, self.E)
         def _(k):
-            self.give_back(k, 0).wait_recv()
-            self.give_back(k, 1).wait_recv()
+            for part in parts:
+                self.give_back(k, part).wait_recv()
 
     def end(self):
         for i in range(2):
@@ -312,20 +336,27 @@
         def _(k):
             for part in range(3 if self.gated else 2):
                 self.dispatch(k, part).wait_send()
-                if part < 2:
-                    self.give_back(k, part).wait_send()
+                self.give_back(k, part).wait_send()
 
 
 def expert_kernel(E, X, G, names, *refs):
     r = Named(names, refs)
     experts = Experts(E, X, G, r, False)
     experts.greet()
+    experts.meet()
     experts.send_out(0, 1)
     experts.share_weights(r.w_in, r.w_dn)
     experts.run()
     experts.end_weights()
-    experts.weight_grads(r.in_grad, r.dn_grad)
-    experts.wait_returns()
+    experts.turn_rows()
+
+    def store(i, at, value):
+        (r.in_grad, r.dn_grad)[i][at, :] = value
+
+    for j in list(range(1, X)) + [0]:
+        experts.start_grads(j)
+        experts.own_grads(j, store)
+    experts.wait_returns(0, 1)
     experts.end()
 
 
@@ -461,7 +492,15 @@
     out[...] = dot(r.pick[...], rows).astype(half).reshape(out.shape)
 
 
-def backward_body(E, total_tokens, r, wts, small, counts):
+def set_output(r):
+    slots, D = r.place.shape[1], r.tokens.shape[1]
+    gate = jnp.sum(r.mine[...] * r.probs[...], axis=1, keepdims=True)
+    expert_tok = dot(r.place[...], r.ret_o[...].reshape(slots, D))
+    r.layer_out[...] = (r.resid[...] + gate * expert_tok).astype(half)
+    return jnp.sum(r.cotangent[...].astype(single) * expert_tok, axis=1, keepdims=True)
+
+
+def backward_body(E, total_tokens, r, wts, small, counts, grad_gate):
     T, D = r.tokens.shape
     slots = r.place.shape[1]
     small_t = small[...].astype(single).T
@@ -469,10 +508,6 @@
     lane = iota((T, LANES), 1)
     chance = r.probs[...]
     mine = r.mine[...]
-    gate = jnp.sum(mine * chance, axis=1, keepdims=True)
-    expert_tok = dot(r.place[...], r.ret_o[...].reshape(slots, D))
-    r.layer_out[...] = (r.resid[...] + gate * expert_tok).astype(half)
-    grad_gate = jnp.sum(cot * expert_tok, axis=1, keepdims=True)
     scale = counts * (balance_weight * E / total_tokens)
     grad_probs = mine * grad_gate + scale
     grad_logits = chance * (grad_probs - jnp.sum(chance * grad_probs, axis=1, keepdims=True))
@@ -612,10 +647,16 @@
         copy = remote(src, dst, self.sems.at[len(self.started)], recv_sem, device)
         copy.start()
         self.started.append(copy)
+        return len(self.started) - 1
+
+    def settle(self, n):
+        self.started[n].wait_send()
+        self.started[n] = None
 
     def finish(self):
         for copy in self.started:
-            copy.wait_send()
+            if copy is not None:
+                copy.wait_send()
 
 
 def arrive(dst, send_sem, recv_sem, device):
@@ -703,17 +744,20 @@
 
     def swap(self):
         r = self.r
-        self.sends.start(r.give.at[:, self.cols], r.got.at[:, self.cols], self.recv.at[0], self.at.core_peer())
+        self.swapped = self.sends.start(
+            r.give.at[:, self.cols], r.got.at[:, self.cols], self.recv.at[0], self.at.core_peer()
+        )
 
     def wait_swap(self):
+        self.sends.settle(self.swapped)
         there = self.r.got.at[:, self.cols]
         arrive(there, self.sends.sems.at[0], self.recv.at[0], self.at.core_peer())
 
-    def send(self, slot, value, device):
-        r = self.r
-        r.sent[slot, :, self.cols] = value.astype(half)
+    def send(self, slot, chip, value, device):
+        r, rows = self.r, self.rows_of(chip)
+        r.give[rows, self.cols] = value.astype(half)
         self.sends.start(
-            r.sent.at[slot, :, self.cols], r.came.at[slot, :, self.cols], self.recv.at[1 + slot], device
+            r.give.at[rows, self.cols], r.came.at[slot, :, self.cols], self.recv.at[1 + slot], device
         )
 
     def take(self, slot):
@@ -730,28 +774,28 @@
         for dz in at.z_steps() + [0]:
             for x in range(2):
                 chip = chip_index(at.z_at(dz), 1 - at.y, x)
-                self.send(dz * 2 + x, self.base(chip), at.y_peer())
-
-    def two(self):
+                self.send(dz * 2 + x, chip, self.base(chip), at.y_peer())
+
+    def two(self, dz):
         at = self.at
-        for dz in at.z_steps() + [0]:
-            for x in range(2):
-                chip = chip_index(at.z_at(dz), at.y, x)
-                value = self.base(chip) + self.take(dz * 2 + x)
-                if dz:
-                    self.send(2 * at.Z + dz * 2 + x, value, at.z_peer(dz))
-                else:
-                    self.r.acc[self.rows_of(chip), self.cols] = value
+        for x in range(2):
+            chip = chip_index(at.z_at(dz), at.y, x)
+            value = self.base(chip) + self.take(dz * 2 + x)
+            if dz:
+                self.send(2 * at.Z + dz * 2 + x, chip, value, at.z_peer(dz))
+            else:
+                self.r.acc[self.rows_of(chip), self.cols] = value
 
     def three(self):
         at = self.at
         for flip in (1, 0):
             x = 1 - at.x if flip else at.x
-            value = self.r.acc[self.rows_of(chip_index(at.z, at.y, x)), self.cols]
+            chip = chip_index(at.z, at.y, x)
+            value = self.r.acc[self.rows_of(chip), self.cols]
             for dz in range(1, at.Z):
                 value = value + self.take(2 * at.Z + dz * 2 + x)
             if flip:
-                self.send(4 * at.Z, value, at.x_peer())
+                self.send(4 * at.Z, chip, value, at.x_peer())
             else:
                 self.r.final[:, self.cols] = value
 
@@ -802,7 +846,7 @@
     D = r.tokens.shape[1]
     set_places(E, r.ret_o.shape[1], r)
     transposes(r)
-    mid_gain, mid_shift = backward_body(E, total_tokens, r, r.wts, r.small, r.counts[0:1])
+    mid_gain, mid_shift = backward_body(E, total_tokens, r, r.wts, r.small, r.counts[0:1], set_output(r))
     first_cols, last_cols = columns_of(D)
     for part in range(2):
         attend_back(r, part)
@@ -826,9 +870,9 @@
     def __init__(self, at, sends, r, rows):
         self.at, self.sends, self.r, self.rows = at, sends, r, rows
 
-    def rows_of(self, z, y, x):
+    def here(self, z, y, x):
         first = chip_index(z, y, x) * 2 * self.rows + self.at.c * self.rows
-        return pl.ds(pl.multiple_of(first, self.rows), self.rows)
+        return self.r.pack_other[pl.ds(pl.multiple_of(first, self.rows), self.rows), :]
 
     def send(self, slot, value, device):
         r = self.r
@@ -849,33 +893,29 @@
         arrive(r.pack_other, r.send.at[0], r.pack_recv.at[0], at.core_peer())
         r.pack_other[...] += r.pack[...]
         for dz in range(at.Z):
-            for y in range(2):
-                self.send(dz * 2 + y, r.pack_other[self.rows_of(at.z_at(dz), y, 1 - at.x), :], at.x_peer())
+            for x in range(2):
+                self.send(dz * 2 + x, self.here(at.z_at(dz), 1 - at.y, x), at.y_peer())
 
     def two(self):
-        r, at = self.r, self.at
-        for dz in range(at.Z):
-            for flip in (1, 0):
-                y = 1 - at.y if flip else at.y
-                here = self.rows_of(at.z_at(dz), y, at.x)
-                value = r.pack_other[here, :] + self.take(dz * 2 + y)
-                if flip:
-                    self.send(2 * at.Z + dz, value, at.y_peer())
-                else:
-                    r.pack_other[here, :] = value
+        at = self.at
+        for dz in at.z_steps():
+            for x in range(2):
+                value = self.here(at.z_at(dz), at.y, x) + self.take(dz * 2 + x)
+                self.send(2 * at.Z + dz * 2 + x, value, at.z_peer(dz))
 
     def three(self):
-        r, at = self.r, self.at
-        for dz in at.z_steps() + [0]:
-            value = r.pack_other[self.rows_of(at.z_at(dz), at.y, at.x), :] + self.take(2 * at.Z + dz)
-            if dz:
-                self.send(3 * at.Z + dz, value, at.z_peer(dz))
+        at = self.at
+        for flip in (1, 0):
+            x = 1 - at.x if flip else at.x
+            value = self.here(at.z, at.y, x) + self.take(x)
+            for dz in range(1, at.Z):
+                value = value + self.take(2 * at.Z + dz * 2 + x)
+            if flip:
+                self.send(4 * at.Z, value, at.x_peer())
         return value
 
     def four(self, total):
-        for dz in range(1, self.at.Z):
-            total = total + self.take(3 * self.at.Z + dz)
-        return total
+        return total + self.take(4 * self.at.Z)
 
 
 def whole_scratch(E, T, D, cap, rows):
@@ -893,13 +933,13 @@
         out_h=pltpu.VMEM(token, half), out_g=pltpu.VMEM(token, half),
         ret_o=pltpu.VMEM(token, half), ret_g=pltpu.VMEM(token, half),
         acc=pltpu.VMEM((D, 2 * D), single), give=pltpu.VMEM((D, 2 * D), half), got=pltpu.VMEM((D, 2 * D), half),
-        sent=pltpu.VMEM((slots, 2 * rows, 2 * D), half), came=pltpu.VMEM((slots, 2 * rows, 2 * D), half),
+        came=pltpu.VMEM((slots, 2 * rows, 2 * D), half),
         final=pltpu.VMEM((2 * rows, 2 * D), single), final_other=pltpu.VMEM((rows, 2 * D), single),
         pack=pltpu.VMEM((D, LANES), single), pack_other=pltpu.VMEM((D, LANES), single),
-        pack_sent=pltpu.VMEM((4 * Z, rows, LANES), single),
-        pack_came=pltpu.VMEM((4 * Z, rows, LANES), single),
-        local=DMA((4,)), send=DMA((40 * Z + 16,)), gather_recv=DMA((2, 3, 4 * Z)), own_recv=DMA((2,)),
-        sum_recv=DMA((2, slots + 2)), pack_recv=DMA((4 * Z + 1,)),
+        pack_sent=pltpu.VMEM((slots, rows, LANES), single),
+        pack_came=pltpu.VMEM((slots, rows, LANES), single),
+        reads=DMA((10,)), writes=DMA((5,)), local=DMA((4,)), send=DMA((40 * Z + 16,)), gather_recv=DMA((2, 3, 4 * Z)), own_recv=DMA((2,)),
+        sum_recv=DMA((2, slots + 2)), pack_recv=DMA((slots + 1,)),
     )
 
 
@@ -908,8 +948,17 @@
     rows, D = r.proj_shard.shape
     T = r.tokens.shape[0]
     cap = r.out_h.shape[1]
+    pairs = [
+        (r.x_qkv, r.qkv_shard), (r.x_proj, r.proj_shard), (r.x_assign, r.assign), (r.x_router, r.router),
+        (r.x_pre_gain, r.pre_gain), (r.x_pre_shift, r.pre_shift), (r.x_mid_gain, r.mid_gain),
+        (r.x_mid_shift, r.mid_shift), (r.x_tokens, r.tokens), (r.x_cotangent, r.cotangent),
+    ]
+    reads = [pltpu.make_async_copy(src, there, r.reads.at[i]) for i, (src, there) in enumerate(pairs)]
     at = Place(E)
     experts = Experts(E, 2, G, r, True)
+    experts.greet()
+    for read in reads:
+        read.start()
     sends = Sends(r.send)
     width = D // 2
     first_cols, last_cols = columns_of(D)
@@ -920,13 +969,17 @@
     ]
     for load in loads:
         load.start()
+    r.square[...] = jnp.zeros_like(r.square)
+    for read in reads[:2]:
+        read.wait()
     for part in range(2):
         for m in range(3):
             first = m * D + part * width
             r.shard[part, :, m * width : (m + 1) * width] = r.qkv_shard[:, first : first + width]
         r.shard[part, :, 3 * width :] = r.proj_shard[:, part * width : (part + 1) * width]
+    for read in reads[2:8]:
+        read.wait()
     assign = r.assign[...].astype(single)
-    r.square[...] = jnp.zeros_like(r.square)
     r.square[0:E, 0:rows] = r.router[...]
     for i, gain in enumerate((r.pre_gain, r.pre_shift, r.mid_gain, r.mid_shift)):
         r.square[E + i : E + i + 1, 0:rows] = gain[...]
@@ -935,7 +988,7 @@
     lane = iota((rows, LANES), 1)
     r.small_shard[...] = jnp.where(lane == E + 4, count, r.square[...].T[0:rows, :])
 
-    experts.greet()
+    experts.meet()
     core = at.core_peer()
     sends.start(r.shard.at[1 - at.c], r.other, r.own_recv.at[0], core)
     sends.start(r.small_shard, r.other_small, r.own_recv.at[1], core)
@@ -962,6 +1015,8 @@
     gather.second(2)
     gather.third(0)
     gather.third(2)
+    for read in reads[8:]:
+        read.wait()
     set_places(E, cap, r)
     to_slots(r, r.cotangent[...], r.out_g)
     gather.own(1)
@@ -989,19 +1044,15 @@
     experts.send_out(2, 0)
     experts.run()
     experts.end_weights()
-    experts.weight_grads(*through)
-    stores = [
-        pltpu.make_async_copy(there, w.at[0], r.local.at[2 + i])
-        for i, (w, there) in enumerate(zip((r.in_own, r.dn_own), through))
-    ]
-    for store in stores:
-        store.start()
+    experts.turn_rows()
+    experts.start_grads(1)
+    experts.own_grads(1, None)
     transposes(r)
-    experts.wait_returns()
-
-    mid_gain, mid_shift = backward_body(E, total_tokens, r, r.wts, r.small, r.counts[0:1])
-    for store in stores:
-        store.wait()
+    experts.wait_returns(1, 2)
+
+    grad_gate = sum(r.ret_gg[i, 0:1, :] for i in range(E))
+    grad_gate = jnp.sum(r.place[...].astype(single) * grad_gate, axis=1, keepdims=True)
+    mid_gain, mid_shift = backward_body(E, total_tokens, r, r.wts, r.small, r.counts[0:1], grad_gate)
     first = SumScatter(at, sends, first_cols, r, r.sum_recv.at[0])
     last = SumScatter(at, sends, last_cols, r, r.sum_recv.at[1])
     smalls = SmallSum(at, sends, r, rows)
@@ -1030,19 +1081,53 @@
     qkv_weight_grad(r, at.c, keep_first)
     first.wait_swap()
     first.one()
-    last.two()
+    for dz in at.z_steps() + [0]:
+        last.two(dz)
     pre_gain, pre_shift = input_body(E, r, r.wts, r.small)
     chance_sum = jnp.sum(r.probs[...], axis=0, keepdims=True)
     r.pack[...] = small_grads(
         E, r.router_sum[...], (pre_gain, pre_shift, mid_gain, mid_shift), chance_sum, rows, D
     )
     smalls.zero()
+    steps_z = at.z_steps()
+    first.two(steps_z[0])
+    experts.wait_returns(0)
+    set_output(r)
+    smalls.one()
+    writes = [
+        pltpu.make_async_copy(there, dst, r.writes.at[i])
+        for i, (there, dst) in enumerate((
+            (r.input_grad, r.y_input_grad), (r.layer_out, r.y_layer_out), (r.small_out, r.y_small_out),
+            (r.qkv_grad, r.y_qkv_grad), (r.proj_grad, r.y_proj_grad),
+        ))
+    ]
+    for write in writes[:2]:
+        write.start()
+    if len(steps_z) > 1:
+        first.two(steps_z[1])
+    pieces = r.resid, r.grad_res
+    leaving = []
+
+    def store(i, rows_at, value):
+        n = len(leaving) % 2
+        if len(leaving) > 1:
+            leaving[-2].wait()
+        pieces[n][0 : rows_at.size, :] = value
+        copy = pltpu.make_async_copy(
+            pieces[n].at[0 : rows_at.size], (r.in_own, r.dn_own)[i].at[0, rows_at, :], r.local.at[2 + n]
+        )
+        copy.start()
+        leaving.append(copy)
+
+    experts.start_grads(0)
+    for dz in steps_z[2:]:
+        first.two(dz)
+    smalls.two()
+    experts.own_grads(0, store)
+    first.two(0)
     last.three()
-    first.two()
-    smalls.one()
+    first.three()
     last.four()
-    smalls.two()
-    first.three()
     total = smalls.three()
     first.four()
     total = smalls.four(total)
@@ -1052,6 +1137,7 @@
     loss = jnp.sum(jnp.sum(chosen, axis=1, keepdims=True), axis=0, keepdims=True) / total_tokens
     r.square[0:rows, :] = jnp.where(lane == E + 5, loss, total)
     r.small_out[...] = r.square[...].T[0 : r.small_out.shape[0], :]
+    writes[2].start()
     last.end()
     first.end()
     half_rows = pl.ds(pl.multiple_of(at.c * rows, rows), rows)
@@ -1061,8 +1147,12 @@
             begin = m * D + part * width
             r.qkv_grad[:, begin : begin + width] = value[:, m * width : (m + 1) * width]
         r.proj_grad[:, part * width : (part + 1) * width] = value[:, 3 * width :]
+    for write in writes[3:]:
+        write.start()
     experts.end()
     sends.finish()
+    for write in writes + leaving[-2:]:
+        write.wait()
 
 
 def out_kernel(E, names, *refs):
@@ -1080,10 +1170,22 @@
     for load in loads:
         load.start()
     rows = r.proj_in.shape[0]
-    r.router[...] = r.small_in[0:E, 0:rows]
-    for i, gain in enumerate((r.pre_gain, r.pre_shift, r.mid_gain, r.mid_shift)):
-        gain[...] = r.small_in[E + i : E + i + 1, 0:rows]
-    r.loss[...] = r.small_in[E + 5 : E + 6, 0:1]
+    small_load = pltpu.make_async_copy(r.small_in, r.h8, r.sems.at[0, 8])
+    small_load.start()
+    small_load.wait()
+    r.s_router[...] = r.h8[0:E, 0:rows]
+    for i, gain in enumerate((r.s_pre_gain, r.s_pre_shift, r.s_mid_gain, r.s_mid_shift)):
+        gain[...] = r.h8[E + i : E + i + 1, 0:rows]
+    r.s_loss[...] = r.h8[E + 5 : E + 6, 0:1]
+    small_outs = [
+        (r.s_router, r.router), (r.s_pre_gain, r.pre_gain), (r.s_pre_shift, r.pre_shift),
+        (r.s_mid_gain, r.mid_gain), (r.s_mid_shift, r.mid_shift), (r.s_loss, r.loss),
+    ]
+    small_stores = [
+        pltpu.make_async_copy(there, dst, r.sems.at[2, i]) for i, (there, dst) in enumerate(small_outs)
+    ]
+    for store in small_stores:
+        store.start()
     for i, (own, came) in enumerate(((r.h0, r.h1), (r.h2, r.h3))):
         loads[2 * i].wait()
         loads[2 * i + 1].wait()
@@ -1096,7 +1198,7 @@
     for load, store in zip(loads[4:], stores[2:]):
         load.wait()
         store.start()
-    for store in stores:
+    for store in stores + small_stores:
         store.wait()
 
 
@@ -1118,50 +1220,62 @@
     token = ((T, D), half)
     slot = ((E, cap, D), half)
     vectors = dict(pre_gain=pre_gain, pre_shift=pre_shift, mid_gain=mid_gain, mid_shift=mid_shift)
-    if X == 2 and E % 2 == 0 and rows % 8 == 0 and E <= rows <= LANES and Fq == D and D % 256 == 0:
+    if X == 2 and E % 2 == 0 and rows % 8 == 0 and E <= rows <= LANES and Fq == D and D % 256 == 0 and T >= 256:
         small_rows = E + 8
         found = call(
             functools.partial(whole_kernel, E, total_tokens, G),
             dict(
-                tokens=tokens_in, cotangent=out_cotangent, assign=assign,
-                qkv_shard=qkv_weight, proj_shard=proj_weight, router=router_weight.T,
-                **dict((name, value.reshape(1, rows)) for name, value in vectors.items()),
+                x_tokens=(tokens_in, ANY_SPEC), x_cotangent=(out_cotangent, ANY_SPEC), x_assign=(assign, ANY_SPEC),
+                x_qkv=(qkv_weight, ANY_SPEC), x_proj=(proj_weight, ANY_SPEC), x_router=(router_weight.T, ANY_SPEC),
+                x_pre_gain=(pre_gain.reshape(1, rows), ANY_SPEC), x_pre_shift=(pre_shift.reshape(1, rows), ANY_SPEC),
+                x_mid_gain=(mid_gain.reshape(1, rows), ANY_SPEC), x_mid_shift=(mid_shift.reshape(1, rows), ANY_SPEC),
                 w_in=(expert_in, ANY_SPEC), w_dn=(expert_down, ANY_SPEC),
             ),
             dict(
-                layer_out=token, input_grad=token, qkv_grad=((rows, 3 * D), single),
-                proj_grad=((rows, D), single), small_out=((small_rows, LANES), single),
+                y_layer_out=token + (ANY_SPEC,), y_input_grad=token + (ANY_SPEC,),
+                y_qkv_grad=((rows, 3 * D), single, ANY_SPEC), y_proj_grad=((rows, D), single, ANY_SPEC),
+                y_small_out=((small_rows, LANES), single, ANY_SPEC),
                 in_own=((1, D, Fq), single, ANY_SPEC), dn_own=((1, Fq, D), single, ANY_SPEC),
                 in_came=((X - 1, D, Fq), half, ANY_SPEC), dn_came=((X - 1, Fq, D), half, ANY_SPEC),
             ),
             dict(
+                tokens=pltpu.VMEM(*token), cotangent=pltpu.VMEM(*token), assign=pltpu.VMEM((1, T), jnp.int32),
+                qkv_shard=pltpu.VMEM((rows, 3 * D), single), proj_shard=pltpu.VMEM((rows, D), single),
+                router=pltpu.VMEM((E, rows), single), pre_gain=pltpu.VMEM((1, rows), single),
+                pre_shift=pltpu.VMEM((1, rows), single), mid_gain=pltpu.VMEM((1, rows), single),
+                mid_shift=pltpu.VMEM((1, rows), single), layer_out=pltpu.VMEM(*token), input_grad=pltpu.VMEM(*token),
+                qkv_grad=pltpu.VMEM((rows, 3 * D), single), proj_grad=pltpu.VMEM((rows, D), single),
+                small_out=pltpu.VMEM((small_rows, LANES), single),
                 **whole_scratch(E, T, D, cap, rows), **model_scratch(E, T, D, cap), **end_scratch(T, D),
                 **expert_scratch(E, X, cap, D, Fq),
             ),
             1, "layer",
         )
         layer_out, input_grad, qkv_grad, proj_grad, small_out, in_own, dn_own, in_came, dn_came = found
-        vector = ((1, rows), single)
+        vector = ((1, rows), single, ANY_SPEC)
         found = call(
             functools.partial(out_kernel, E),
             dict(
                 layer_in=(layer_out, ANY_SPEC), input_in=(input_grad, ANY_SPEC),
                 qkv_in=(qkv_grad, ANY_SPEC), proj_in=(proj_grad, ANY_SPEC),
                 in_own=(in_own, ANY_SPEC), dn_own=(dn_own, ANY_SPEC),
-                in_came=(in_came, ANY_SPEC), dn_came=(dn_came, ANY_SPEC), small_in=small_out,
+                in_came=(in_came, ANY_SPEC), dn_came=(dn_came, ANY_SPEC), small_in=(small_out, ANY_SPEC),
             ),
             dict(
                 layer_out=token + (ANY_SPEC,), input_grad=token + (ANY_SPEC,),
                 qkv_grad=((rows, 3 * D), single, ANY_SPEC), proj_grad=((rows, D), single, ANY_SPEC),
                 in_grad=((1, D, Fq), single, ANY_SPEC), dn_grad=((1, Fq, D), single, ANY_SPEC),
-                router=((E, rows), single), pre_gain=vector, pre_shift=vector, mid_gain=vector,
-                mid_shift=vector, loss=((1, 1), single),
+                router=((E, rows), single, ANY_SPEC), pre_gain=vector, pre_shift=vector, mid_gain=vector,
+                mid_shift=vector, loss=((1, 1), single, ANY_SPEC),
             ),
             dict(
                 h0=pltpu.VMEM((1, D, Fq), single), h1=pltpu.VMEM((X - 1, D, Fq), half),
                 h2=pltpu.VMEM((1, Fq, D), single), h3=pltpu.VMEM((X - 1, Fq, D), half),
                 h4=pltpu.VMEM(*token), h5=pltpu.VMEM(*token), h6=pltpu.VMEM((rows, 3 * D), single),
-                h7=pltpu.VMEM((rows, D), single), sems=DMA((2, 8)),
+                h7=pltpu.VMEM((rows, D), single), h8=pltpu.VMEM((small_rows, LANES), single),
+                s_router=pltpu.VMEM((E, rows), single), s_pre_gain=pltpu.VMEM((1, rows), single),
+                s_pre_shift=pltpu.VMEM((1, rows), single), s_mid_gain=pltpu.VMEM((1, rows), single),
+                s_mid_shift=pltpu.VMEM((1, rows), single), s_loss=pltpu.VMEM((1, 1), single), sems=DMA((3, 9)),
             ),
             None, "results",
         )

time: 178 us -> 170 us (0.955)
  Pallas kernels: 177 us -> 168 us
    pallas_call x2, Pallas kernels: 177 us -> 168 us  [call(): pl.pallas_call(functools.partial(kernel, names), out_shape=tuple((jax.Sha...]
where the time goes in v4:
time: 170 us; the launch traced here: 168 us
  Pallas kernels  168 us (99%)
    pallas_call x2, Pallas kernels, call(): pl.pallas_call(functools.partial(kernel, names), out_shape=tuple((jax.Sha...  168 us

profile of v4, /device:TPU:0, one launch (start us, length us, event | category | flops | bytes accessed | tf_op | source)
XLA Modules:
  0.0 168.5 jit_solution(13384688357034175213)
XLA Ops:
  0.6 161.5 %layer.1 = (bf16[256,768]{1,0:T(8,128)(2,1)}, bf16[256,768]{1,0:T(8,128)(2,1)}, f32[24,2304]{1,0:T(8,128)}, f32[24,768]{1,0:T(8,128)}, f32[16,128]{1,0:T(8,128)}...) custom-call(bf16[256,768]{1,0:T(8,128)(2,1)} %refs_0_.1, ...), custom_call_target="tpu_custom_call" | custom-call | tf_op jit(solution)/shard_map/layer/pallas_call | solution.py:371
  162.2 6.1 %results.1 = (bf16[256,768]{1,0:T(8,128)(2,1)}, bf16[256,768]{1,0:T(8,128)(2,1)}, f32[24,2304]{1,0:T(8,128)}, f32[24,768]{1,0:T(8,128)}, f32[1,768,768]{2,1,0:T(...) custom-call(bf16[256,768]{1,0:T(8,128)(2,1)} %get-tuple-element.33.r, ...), custom_call_target="tpu_custom_call" | custom-call | tf_op jit(solution)/shard_map/results/pallas_call | solution.py:371

commit v5 on v4

--- a/solution.py
+++ b/solution.py
@@ -265,14 +265,15 @@
                     for part in parts:
                         self.give_back(k, part).start()
 
-        @pl.loop(1, self.E)
-        def _(k):
-            self.give_back(k, 0).start()
-
         r.ret_o[self.e] = r.to[0]
         r.ret_g[self.e] = r.tg[0]
         if self.gated:
             r.ret_gg[self.e] = r.tgg[0]
+
+    def send_outputs(self):
+        @pl.loop(1, self.E)
+        def _(k):
+            self.give_back(k, 0).start()
 
     def grad_to_core(self, i, j):
         r, w, came = self.r, (self.r.win, self.r.wdn)[i], (self.r.core_in, self.r.core_dn)[i]
@@ -347,6 +348,7 @@
     experts.send_out(0, 1)
     experts.share_weights(r.w_in, r.w_dn)
     experts.run()
+    experts.send_outputs()
     experts.end_weights()
     experts.turn_rows()
 
@@ -439,7 +441,7 @@
 
 
 def pair_columns(D, m, p):
-    return pl.ds(pl.multiple_of(m * (D // 2) + p * LANES, LANES), LANES)
+    return pl.ds(pl.multiple_of((3 * p + m) * LANES, LANES), LANES)
 
 
 def attend(E, r, wts, small, between=lambda: None, then=lambda: None):
@@ -525,30 +527,27 @@
     return mid_gain, mid_shift
 
 
-def attend_back(r, part):
+def attend_back(r, part, p):
     T, D = r.tokens.shape
     allowed = iota((T, T), 1) <= iota((T, T), 0)
     first, masks = head_masks(T)
-
-    @pl.loop(0, D // LANES // 2)
-    def _(p):
-        q_pair, k_pair, v_pair = (r.qkv[part, :, pair_columns(D, m, p)] for m in range(3))
-        g_pair = r.gatt[:, pl.ds(pl.multiple_of(part * (D // 2) + p * LANES, LANES), LANES)]
-        found = []
-        for mask in masks:
-            weights = head_probs(q_pair * mask, k_pair, allowed)
-            grad_w = dot_cols(g_pair * mask, v_pair)
-            grad_s = weights * (grad_w - jnp.sum(weights * grad_w, axis=-1, keepdims=True))
-            grad_s = grad_s.astype(half)
-            found.append(
-                (
-                    dot(grad_s, k_pair) * (HEAD_DIM ** -0.5),
-                    dot_rows(grad_s, q_pair) * (HEAD_DIM ** -0.5),
-                    dot_rows(weights.astype(half), g_pair),
-                )
+    q_pair, k_pair, v_pair = (r.qkv[part, :, pair_columns(D, m, p)] for m in range(3))
+    g_pair = r.gatt[:, pl.ds(pl.multiple_of(part * (D // 2) + p * LANES, LANES), LANES)]
+    found = []
+    for mask in masks:
+        weights = head_probs(q_pair * mask, k_pair, allowed)
+        grad_w = dot_cols(g_pair * mask, v_pair)
+        grad_s = weights * (grad_w - jnp.sum(weights * grad_w, axis=-1, keepdims=True))
+        grad_s = grad_s.astype(half)
+        found.append(
+            (
+                dot(grad_s, k_pair) * (HEAD_DIM ** -0.5),
+                dot_rows(grad_s, q_pair) * (HEAD_DIM ** -0.5),
+                dot_rows(weights.astype(half), g_pair),
             )
-        for m in range(3):
-            r.gqkv[part, :, pair_columns(D, m, p)] = jnp.where(first, found[0][m], found[1][m]).astype(half)
+        )
+    for m in range(3):
+        r.gqkv[part, :, pair_columns(D, m, p)] = jnp.where(first, found[0][m], found[1][m]).astype(half)
 
 
 def transposes(r):
@@ -556,12 +555,13 @@
     r.att_t[...] = r.att[...].T
 
 
-def qkv_weight_grad(r, part, write):
+def qkv_weight_grad(r, part, p, write):
     D = r.hid_a_t.shape[0]
+    cols = pl.ds(3 * LANES * p, 3 * LANES)
 
     @steps(D, 256 if D % 256 == 0 else LANES)
     def _(rows):
-        write(rows, dot(r.hid_a_t[rows, :], r.gqkv[part]))
+        write(rows, cols, dot(r.hid_a_t[rows, :], r.gqkv[part, :, cols]))
 
 
 def proj_weight_grad(r, part, write):
@@ -847,17 +847,17 @@
     set_places(E, r.ret_o.shape[1], r)
     transposes(r)
     mid_gain, mid_shift = backward_body(E, total_tokens, r, r.wts, r.small, r.counts[0:1], set_output(r))
-    first_cols, last_cols = columns_of(D)
+    _, last_cols = columns_of(D)
     for part in range(2):
-        attend_back(r, part)
-
-        def write_first(rows, value):
-            r.weight_grads[part, rows, first_cols] = value
+        def write_first(rows, cols, value):
+            r.weight_grads[part, rows, cols] = value
 
         def write_last(rows, value):
             r.weight_grads[part, rows, last_cols] = value
 
-        qkv_weight_grad(r, part, write_first)
+        for p in range(D // LANES // 2):
+            attend_back(r, part, p)
+            qkv_weight_grad(r, part, p, write_first)
         proj_weight_grad(r, part, write_last)
     pre_gain, pre_shift = input_body(E, r, r.wts, r.small)
     chance_sum = jnp.sum(r.probs[...], axis=0, keepdims=True)
@@ -938,8 +938,8 @@
         pack=pltpu.VMEM((D, LANES), single), pack_other=pltpu.VMEM((D, LANES), single),
         pack_sent=pltpu.VMEM((slots, rows, LANES), single),
         pack_came=pltpu.VMEM((slots, rows, LANES), single),
-        reads=DMA((10,)), writes=DMA((5,)), local=DMA((4,)), send=DMA((40 * Z + 16,)), gather_recv=DMA((2, 3, 4 * Z)), own_recv=DMA((2,)),
-        sum_recv=DMA((2, slots + 2)), pack_recv=DMA((slots + 1,)),
+        reads=DMA((10,)), writes=DMA((5,)), local=DMA((4,)), send=DMA((60 * Z + 32,)), gather_recv=DMA((2, 3, 4 * Z)), own_recv=DMA((2,)),
+        sum_recv=DMA((D // LANES // 2 + 1, slots + 2)), pack_recv=DMA((slots + 1,)),
     )
 
 
@@ -961,6 +961,7 @@
         read.start()
     sends = Sends(r.send)
     width = D // 2
+    pairs_here = width // LANES
     first_cols, last_cols = columns_of(D)
     through = r.acc.at[:, 0:D], r.acc.at[:, D : 2 * D]
     loads = [
@@ -973,9 +974,10 @@
     for read in reads[:2]:
         read.wait()
     for part in range(2):
-        for m in range(3):
-            first = m * D + part * width
-            r.shard[part, :, m * width : (m + 1) * width] = r.qkv_shard[:, first : first + width]
+        for p in range(pairs_here):
+            for m in range(3):
+                first, to = m * D + part * width + p * LANES, (3 * p + m) * LANES
+                r.shard[part, :, to : to + LANES] = r.qkv_shard[:, first : first + LANES]
         r.shard[part, :, 3 * width :] = r.proj_shard[:, part * width : (part + 1) * width]
     for read in reads[2:8]:
         read.wait()
@@ -1049,12 +1051,15 @@
     experts.own_grads(1, None)
     transposes(r)
     experts.wait_returns(1, 2)
+    experts.send_outputs()
 
     grad_gate = sum(r.ret_gg[i, 0:1, :] for i in range(E))
     grad_gate = jnp.sum(r.place[...].astype(single) * grad_gate, axis=1, keepdims=True)
     mid_gain, mid_shift = backward_body(E, total_tokens, r, r.wts, r.small, r.counts[0:1], grad_gate)
-    first = SumScatter(at, sends, first_cols, r, r.sum_recv.at[0])
-    last = SumScatter(at, sends, last_cols, r, r.sum_recv.at[1])
+    last = SumScatter(at, sends, last_cols, r, r.sum_recv.at[pairs_here])
+    firsts = [
+        SumScatter(at, sends, pl.ds(3 * LANES * p, 3 * LANES), r, r.sum_recv.at[p]) for p in range(pairs_here)
+    ]
     smalls = SmallSum(at, sends, r, rows)
 
     def give_last(here, value):
@@ -1063,25 +1068,28 @@
     def keep_last(here, value):
         r.acc[here, last_cols] = value
 
-    def give_first(here, value):
-        r.give[here, first_cols] = value.astype(half)
-
-    def keep_first(here, value):
-        r.acc[here, first_cols] = value
+    def give_first(here, cols, value):
+        r.give[here, cols] = value.astype(half)
+
+    def keep_first(here, cols, value):
+        r.acc[here, cols] = value
 
     proj_weight_grad(r, 1 - at.c, give_last)
     last.swap()
     proj_weight_grad(r, at.c, keep_last)
-    attend_back(r, 1 - at.c)
-    qkv_weight_grad(r, 1 - at.c, give_first)
-    first.swap()
-    last.wait_swap()
-    last.one()
-    attend_back(r, at.c)
-    qkv_weight_grad(r, at.c, keep_first)
-    first.wait_swap()
-    first.one()
-    for dz in at.z_steps() + [0]:
+    for p, first in enumerate(firsts):
+        attend_back(r, 1 - at.c, p)
+        qkv_weight_grad(r, 1 - at.c, p, give_first)
+        first.swap()
+        if p == 0:
+            last.wait_swap()
+            last.one()
+        attend_back(r, at.c, p)
+        qkv_weight_grad(r, at.c, p, keep_first)
+        first.wait_swap()
+        first.one()
+    steps_z = at.z_steps() + [0]
+    for dz in steps_z:
         last.two(dz)
     pre_gain, pre_shift = input_body(E, r, r.wts, r.small)
     chance_sum = jnp.sum(r.probs[...], axis=0, keepdims=True)
@@ -1089,8 +1097,8 @@
         E, r.router_sum[...], (pre_gain, pre_shift, mid_gain, mid_shift), chance_sum, rows, D
     )
     smalls.zero()
-    steps_z = at.z_steps()
-    first.two(steps_z[0])
+    for dz in steps_z:
+        firsts[0].two(dz)
     experts.wait_returns(0)
     set_output(r)
     smalls.one()
@@ -1103,8 +1111,9 @@
     ]
     for write in writes[:2]:
         write.start()
-    if len(steps_z) > 1:
-        first.two(steps_z[1])
+    for first in firsts[1:-1]:
+        for dz in steps_z:
+            first.two(dz)
     pieces = r.resid, r.grad_res
     leaving = []
 
@@ -1120,16 +1129,17 @@
         leaving.append(copy)
 
     experts.start_grads(0)
-    for dz in steps_z[2:]:
-        first.two(dz)
+    for dz in steps_z if len(firsts) > 1 else ():
+        firsts[-1].two(dz)
     smalls.two()
     experts.own_grads(0, store)
-    first.two(0)
     last.three()
-    first.three()
+    for first in firsts:
+        first.three()
     last.four()
     total = smalls.three()
-    first.four()
+    for first in firsts:
+        first.four()
     total = smalls.four(total)
     scale = r.counts[0:1] * (balance_weight * E / total_tokens)
     chance = jnp.sum(jnp.where(lane == E + 4, total, 0.0), axis=1, keepdims=True)
@@ -1139,13 +1149,15 @@
     r.small_out[...] = r.square[...].T[0 : r.small_out.shape[0], :]
     writes[2].start()
     last.end()
-    first.end()
+    for first in firsts:
+        first.end()
     half_rows = pl.ds(pl.multiple_of(at.c * rows, rows), rows)
     mine, theirs = r.final[half_rows, :], r.final_other[...]
     for part, value in enumerate((jnp.where(at.c == 0, mine, theirs), jnp.where(at.c == 0, theirs, mine))):
-        for m in range(3):
-            begin = m * D + part * width
-            r.qkv_grad[:, begin : begin + width] = value[:, m * width : (m + 1) * width]
+        for p in range(pairs_here):
+            for m in range(3):
+                begin, come = m * D + part * width + p * LANES, (3 * p + m) * LANES
+                r.qkv_grad[:, begin : begin + LANES] = value[:, come : come + LANES]
         r.proj_grad[:, part * width : (part + 1) * width] = value[:, 3 * width :]
     for write in writes[3:]:
         write.start()
@@ -1163,11 +1175,10 @@
     ]
     loads = [pltpu.make_async_copy(src, there, r.sems.at[0, i]) for i, (src, there) in enumerate(pairs)]
     outs = [
-        (r.h0, r.in_grad), (r.h2, r.dn_grad), (r.h4, r.layer_out), (r.h5, r.input_grad), (r.h6, r.qkv_grad),
-        (r.h7, r.proj_grad),
+        (r.h4, r.layer_out), (r.h5, r.input_grad), (r.h6, r.qkv_grad), (r.h7, r.proj_grad),
     ]
     stores = [pltpu.make_async_copy(there, dst, r.sems.at[1, i]) for i, (there, dst) in enumerate(outs)]
-    for load in loads:
+    for load in loads[4:] + loads[:4]:
         load.start()
     rows = r.proj_in.shape[0]
     small_load = pltpu.make_async_copy(r.small_in, r.h8, r.sems.at[0, 8])
@@ -1186,18 +1197,19 @@
     ]
     for store in small_stores:
         store.start()
-    for i, (own, came) in enumerate(((r.h0, r.h1), (r.h2, r.h3))):
+    for load, store in zip(loads[4:], stores):
+        load.wait()
+        store.start()
+    for i, (own, came, dst) in enumerate(((r.h0, r.h1, r.in_grad), (r.h2, r.h3, r.dn_grad))):
         loads[2 * i].wait()
         loads[2 * i + 1].wait()
-
-        @steps(own.shape[1], STEP)
-        def _(at):
+        size = own.shape[1] // 4
+        for piece in range(4):
+            at = pl.ds(piece * size, size)
             own[0, at, :] += sum(came[j, at, :].astype(single) for j in range(came.shape[0]))
-
-        stores[i].start()
-    for load, store in zip(loads[4:], stores[2:]):
-        load.wait()
-        store.start()
+            store = pltpu.make_async_copy(own.at[0, at, :], dst.at[0, at, :], r.sems.at[1, 4 + 4 * i + piece])
+            store.start()
+            stores.append(store)
     for store in stores + small_stores:
         store.wait()
 
@@ -1275,7 +1287,7 @@
                 h7=pltpu.VMEM((rows, D), single), h8=pltpu.VMEM((small_rows, LANES), single),
                 s_router=pltpu.VMEM((E, rows), single), s_pre_gain=pltpu.VMEM((1, rows), single),
                 s_pre_shift=pltpu.VMEM((1, rows), single), s_mid_gain=pltpu.VMEM((1, rows), single),
-                s_mid_shift=pltpu.VMEM((1, rows), single), s_loss=pltpu.VMEM((1, 1), single), sems=DMA((3, 9)),
+                s_mid_shift=pltpu.VMEM((1, rows), single), s_loss=pltpu.VMEM((1, 1), single), sems=DMA((3, 12)),
             ),
             None, "results",
         )
@@ -1288,8 +1300,14 @@
     small_in = jnp.concatenate([router_weight] + [value[:, None] for value in vectors.values()], axis=1)
     small_in = jnp.pad(small_in, ((0, 0), (0, LANES - small_in.shape[1])))
     shard = jnp.concatenate([qkv_weight, proj_weight], axis=1).astype(half)
-    wts = lax.all_gather(shard, both, axis=0, tiled=True).reshape(D, 4, 2, D // 2)
-    wts = wts.transpose(2, 0, 1, 3).reshape(2, D, 2 * D)
+    wts = lax.all_gather(shard, both, axis=0, tiled=True)
+    wts = jnp.concatenate(
+        [
+            wts[:, : 3 * D].reshape(D, 3, 2, D // 2 // LANES, LANES).transpose(2, 0, 3, 1, 4).reshape(2, D, 3 * D // 2),
+            wts[:, 3 * D :].reshape(D, 2, D // 2).transpose(1, 0, 2),
+        ],
+        axis=2,
+    )
     small = lax.all_gather(small_in.astype(half), both, axis=0, tiled=True)
     onehot = assignment[:, None] == jnp.arange(LANES, dtype=jnp.int32)[None, :]
     counts = lax.psum(jnp.sum(onehot.astype(single), axis=0), both)
@@ -1325,7 +1343,14 @@
         ),
         dict(**model_scratch(E, T, D, cap), **end_scratch(T, D)), None, "end",
     )
-    gathered = weight_grads.reshape(2, D, 4, D // 2).transpose(1, 2, 0, 3).reshape(D, 4 * D)
+    pairs = weight_grads[:, :, : 3 * D // 2].reshape(2, D, D // 2 // LANES, 3, LANES)
+    gathered = jnp.concatenate(
+        [
+            pairs.transpose(1, 3, 0, 2, 4).reshape(D, 3 * D),
+            weight_grads[:, :, 3 * D // 2 :].transpose(1, 0, 2).reshape(D, D),
+        ],
+        axis=1,
+    )
     gathered = lax.psum_scatter(gathered, both, scatter_dimension=0, tiled=True)
     small_out = lax.psum_scatter(packed, both, scatter_dimension=0, tiled=True)
     chance = lax.psum(jnp.sum(rest[-1], axis=0), both)

time: 170 us -> 165 us (0.971)
  Pallas kernels: 168 us -> 164 us
    pallas_call x2, Pallas kernels: 168 us -> 164 us  [call(): pl.pallas_call(functools.partial(kernel, names), out_shape=tuple((jax.Sha...]
where the time goes in v5:
time: 165 us
  Pallas kernels  164 us (99%)
    pallas_call x2, Pallas kernels, call(): pl.pallas_call(functools.partial(kernel, names), out_shape=tuple((jax.Sha...  164 us

profile of v5, /device:TPU:0, one launch (start us, length us, event | category | flops | bytes accessed | tf_op | source)
XLA Modules:
  0.0 164.9 jit_solution(13632609789772205214)
XLA Ops:
  0.6 158.1 %layer.1 = (bf16[256,768]{1,0:T(8,128)(2,1)}, bf16[256,768]{1,0:T(8,128)(2,1)}, f32[24,2304]{1,0:T(8,128)}, f32[24,768]{1,0:T(8,128)}, f32[16,128]{1,0:T(8,128)}...) custom-call(bf16[256,768]{1,0:T(8,128)(2,1)} %refs_0_.1, ...), custom_call_target="tpu_custom_call" | custom-call | tf_op jit(solution)/shard_map/layer/pallas_call | solution.py:373
  158.7 6.0 %results.1 = (bf16[256,768]{1,0:T(8,128)(2,1)}, bf16[256,768]{1,0:T(8,128)(2,1)}, f32[24,2304]{1,0:T(8,128)}, f32[24,768]{1,0:T(8,128)}, f32[1,768,768]{2,1,0:T(...) custom-call(bf16[256,768]{1,0:T(8,128)(2,1)} %get-tuple-element.33.r, ...), custom_call_target="tpu_custom_call" | custom-call | tf_op jit(solution)/shard_map/results/pallas_call | solution.py:373

commit v6 on v5

--- a/solution.py
+++ b/solution.py
@@ -1021,9 +1021,9 @@
         read.wait()
     set_places(E, cap, r)
     to_slots(r, r.cotangent[...], r.out_g)
-    gather.own(1)
     gather.fourth(0)
     gather.fourth(2)
+    gather.own(1)
     gather.second(1)
     experts.send_out(1)
     gather.finish(0)

time: 165 us -> 164 us (level)
  Pallas kernels: 164 us -> 162 us
where the time goes in v6:
time: 164 us; the launch traced here: 163 us
  Pallas kernels  162 us (99%)
    pallas_call x2, Pallas kernels, call(): pl.pallas_call(functools.partial(kernel, names), out_shape=tuple((jax.Sha...  162 us

profile of v6, /device:TPU:0, one launch (start us, length us, event | category | flops | bytes accessed | tf_op | source)
XLA Modules:
  0.0 163.3 jit_solution(3602457074334954156)
XLA Ops:
  0.6 156.5 %layer.1 = (bf16[256,768]{1,0:T(8,128)(2,1)}, bf16[256,768]{1,0:T(8,128)(2,1)}, f32[24,2304]{1,0:T(8,128)}, f32[24,768]{1,0:T(8,128)}, f32[16,128]{1,0:T(8,128)}...) custom-call(bf16[256,768]{1,0:T(8,128)(2,1)} %refs_0_.1, ...), custom_call_target="tpu_custom_call" | custom-call | tf_op jit(solution)/shard_map/layer/pallas_call | solution.py:373
  157.1 6.0 %results.1 = (bf16[256,768]{1,0:T(8,128)(2,1)}, bf16[256,768]{1,0:T(8,128)(2,1)}, f32[24,2304]{1,0:T(8,128)}, f32[24,768]{1,0:T(8,128)}, f32[1,768,768]{2,1,0:T(...) custom-call(bf16[256,768]{1,0:T(8,128)(2,1)} %get-tuple-element.33.r, ...), custom_call_target="tpu_custom_call" | custom-call | tf_op jit(solution)/shard_map/results/pallas_call | solution.py:373
